TPU v7x, 256 devices: a whole 4x4x8 slice. The times are simulated.
256 devices in a mesh: fsdp: 32 (over z, y_hi, core), tp: 8 (over y_lo, x).
Axes of the slice: x: 4, y: 4 (y_hi: 2, y_lo: 2; y = y_hi * 2 + y_lo), z: 8, core: 2. Of those that a mesh axis runs over, the one named last changes fastest.
Arguments:
- train_x: bfloat16 [32768, 8192], P('fsdp'), may hold values from -6 to 6
- train_q: bfloat16 [32768, 8192], P('fsdp', 'tp'), may hold values from -17 to 17
- train_k: bfloat16 [32768, 1024], P('fsdp', 'tp'), may hold values from -14 to 14
- train_target: bfloat16 [32768, 8192], P('fsdp', 'tp'), may hold values from -6 to 6
- train_skill: int32 [128], replicated, may hold values from 0 to 3, as said below
- value_weight: bfloat16 [8192, 1024], P('fsdp', 'tp'), may hold values from -0.0625 to 0.0625
- val_x: bfloat16 [4096, 8192], P('fsdp'), may hold values from -6 to 6
- val_q: bfloat16 [4096, 8192], P('fsdp', 'tp'), may hold values from -17 to 17
- val_k: bfloat16 [4096, 1024], P('fsdp', 'tp'), may hold values from -14 to 14
- val_target: bfloat16 [4096, 8192], P('fsdp', 'tp'), may hold values from -6 to 6
- val_skill: int32 [32], replicated, may hold values from 0 to 3, as said below
Outputs:
- skill_grads: bfloat16 [4, 8192, 1024], P(None, 'fsdp', 'tp')
- transfer: float32 [4, 4], replicated
Inputs may be any that keep to these rules, and one draw needn't show every extreme that they name: `train_skill`: each of the 4 skills labels exactly 32 sequences. `val_skill`: each of the 4 skills labels exactly 8 sequences.
All inputs are finite; a program needn't handle non-finite values.
Results may differ from a plain program's by a relative error of at most 0.0052.
The roundings to bfloat16 on the way count: a program that leaves them out, or rounds other values in their place, can miss the bound.
Values may be sent and summed in bfloat16 or wider, within the bound.
No kernel may reach another device: no remote copies, remote signals or barrier semaphores. Data moves between devices by JAX's collectives and lax.ppermute only.
A program may use at most 192 MiB of HBM per device.

v0:
```python
import functools
import math

import jax
import jax.numpy as jnp
from jax import lax
from jax.experimental import pallas as pl
from jax.experimental.pallas import tpu as pltpu
from jax.sharding import PartitionSpec as P

HD = 128
GROUP = 8
SKILLS = 4
SEQ = 256
VSEQ = 128
MEMBERS = 4
NZ, NY, NC = 8, 2, 2
NX, NL = 4, 2
ROWS = 256

step_size = 0.01
bf16 = jnp.bfloat16
f32 = jnp.float32


def place(z, y, c):
    return (z % NZ) * 4 + (y % NY) * 2 + (c % NC)


def moves(fn):
    return [
        (place(z, y, c), place(*fn(z, y, c)))
        for z in range(NZ)
        for y in range(NY)
        for c in range(NC)
    ]


DIAGONAL = moves(lambda z, y, c: (z, y + 1, c + 1))
CORE = moves(lambda z, y, c: (z, y, c + 1))
YHI = moves(lambda z, y, c: (z, y + 1, c))
UP = moves(lambda z, y, c: (z + 1, y, c))
DOWN = moves(lambda z, y, c: (z - 1, y, c))


def send(value, way):
    return lax.ppermute(value, "fsdp", way)


def call(kernel, prefetched, operands, waits, grid, in_specs, out_specs, out_shape, cost_estimate, scratch=(), mib=50):
    first = len(prefetched) + len(operands)

    def body(*refs):
        kernel(*refs[:first], *refs[first + len(waits) :])

    return pl.pallas_call(
        body,
        grid_spec=pltpu.PrefetchScalarGridSpec(
            num_scalar_prefetch=len(prefetched),
            grid=grid,
            in_specs=list(in_specs) + [pl.BlockSpec(memory_space=pl.ANY)] * len(waits),
            out_specs=out_specs,
            scratch_shapes=list(scratch),
        ),
        out_shape=out_shape,
        compiler_params=pltpu.CompilerParams(vmem_limit_bytes=mib * 2**20),
        cost_estimate=cost_estimate,
    )(*prefetched, *operands, *waits)


def joined(values, waits):
    return pl.pallas_call(
        lambda *refs: None,
        in_specs=[pl.BlockSpec(memory_space=pl.ANY)] * (len(values) + len(waits)),
        out_specs=[pl.BlockSpec(memory_space=pl.ANY)] * len(values),
        out_shape=[jax.ShapeDtypeStruct(v.shape, v.dtype) for v in values],
        input_output_aliases={i: i for i in range(len(values))},
        compiler_params=pltpu.CompilerParams(vmem_limit_bytes=50 * 2**20),
        cost_estimate=cost(1, 1),
    )(*values, *waits)


def vmem(shape):
    return pl.BlockSpec(shape, lambda i, *_: (0,) * len(shape))


def cost(flops, moved, exps=0):
    return pl.CostEstimate(flops=flops // 64, bytes_accessed=moved // 64, transcendentals=exps // 64)


def dot(a, b, dims=((1,), (0,))):
    return lax.dot_general(a, b, (dims, ((), ())), preferred_element_type=f32)


def attend_kernel(length, q_ref, k_ref, p_ref):
    keys = k_ref[...]
    rows = lax.broadcasted_iota(jnp.int32, (length, length), 0)
    columns = lax.broadcasted_iota(jnp.int32, (length, length), 1)
    allowed = rows >= columns
    for h in range(GROUP):
        scores = dot(q_ref[:, h * HD : (h + 1) * HD], keys, ((1,), (1,)))
        scores = jnp.where(allowed, scores * (1.0 / math.sqrt(HD)), jnp.float32(-1e30))
        raised = jnp.exp(scores - jnp.max(scores, axis=-1, keepdims=True))
        total = jnp.sum(raised, axis=-1, keepdims=True)
        p_ref[0, h] = (raised * (1.0 / total)).astype(bf16)


def attend(queries, keys, length, waits=()):
    members = queries.shape[0] // length
    count = members * GROUP * length * length
    return call(
        functools.partial(attend_kernel, length),
        (),
        (queries, keys),
        waits,
        (members,),
        [
            pl.BlockSpec((length, GROUP * HD), lambda i: (i, 0)),
            pl.BlockSpec((length, HD), lambda i: (i, 0)),
        ],
        pl.BlockSpec((1, GROUP, length, length), lambda i: (i, 0, 0, 0)),
        jax.ShapeDtypeStruct((members, GROUP, length, length), bf16),
        cost(2 * count * HD, 4 * count, count),
    )


def z_of(place_ref, dz):
    return lax.rem(place_ref[0] + dz, NZ)


def lay_weights(place_ref, blocks, whole):
    for dc in range(NC):
        for dy in range(NY):
            y = lax.rem(place_ref[1] + dy, NY)
            c = lax.rem(place_ref[2] + dc, NC)
            row = pl.multiple_of((y * 2 + c) * ROWS, ROWS)
            whole[pl.ds(row, ROWS), :] = blocks[dc * NY + dy]


def project_kernel(n, first, place_ref, *refs):
    xs, refs = refs[:n], refs[n:]
    vs, refs = refs[:n], refs[n:]
    ws, refs = refs[:n], refs[n:]
    if first:
        sum_out, val_out, *whole = refs
    else:
        sum_in, val_in, sum_out, val_out, *whole = refs

    @pl.when(pl.program_id(0) == 0)
    def _():
        for j in range(n):
            lay_weights(place_ref, ws[j], whole[j])
        total = sum(dot(vs[j][...], whole[j][...]) for j in range(n))
        val_out[...] = total if first else total + val_in[...]

    total = sum(dot(xs[j][...], whole[j][...]) for j in range(n))
    sum_out[...] = total if first else total + sum_in[...]


WIDE = NY * NC * ROWS
TILE = 512


def project(where, train_x, val_x, zs, weights, sums, waits=()):
    n = len(zs)
    rows = train_x.shape[0]
    sum_specs = [pl.BlockSpec((TILE, HD), lambda i, p: (i, 0)), vmem((VSEQ, HD))]
    first = sums is None
    return call(
        functools.partial(project_kernel, n, first),
        (where,),
        (*[train_x] * n, *[val_x] * n, *weights, *([] if first else sums)),
        waits,
        (rows // TILE,),
        [pl.BlockSpec((TILE, WIDE), lambda i, p, dz=dz: (i, z_of(p, dz))) for dz in zs]
        + [pl.BlockSpec((VSEQ, WIDE), lambda i, p, dz=dz: (0, z_of(p, dz))) for dz in zs]
        + [vmem((NC * NY, ROWS, HD))] * n
        + ([] if first else sum_specs),
        sum_specs,
        [jax.ShapeDtypeStruct((rows, HD), f32), jax.ShapeDtypeStruct((VSEQ, HD), f32)],
        cost(2 * rows * n * WIDE * HD, 2 * rows * n * WIDE),
        [pltpu.VMEM((WIDE, HD), bf16)] * n,
    )


def grads_kernel(place_ref, x_ref, w_ref, sum_ref, p_ref, target_ref, out_ref, whole):
    @pl.when(pl.program_id(0) == 0)
    def _():
        lay_weights(place_ref, w_ref, whole)

    values = (sum_ref[...] + dot(x_ref[...], whole[...])).astype(bf16)
    attention = p_ref[0].reshape(GROUP * SEQ, SEQ)
    mixed = dot(attention, values)
    target = jnp.concatenate(
        [target_ref[:, h * HD : (h + 1) * HD] for h in range(GROUP)], axis=0
    ).astype(f32)
    residual = ((mixed - target) * (1.0 / SEQ)).astype(bf16)
    pulled = dot(residual, attention, ((0,), (0,)))
    out_ref[...] = pulled.astype(bf16)


def value_grads(where, train_x, weights, sums, attention, target, waits=()):
    rows = train_x.shape[0]
    return call(
        grads_kernel,
        (where,),
        (train_x, weights, sums, attention, target),
        waits,
        (MEMBERS,),
        [
            pl.BlockSpec((SEQ, WIDE), lambda i, p: (i, z_of(p, 4))),
            vmem((NC * NY, ROWS, HD)),
            pl.BlockSpec((SEQ, HD), lambda i, p: (i, 0)),
            pl.BlockSpec((1, GROUP, SEQ, SEQ), lambda i, p: (i, 0, 0, 0)),
            pl.BlockSpec((SEQ, GROUP * HD), lambda i, p: (i, 0)),
        ],
        pl.BlockSpec((HD, SEQ), lambda i, p: (0, i)),
        jax.ShapeDtypeStruct((HD, rows), bf16),
        cost(4 * rows * GROUP * SEQ * HD, 8 * 2**20),
        [pltpu.VMEM((WIDE, HD), bf16)],
    )


def val_kernel(place_ref, x_ref, w_ref, sum_ref, p_ref, target_ref, out_ref, whole):
    lay_weights(place_ref, w_ref, whole)
    values = (sum_ref[...] + dot(x_ref[...], whole[...])).astype(bf16)
    attention = p_ref[0].reshape(GROUP * VSEQ, VSEQ)
    target = jnp.concatenate(
        [target_ref[:, h * HD : (h + 1) * HD] for h in range(GROUP)], axis=0
    ).astype(f32)
    residual = (dot(attention, values) - target) * (1.0 / VSEQ)
    high = residual.astype(bf16)
    low = (residual - high.astype(f32)).astype(bf16)
    pulled = dot(high, attention, ((0,), (0,))) + dot(low, attention, ((0,), (0,)))
    out_ref[...] = pulled.astype(bf16)


def val_pulls(where, val_x, weights, sums, attention, target, waits=()):
    return call(
        val_kernel,
        (where,),
        (val_x, weights, sums, attention, target),
        waits,
        (1,),
        [
            pl.BlockSpec((VSEQ, WIDE), lambda i, p: (0, z_of(p, 4))),
            vmem((NC * NY, ROWS, HD)),
            vmem((VSEQ, HD)),
            vmem((1, GROUP, VSEQ, VSEQ)),
            vmem((VSEQ, GROUP * HD)),
        ],
        vmem((HD, VSEQ)),
        jax.ShapeDtypeStruct((HD, VSEQ), bf16),
        cost(10 * VSEQ * GROUP * VSEQ * HD, 2**20),
        [pltpu.VMEM((WIDE, HD), bf16)],
    )


def pick_kernel(place_ref, x_ref, out_ref, sems):
    copies = []
    for i in range(NZ * NY):
        column = pl.multiple_of((2 * i + 1 - place_ref[2]) * ROWS, ROWS)
        source = x_ref.at[:, pl.ds(column, ROWS)]
        copies.append(pltpu.make_async_copy(source, out_ref.at[:, i * ROWS : (i + 1) * ROWS], sems.at[i]))
    for copy in copies:
        copy.start()
    for copy in copies:
        copy.wait()


def other_core_columns(where, train_x, waits=()):
    rows, columns = train_x.shape
    anywhere = pl.BlockSpec(memory_space=pl.ANY)
    return call(
        pick_kernel,
        (where,),
        (train_x,),
        waits,
        (1,),
        [anywhere],
        anywhere,
        jax.ShapeDtypeStruct((rows, columns // NC), bf16),
        cost(0, 2 * rows * columns),
        [pltpu.SemaphoreType.DMA((NZ * NY,))],
    )


def skills_kernel(place_ref, own_x, other_x, own_grads, other_grads, out_ref, total):
    total[...] = jnp.zeros_like(total)
    for k, (x_ref, grads_ref) in enumerate(((own_x, own_grads), (other_x, other_grads))):
        for m in range(MEMBERS):
            tokens = slice(m * SEQ, (m + 1) * SEQ)
            total[place_ref[3 + k * MEMBERS + m]] += dot(grads_ref[:, tokens], x_ref[tokens, :])
    out_ref[0, 0] = total[...].reshape(SKILLS * HD, ROWS)


def skill_terms(where, own_x, other_x, grads, zs, waits=()):
    rows = own_x.shape[0]
    first, step = zs[0], zs[-1] - zs[0]

    def pair_of(i, j, p):
        return z_of(p, first + i * step) * 2 + lax.rem(p[1] + j, NY)

    return call(
        skills_kernel,
        (where,),
        (own_x, other_x, *grads),
        waits,
        (len(zs), NY),
        [
            pl.BlockSpec((rows, ROWS), lambda i, j, p: (0, pair_of(i, j, p) * 2 + p[2])),
            pl.BlockSpec((rows, ROWS), lambda i, j, p: (0, pair_of(i, j, p))),
            pl.BlockSpec((HD, rows), lambda i, j, p: (0, 0)),
            pl.BlockSpec((HD, rows), lambda i, j, p: (0, 0)),
        ],
        pl.BlockSpec((1, 1, SKILLS * HD, ROWS), lambda i, j, p: (i, j, 0, 0)),
        jax.ShapeDtypeStruct((len(zs), NY, SKILLS * HD, ROWS), f32),
        cost(2 * rows * len(zs) * WIDE * HD, len(zs) * 5 * 2**20),
        [pltpu.VMEM((SKILLS, HD, ROWS), f32)],
    )


HALF = SKILLS * HD


def step_kernel(step, mine_ref, up_ref, down_ref, up_out, down_out):
    if step == 1:
        up_out[:HALF, :] = mine_ref[0, 0].astype(bf16)
        down_out[:HALF, :] = mine_ref[0, 1].astype(bf16)
        up_out[HALF:, :] = up_ref[...]
        down_out[HALF:, :] = down_ref[...]
        return
    for dy in range(NY):
        rows = slice(dy * HALF, (dy + 1) * HALF)
        if step == 2:
            came = (up_ref if dy == 0 else None, down_ref if dy == 1 else None)
            there = slice(0, HALF)
        else:
            came, there = (up_ref, down_ref), rows
        for k, (ref, out) in enumerate(zip(came, (up_out, down_out))):
            total = mine_ref[k, dy]
            if ref is not None:
                total = total + ref[there, :].astype(f32)
            out[rows, :] = total.astype(bf16)
    if step < 4:
        for ref, out in ((up_ref, up_out), (down_ref, down_out)):
            out[NY * HALF :, :] = ref[ref.shape[0] - HD :, :]


def ring_step(step, mine, up, down):
    rows = {1: HALF + HD, 2: NY * HALF + HD, 3: NY * HALF + HD, 4: NY * HALF}[step]
    shape = (rows, ROWS)
    operands = (mine, up, down)
    up, down = call(
        functools.partial(step_kernel, step),
        (),
        operands,
        (),
        (1,),
        [vmem(o.shape) for o in operands],
        [vmem(shape), vmem(shape)],
        [jax.ShapeDtypeStruct(shape, bf16)] * 2,
        cost(2**20, 4 * 2**20),
    )
    return up, (send(up, UP), send(down, DOWN))


def stack_kernel(*refs):
    for i, ref in enumerate(refs[:-1]):
        refs[-1][i] = ref[...]


def stacked(arrays):
    tails = [pl.BlockSpec((HD, ROWS), lambda i, n=a.shape[0] // HD - 1: (n, 0)) for a in arrays]
    return call(
        stack_kernel,
        (),
        arrays,
        (),
        (1,),
        tails,
        vmem((len(arrays), HD, ROWS)),
        jax.ShapeDtypeStruct((len(arrays), HD, ROWS), bf16),
        cost(0, 2**20),
    )


def directions_kernel(place_ref, skill_ref, near_ref, far_ref, x_ref, out_ref):
    out_ref[...] = jnp.zeros_like(out_ref)
    for dz in range(NZ):
        for dy in range(NY):
            for dc, ref in enumerate((near_ref, far_ref)):
                f = z_of(place_ref, dz) * 4 + lax.rem(place_ref[1] + dy, NY) * 2 + lax.rem(place_ref[2] + dc, NC)
                tokens = x_ref[:, f].reshape(VSEQ, ROWS)
                out_ref[skill_ref[f]] += dot(ref[dz, :, dy * HD : (dy + 1) * HD], tokens)


def directions_of(where, val_skill, near, far, columns):
    return call(
        directions_kernel,
        (where, val_skill),
        (near, far, columns),
        (),
        (1,),
        [vmem(near.shape), vmem(far.shape), vmem(columns.shape)],
        vmem((SKILLS, HD, ROWS)),
        jax.ShapeDtypeStruct((SKILLS, HD, ROWS), f32),
        cost(2 * 4096 * ROWS * HD, 4 * 2**20),
    )


def local_kernel(mine_ref, up_ref, down_ref, here_ref, there_ref, keep_ref, give_ref, local_ref):
    lane = lax.broadcasted_iota(jnp.int32, (1, HD), 1)
    local = jnp.zeros((1, HD), f32)
    for s in range(SKILLS):
        rows = slice(s * HD, (s + 1) * HD)
        totals = [
            mine_ref[0, dy, rows, :]
            + up_ref[dy * HALF + s * HD : dy * HALF + (s + 1) * HD, :].astype(f32)
            + down_ref[dy * HALF + s * HD : dy * HALF + (s + 1) * HD, :].astype(f32)
            for dy in range(NY)
        ]
        keep_ref[rows, :] = totals[0]
        give_ref[rows, :] = totals[1].astype(bf16)
        for v in range(SKILLS):
            product = totals[0] * here_ref[v] + totals[1] * there_ref[v].astype(f32)
            product = jnp.sum(product, axis=0, keepdims=True)
            entry = step_size * jnp.sum(product, axis=1, keepdims=True)
            local = jnp.where(lane == s * SKILLS + v, entry, local)
    local_ref[...] = local


def local_transfer(mine, up, down, here, there):
    operands = (mine, up, down, here, there)
    return call(
        local_kernel,
        (),
        operands,
        (),
        (1,),
        [vmem(o.shape) for o in operands],
        [vmem((SKILLS * HD, ROWS)), vmem((SKILLS * HD, ROWS)), vmem((1, HD))],
        [
            jax.ShapeDtypeStruct((SKILLS * HD, ROWS), f32),
            jax.ShapeDtypeStruct((SKILLS * HD, ROWS), bf16),
            jax.ShapeDtypeStruct((1, HD), f32),
        ],
        cost(2**22, 4 * 2**20),
    )


def finish_kernel(keep_ref, got_ref, grads_ref):
    for s in range(SKILLS):
        rows = slice(s * HD, (s + 1) * HD)
        grads_ref[s] = (keep_ref[rows, :] + got_ref[rows, :].astype(f32)).T.astype(bf16)


def finish(keep, got):
    return call(
        finish_kernel,
        (),
        (keep, got),
        (),
        (1,),
        [vmem(keep.shape), vmem(got.shape)],
        vmem((SKILLS, ROWS, HD)),
        jax.ShapeDtypeStruct((SKILLS, ROWS, HD), bf16),
        cost(2**20, 2**20),
    )


def sum_all(row):
    copies = jnp.broadcast_to(row, (NZ * NY * NC * NX * NL,) + row.shape)
    return jnp.sum(lax.all_to_all(copies, ("fsdp", "tp"), 0, 0), axis=0)


def on_device(
    train_x, train_q, train_k, train_target, train_skill, value_weight, val_x, val_q, val_k, val_target, val_skill
):
    f, t = lax.axis_index("fsdp"), lax.axis_index("tp")
    z, y, c = f // 4, (f // 2) % 2, f % 2
    own_skill = lax.dynamic_slice_in_dim(train_skill, f * MEMBERS, MEMBERS)
    other_skill = lax.dynamic_slice_in_dim(train_skill, (f + 1 - 2 * c) * MEMBERS, MEMBERS)
    where = jnp.concatenate([jnp.stack([z, y, c]).astype(jnp.int32), own_skill, other_skill])

    part = VSEQ // 8
    own_tokens = lax.dynamic_slice_in_dim(val_x, t * part, part).reshape(part, 32, ROWS)
    crossed = lax.all_to_all(own_tokens.transpose(1, 0, 2), "fsdp", 0, 0)
    columns = lax.all_to_all(jnp.broadcast_to(crossed, (8,) + crossed.shape), "tp", 0, 0)

    own = value_weight
    quad = jnp.stack([own, send(own, YHI), send(own, CORE), send(own, DIAGONAL)])
    val_attention = attend(val_q, val_k, VSEQ)
    attention = attend(train_q, train_k, SEQ, (val_attention, quad))
    up1, down1 = send(quad, UP), send(quad, DOWN)
    up1, down1 = joined((up1, down1), (attention,))
    up2, down2 = send(up1, UP), send(down1, DOWN)
    sums = project(where, train_x, val_x, (0,), [quad], None, (attention, up1))
    picked = other_core_columns(where, train_x, (up1,))
    other_x = send(picked, CORE)
    up2, down2 = joined((up2, down2), (sums[1], picked))
    up3, down3 = send(up2, UP), send(down2, DOWN)
    sums = project(where, train_x, val_x, (1, 7), [down1, up1], sums)
    up3, down3 = joined((up3, down3), (sums[1], crossed))
    last = jnp.concatenate([send(up3[:2], UP), send(down3[2:], DOWN)])
    sums = project(where, train_x, val_x, (2, 6), [down2, up2], sums)
    sums = project(where, train_x, val_x, (3, 5), [down3, up3], sums)
    own_pull = val_pulls(where, val_x, last, sums[1], val_attention, val_target)
    pull = jnp.concatenate([own_pull, send(own_pull, YHI)], axis=1)
    p_up, p_down = send(pull, UP), send(pull, DOWN)
    grads = value_grads(where, train_x, last, sums[0], attention, train_target, (own_pull,))
    grads = (grads, send(grads, CORE))

    def terms(zs, *waits):
        return skill_terms(where, train_x, other_x, grads, zs, waits)

    pulls = {0: pull, 1: p_down, 7: p_up}
    sent, (up, down) = ring_step(1, terms((4,)), p_up, p_down)
    mine = terms((3, 5), sent)
    pulls[6], pulls[2] = up, down
    sent, (up, down) = ring_step(2, mine, up, down)
    mine = terms((2, 6), sent)
    pulls[5], pulls[3] = up, down
    sent, (up, down) = ring_step(3, mine, up, down)
    mine = terms((1, 7), sent)
    pulls[4] = up
    sent, (up, down) = ring_step(4, mine, up, down)
    near_pulls = stacked([pulls[dz] for dz in range(NZ)])
    here = directions_of(where, val_skill, near_pulls, send(near_pulls, CORE), columns)
    there = send(here.astype(bf16), YHI)
    keep, give, local = local_transfer(terms((0,), sent, here), up, down, here, there)
    row = sum_all(local)
    skill_grads = finish(keep, send(give, YHI))
    return (skill_grads, row[0, : SKILLS * SKILLS].reshape(SKILLS, SKILLS))


def solution(mesh):
    placed = (
        P("fsdp", None),
        P("fsdp", "tp"),
        P("fsdp", "tp"),
        P("fsdp", "tp"),
        P(),
        P("fsdp", "tp"),
        P("fsdp", None),
        P("fsdp", "tp"),
        P("fsdp", "tp"),
        P("fsdp", "tp"),
        P(),
    )
    return jax.shard_map(
        on_device,
        mesh=mesh,
        in_specs=placed,
        out_specs=(P(None, "fsdp", "tp"), P()),
        check_vma=False,
    )
```

profile of v0, /device:TPU:1, one launch (start us, length us, event | category | flops | bytes accessed | tf_op | source)
XLA Modules:
  0.0 441.4 jit_solution(10392127922959162473)
XLA Ops:
  0.6 3.8 collective-permute-start
  7.1 3.7 collective-permute-done.2
  13.4 4.0 collective-permute-start.4
  23.2 4.7 %shard_map.123.refs_2_.refs_4_ = bf16[4,8,256,256]{3,2,1,0:T(8,128)(2,1)} custom-call(bf16[1024,1024]{1,0:T(8,128)(2,1)S(1)} %copy-done.3, bf16[1024,128]{1,0:T(8,128)(2,1)S(1)} %copy-done.9, bf16[1,8,128,128]{3,2,1,0:T(8,128)(2,1)S(1)} %shard_map.122.refs_2_.refs_4_, bf16[4,256,128]{2,1,0:T(8,128)(2,1)S(1)} %pad_maximum_fusion.refs_3_), custom_call_target="tpu_custom_call" | custom-call | flops 8388608 | bytes 131072 | tf_op jit(solution)/shard_map/pallas_call | solution.py:56
  27.8 255.9 %shard_map.125.refs_3_ = bf16[1024,4096]{1,0:T(8,128)(2,1)} custom-call(s32[11]{0:T(128)S(1)} %concatenate.9.refs_0_, bf16[1024,8192]{1,0:T(8,128)(2,1)} %refs_1_.29, bf16[4,256,128]{2,1,0:T(8,128)(2,1)S(1)} %get-tuple-element.27.refs_2_.refs_5_.refs_6_), custom_call_target="tpu_custom_call" | custom-call | bytes 262144 | tf_op jit(solution)/shard_map/pallas_call | solution.py:56
  284.2 2.7 collective-permute-start.7
  287.6 7.1 %all-to-all-start = ((bf16[32,16,256]{2,1,0:T(8,128)(2,1)}), bf16[32,16,256]{2,1,0:T(8,128)(2,1)S(1)}, u32[]{:S(2)}, u32[]{:S(2)}) async-start(bf16[32,16,256]{2,1,0:T(8,128)(2,1)} %bitcast.19), calls=%async_computation | async-start | bytes 524288 | tf_op jit(solution)/shard_map/all_to_all | solution.py:488
  294.7 2.9 shard_map.126
  300.5 4.0 shard_map.128
  309.8 2.9 collective-permute-start.11
  313.7 4.1 shard_map.130
  317.8 4.0 shard_map.131
  323.4 6.8 %shard_map.133.refs_3_ = bf16[128,1024]{1,0:T(8,128)(2,1)S(1)} custom-call(s32[11]{0:T(128)S(1)} %concatenate.9.refs_0_, bf16[1024,8192]{1,0:T(8,128)(2,1)} %refs_1_.29, bf16[4,256,128]{2,1,0:T(8,128)(2,1)S(1)} %constant_dynamic-update-slice_fusion.refs_2_, f32[1024,128]{1,0:T(8,128)S(1)} %get-tuple-element.39.refs_3_, ...), custom_call_target="tpu_custom_call" | custom-call | flops 16777216 | bytes 131072 | tf_op jit(solution)/shard_map/pallas_call | solution.py:56
  331.5 2.7 collective-permute-start.13
  335.9 2.7 collective-permute-start.15
  342.1 2.7 collective-permute-start.17
  346.2 4.4 all-to-all-start.1
  350.6 4.2 shard_map.136.refs_0_
  356.1 2.7 collective-permute-start.19
  358.8 4.2 shard_map.138.refs_0_
  364.4 5.1 %collective-permute-done.18.refs_1_.refs_5_ = bf16[1152,256]{1,0:T(8,128)(2,1)S(1)} collective-permute-done((bf16[1152,256]{1,0:T(8,128)(2,1)S(1)}, bf16[1152,256]{1,0:T(8,128)(2,1)S(1)}, u32[]{:S(2)}, u32[]{:S(2)}) %collective-permute-start.18) | collective-permute-done | bytes 589856 | tf_op jit(solution)/shard_map/ppermute | solution.py:47
  371.4 2.7 collective-permute-start.21
  374.0 9.8 %collective-permute-done.20.refs_1_.refs_4_ = bf16[1152,256]{1,0:T(8,128)(2,1)S(1)} collective-permute-done((bf16[1152,256]{1,0:T(8,128)(2,1)S(1)}, bf16[1152,256]{1,0:T(8,128)(2,1)S(1)}, u32[]{:S(2)}, u32[]{:S(2)}) %collective-permute-start.20) | collective-permute-done | bytes 589856 | tf_op jit(solution)/shard_map/ppermute | solution.py:47
  384.7 4.6 %collective-permute-start.22 = (bf16[8,128,256]{2,1,0:T(8,128)(2,1)S(1)}, bf16[8,128,256]{2,1,0:T(8,128)(2,1)}, u32[]{:S(2)}, u32[]{:S(2)}) collective-permute-start(bf16[8,128,256]{2,1,0:T(8,128)(2,1)S(1)} %shard_map.142.refs_2_), channel_id=1, source_target_pairs={{0,8},{8,0},{16,24},{24,16},{32,40},{40,32},{48,56},{56,48},{64,72... | collective-permute-start | bytes 1572872 | tf_op jit(solution)/shard_map/ppermute | solution.py:47
  389.3 4.2 shard_map.140.refs_0_
  394.9 2.7 shard_map.141
  397.6 2.7 collective-permute-start.24
  402.7 3.4 collective-permute-start.25
  408.7 4.0 collective-permute-done.23.refs_1_
  415.4 11.6 %all-to-all-start.2 = ((f32[256,1,128]{2,1,0:T(1,128)}), f32[256,1,128]{2,1,0:T(1,128)S(1)}, u32[]{:S(2)}, u32[]{:S(2)}) async-start(f32[256,1,128]{2,1,0:T(1,128)} %broadcast_in_dim.7), calls=%async_computation.2 | async-start | bytes 262144 | tf_op jit(solution)/shard_map/all_to_all | solution.py:474
  427.0 3.0 collective-permute-start.26
  430.0 9.8 %all-to-all-done.2 = f32[256,1,128]{2,1,0:T(1,128)S(1)} async-done(((f32[256,1,128]{2,1,0:T(1,128)}), f32[256,1,128]{2,1,0:T(1,128)S(1)}, u32[]{:S(2)}, u32[]{:S(2)}) %all-to-all-start.2) | async-done | bytes 131104 | tf_op jit(solution)/shard_map/all_to_all | solution.py:474
  (105 shorter events, 46.8 us)
Async XLA Ops:
  0.6 6.5 %collective-permute-start = (bf16[256,128]{1,0:T(8,128)(2,1)}, bf16[256,128]{1,0:T(8,128)(2,1)S(1)}, u32[]{:S(2)}, u32[]{:S(2)}) collective-permute-start(bf16[256,128]{1,0:T(8,128)(2,1)} %param.16), channel_id=1, source_target_pairs={{0,16},{8,24},{16,0},{24,8},{32,48},{40,56},{48,32},{56,40},{64,80... | collective-permute-start | bytes 196616 | tf_op jit(solution)/shard_map/ppermute | solution.py:47
  4.5 2.6 collective-permute-start.1
  5.4 5.4 %collective-permute-start.2 = (bf16[256,128]{1,0:T(8,128)(2,1)}, bf16[256,128]{1,0:T(8,128)(2,1)S(1)}, u32[]{:S(2)}, u32[]{:S(2)}) collective-permute-start(bf16[256,128]{1,0:T(8,128)(2,1)} %param.16), channel_id=1, source_target_pairs={{0,24},{8,16},{16,8},{24,0},{32,56},{40,48},{48,40},{56,32},{64,88... | collective-permute-start | bytes 196616 | tf_op jit(solution)/shard_map/ppermute | solution.py:47
  11.7 16.1 %collective-permute-start.3 = (bf16[4,256,128]{2,1,0:T(8,128)(2,1)S(1)}, bf16[4,256,128]{2,1,0:T(8,128)(2,1)S(1)}, u32[]{:S(2)}, u32[]{:S(2)}) collective-permute-start(bf16[4,256,128]{2,1,0:T(8,128)(2,1)S(1)} %pad_maximum_fusion.refs_3_), channel_id=1, source_target_pairs={{0,32},{8,40},{16,48},{24,56},{32,64},{40,72},{48,80},{56,88},{64,... | collective-permute-start | bytes 786440 | tf_op jit(solution)/shard_map/ppermute | solution.py:47
  13.4 14.4 %collective-permute-start.4 = (bf16[4,256,128]{2,1,0:T(8,128)(2,1)S(1)}, bf16[4,256,128]{2,1,0:T(8,128)(2,1)S(1)}, u32[]{:S(2)}, u32[]{:S(2)}) collective-permute-start(bf16[4,256,128]{2,1,0:T(8,128)(2,1)S(1)} %pad_maximum_fusion.refs_3_), channel_id=1, source_target_pairs={{0,224},{8,232},{16,240},{24,248},{32,0},{40,8},{48,16},{56,24},{6... | collective-permute-start | bytes 786440 | tf_op jit(solution)/shard_map/ppermute | solution.py:47
  27.8 256.4 %copy-start.5 = (bf16[4,256,128]{2,1,0:T(8,128)(2,1)}, bf16[4,256,128]{2,1,0:T(8,128)(2,1)S(1)}, u32[]{:S(2)}) copy-start(bf16[4,256,128]{2,1,0:T(8,128)(2,1)S(1)} %get-tuple-element.28.refs_5_) | copy-start | bytes 786436
  27.8 259.0 %copy-start = (bf16[128,8192]{1,0:T(8,128)(2,1)S(1)}, bf16[128,8192]{1,0:T(8,128)(2,1)}, u32[]{:S(2)}) copy-start(bf16[128,8192]{1,0:T(8,128)(2,1)} %refs_1_.22) | copy-start | bytes 6291460
  283.7 54.8 %collective-permute-start.5 = (bf16[1024,4096]{1,0:T(8,128)(2,1)}, bf16[1024,4096]{1,0:T(8,128)(2,1)}, u32[]{:S(2)}, u32[]{:S(2)}) collective-permute-start(bf16[1024,4096]{1,0:T(8,128)(2,1)} %shard_map.125.refs_3_), channel_id=1, source_target_pairs={{0,8},{8,0},{16,24},{24,16},{32,40},{40,32},{48,56},{56,48},{64,72... | collective-permute-start | bytes 25165832 | tf_op jit(solution)/shard_map/ppermute | solution.py:47
  284.2 13.5 %collective-permute-start.6 = (bf16[4,256,128]{2,1,0:T(8,128)(2,1)S(1)}, bf16[4,256,128]{2,1,0:T(8,128)(2,1)}, u32[]{:S(2)}, u32[]{:S(2)}) collective-permute-start(bf16[4,256,128]{2,1,0:T(8,128)(2,1)S(1)} %get-tuple-element.27.refs_2_.refs_5_.refs_6_), channel_id=1, source_target_pairs={{0,32},{8,40},{16,48},{24,56},{32,64},{40,72},{48,80},{56,88},{64,... | collective-permute-start | bytes 786440 | tf_op jit(solution)/shard_map/ppermute | solution.py:47
  284.2 13.5 %collective-permute-start.7 = (bf16[4,256,128]{2,1,0:T(8,128)(2,1)S(1)}, bf16[4,256,128]{2,1,0:T(8,128)(2,1)}, u32[]{:S(2)}, u32[]{:S(2)}) collective-permute-start(bf16[4,256,128]{2,1,0:T(8,128)(2,1)S(1)} %get-tuple-element.28.refs_5_), channel_id=1, source_target_pairs={{0,224},{8,232},{16,240},{24,248},{32,0},{40,8},{48,16},{56,24},{6... | collective-permute-start | bytes 786440 | tf_op jit(solution)/shard_map/ppermute | solution.py:47
  287.6 20.0 %all-to-all-start = ((bf16[32,16,256]{2,1,0:T(8,128)(2,1)}), bf16[32,16,256]{2,1,0:T(8,128)(2,1)S(1)}, u32[]{:S(2)}, u32[]{:S(2)}) async-start(bf16[32,16,256]{2,1,0:T(8,128)(2,1)} %bitcast.19), calls=%async_computation | async-start | bytes 524288 | tf_op jit(solution)/shard_map/all_to_all | solution.py:488
  297.7 12.0 %collective-permute-start.8 = (bf16[4,256,128]{2,1,0:T(8,128)(2,1)}, bf16[4,256,128]{2,1,0:T(8,128)(2,1)S(1)}, u32[]{:S(2)}, u32[]{:S(2)}) collective-permute-start(bf16[4,256,128]{2,1,0:T(8,128)(2,1)} %get-tuple-element.30.refs_6_), channel_id=1, source_target_pairs={{0,32},{8,40},{16,48},{24,56},{32,64},{40,72},{48,80},{56,88},{64,... | collective-permute-start | bytes 786440 | tf_op jit(solution)/shard_map/ppermute | solution.py:47
  299.1 10.5 %collective-permute-start.9 = (bf16[4,256,128]{2,1,0:T(8,128)(2,1)}, bf16[4,256,128]{2,1,0:T(8,128)(2,1)S(1)}, u32[]{:S(2)}, u32[]{:S(2)}) collective-permute-start(bf16[4,256,128]{2,1,0:T(8,128)(2,1)} %get-tuple-element.31.refs_5_), channel_id=1, source_target_pairs={{0,224},{8,232},{16,240},{24,248},{32,0},{40,8},{48,16},{56,24},{6... | collective-permute-start | bytes 786440 | tf_op jit(solution)/shard_map/ppermute | solution.py:47
  309.6 12.2 %collective-permute-start.10 = (bf16[2,256,128]{2,1,0:T(8,128)(2,1)S(1)}, bf16[2,256,128]{2,1,0:T(8,128)(2,1)S(1)}, u32[]{:S(2)}, u32[]{:S(2)}) collective-permute-start(bf16[2,256,128]{2,1,0:T(8,128)(2,1)S(1)} %slice.9), channel_id=1, source_target_pairs={{0,32},{8,40},{16,48},{24,56},{32,64},{40,72},{48,80},{56,88},{64,... | collective-permute-start | bytes 393224 | tf_op jit(solution)/shard_map/ppermute | solution.py:47
  309.8 12.1 %collective-permute-start.11 = (bf16[2,256,128]{2,1,0:T(8,128)(2,1)S(1)}, bf16[2,256,128]{2,1,0:T(8,128)(2,1)S(1)}, u32[]{:S(2)}, u32[]{:S(2)}) collective-permute-start(bf16[2,256,128]{2,1,0:T(8,128)(2,1)S(1)} %slice.10), channel_id=1, source_target_pairs={{0,224},{8,232},{16,240},{24,248},{32,0},{40,8},{48,16},{56,24},{6... | collective-permute-start | bytes 393224 | tf_op jit(solution)/shard_map/ppermute | solution.py:47
  330.2 8.4 %collective-permute-start.12 = (bf16[128,1024]{1,0:T(8,128)(2,1)S(1)}, bf16[128,1024]{1,0:T(8,128)(2,1)S(1)}, u32[]{:S(2)}, u32[]{:S(2)}) collective-permute-start(bf16[128,1024]{1,0:T(8,128)(2,1)S(1)} %shard_map.133.refs_3_), channel_id=1, source_target_pairs={{0,8},{8,0},{16,24},{24,16},{32,40},{40,32},{48,56},{56,48},{64,72... | collective-permute-start | bytes 786440 | tf_op jit(solution)/shard_map/ppermute | solution.py:47
  331.5 4.3 collective-permute-start.13
  335.8 5.3 %collective-permute-start.14 = (bf16[128,256]{1,0:T(8,128)(2,1)S(1)}, bf16[128,256]{1,0:T(8,128)(2,1)S(1)}, u32[]{:S(2)}, u32[]{:S(2)}) collective-permute-start(bf16[128,256]{1,0:T(8,128)(2,1)S(1)} %pad_maximum_fusion.1.refs_0_), channel_id=1, source_target_pairs={{0,32},{8,40},{16,48},{24,56},{32,64},{40,72},{48,80},{56,88},{64,... | collective-permute-start | bytes 196616 | tf_op jit(solution)/shard_map/ppermute | solution.py:47
  335.9 5.3 %collective-permute-start.15 = (bf16[128,256]{1,0:T(8,128)(2,1)S(1)}, bf16[128,256]{1,0:T(8,128)(2,1)S(1)}, u32[]{:S(2)}, u32[]{:S(2)}) collective-permute-start(bf16[128,256]{1,0:T(8,128)(2,1)S(1)} %pad_maximum_fusion.1.refs_0_), channel_id=1, source_target_pairs={{0,224},{8,232},{16,240},{24,248},{32,0},{40,8},{48,16},{56,24},{6... | collective-permute-start | bytes 196616 | tf_op jit(solution)/shard_map/ppermute | solution.py:47
  342.0 12.8 %collective-permute-start.16 = (bf16[640,256]{1,0:T(8,128)(2,1)}, bf16[640,256]{1,0:T(8,128)(2,1)S(1)}, u32[]{:S(2)}, u32[]{:S(2)}) collective-permute-start(bf16[640,256]{1,0:T(8,128)(2,1)} %get-tuple-element.41.refs_5_), channel_id=1, source_target_pairs={{0,32},{8,40},{16,48},{24,56},{32,64},{40,72},{48,80},{56,88},{64,... | collective-permute-start | bytes 983048 | tf_op jit(solution)/shard_map/ppermute | solution.py:47
  342.1 12.8 %collective-permute-start.17 = (bf16[640,256]{1,0:T(8,128)(2,1)}, bf16[640,256]{1,0:T(8,128)(2,1)}, u32[]{:S(2)}, u32[]{:S(2)}) collective-permute-start(bf16[640,256]{1,0:T(8,128)(2,1)} %get-tuple-element.42), channel_id=1, source_target_pairs={{0,224},{8,232},{16,240},{24,248},{32,0},{40,8},{48,16},{56,24},{6... | collective-permute-start | bytes 983048 | tf_op jit(solution)/shard_map/ppermute | solution.py:47
  346.2 54.1 %all-to-all-start.1 = ((bf16[8,32,16,256]{3,2,1,0:T(8,128)(2,1)}), bf16[8,32,16,256]{3,2,1,0:T(8,128)(2,1)S(1)}, u32[]{:S(2)}, u32[]{:S(2)}) async-start(bf16[8,32,16,256]{3,2,1,0:T(8,128)(2,1)} %broadcast_in_dim.6), calls=%async_computation.1 | async-start | bytes 4194304 | tf_op jit(solution)/shard_map/all_to_all | solution.py:489
  356.0 13.5 %collective-permute-start.18 = (bf16[1152,256]{1,0:T(8,128)(2,1)S(1)}, bf16[1152,256]{1,0:T(8,128)(2,1)S(1)}, u32[]{:S(2)}, u32[]{:S(2)}) collective-permute-start(bf16[1152,256]{1,0:T(8,128)(2,1)S(1)} %get-tuple-element.43.refs_5_), channel_id=1, source_target_pairs={{0,32},{8,40},{16,48},{24,56},{32,64},{40,72},{48,80},{56,88},{64,... | collective-permute-start | bytes 1769480 | tf_op jit(solution)/shard_map/ppermute | solution.py:47
  356.1 13.4 %collective-permute-start.19 = (bf16[1152,256]{1,0:T(8,128)(2,1)S(1)}, bf16[1152,256]{1,0:T(8,128)(2,1)S(1)}, u32[]{:S(2)}, u32[]{:S(2)}) collective-permute-start(bf16[1152,256]{1,0:T(8,128)(2,1)S(1)} %get-tuple-element.44), channel_id=1, source_target_pairs={{0,224},{8,232},{16,240},{24,248},{32,0},{40,8},{48,16},{56,24},{6... | collective-permute-start | bytes 1769480 | tf_op jit(solution)/shard_map/ppermute | solution.py:47
  371.3 12.6 %collective-permute-start.20 = (bf16[1152,256]{1,0:T(8,128)(2,1)S(1)}, bf16[1152,256]{1,0:T(8,128)(2,1)S(1)}, u32[]{:S(2)}, u32[]{:S(2)}) collective-permute-start(bf16[1152,256]{1,0:T(8,128)(2,1)S(1)} %get-tuple-element.45.refs_5_), channel_id=1, source_target_pairs={{0,32},{8,40},{16,48},{24,56},{32,64},{40,72},{48,80},{56,88},{64,... | collective-permute-start | bytes 1769480 | tf_op jit(solution)/shard_map/ppermute | solution.py:47
  371.4 23.6 %collective-permute-start.21 = (bf16[1152,256]{1,0:T(8,128)(2,1)S(1)}, bf16[1152,256]{1,0:T(8,128)(2,1)S(1)}, u32[]{:S(2)}, u32[]{:S(2)}) collective-permute-start(bf16[1152,256]{1,0:T(8,128)(2,1)S(1)} %get-tuple-element.46), channel_id=1, source_target_pairs={{0,224},{8,232},{16,240},{24,248},{32,0},{40,8},{48,16},{56,24},{6... | collective-permute-start | bytes 1769480 | tf_op jit(solution)/shard_map/ppermute | solution.py:47
  384.7 15.6 %collective-permute-start.22 = (bf16[8,128,256]{2,1,0:T(8,128)(2,1)S(1)}, bf16[8,128,256]{2,1,0:T(8,128)(2,1)}, u32[]{:S(2)}, u32[]{:S(2)}) collective-permute-start(bf16[8,128,256]{2,1,0:T(8,128)(2,1)S(1)} %shard_map.142.refs_2_), channel_id=1, source_target_pairs={{0,8},{8,0},{16,24},{24,16},{32,40},{40,32},{48,56},{56,48},{64,72... | collective-permute-start | bytes 1572872 | tf_op jit(solution)/shard_map/ppermute | solution.py:47
  397.6 15.1 %collective-permute-start.23 = (bf16[1024,256]{1,0:T(8,128)(2,1)}, bf16[1024,256]{1,0:T(8,128)(2,1)}, u32[]{:S(2)}, u32[]{:S(2)}) collective-permute-start(bf16[1024,256]{1,0:T(8,128)(2,1)} %get-tuple-element.47.refs_5_), channel_id=1, source_target_pairs={{0,32},{8,40},{16,48},{24,56},{32,64},{40,72},{48,80},{56,88},{64,... | collective-permute-start | bytes 1572872 | tf_op jit(solution)/shard_map/ppermute | solution.py:47
  397.6 15.1 %collective-permute-start.24 = (bf16[1024,256]{1,0:T(8,128)(2,1)}, bf16[1024,256]{1,0:T(8,128)(2,1)}, u32[]{:S(2)}, u32[]{:S(2)}) collective-permute-start(bf16[1024,256]{1,0:T(8,128)(2,1)} %get-tuple-element.48), channel_id=1, source_target_pairs={{0,224},{8,232},{16,240},{24,248},{32,0},{40,8},{48,16},{56,24},{6... | collective-permute-start | bytes 1572872 | tf_op jit(solution)/shard_map/ppermute | solution.py:47
  402.7 10.0 %collective-permute-start.25 = (bf16[4,128,256]{2,1,0:T(8,128)(2,1)S(1)}, bf16[4,128,256]{2,1,0:T(8,128)(2,1)S(1)}, u32[]{:S(2)}, u32[]{:S(2)}) collective-permute-start(bf16[4,128,256]{2,1,0:T(8,128)(2,1)S(1)} %convert_element_type.3), channel_id=1, source_target_pairs={{0,16},{8,24},{16,0},{24,8},{32,48},{40,56},{48,32},{56,40},{64,80... | collective-permute-start | bytes 786440 | tf_op jit(solution)/shard_map/ppermute | solution.py:47
  415.4 24.4 %all-to-all-start.2 = ((f32[256,1,128]{2,1,0:T(1,128)}), f32[256,1,128]{2,1,0:T(1,128)S(1)}, u32[]{:S(2)}, u32[]{:S(2)}) async-start(f32[256,1,128]{2,1,0:T(1,128)} %broadcast_in_dim.7), calls=%async_computation.2 | async-start | bytes 262144 | tf_op jit(solution)/shard_map/all_to_all | solution.py:474
  427.0 13.6 %collective-permute-start.26 = (bf16[512,256]{1,0:T(8,128)(2,1)S(1)}, bf16[512,256]{1,0:T(8,128)(2,1)S(1)}, u32[]{:S(2)}, u32[]{:S(2)}) collective-permute-start(bf16[512,256]{1,0:T(8,128)(2,1)S(1)} %get-tuple-element.50), channel_id=1, source_target_pairs={{0,16},{8,24},{16,0},{24,8},{32,48},{40,56},{48,32},{56,40},{64,80... | collective-permute-start | bytes 786440 | tf_op jit(solution)/shard_map/ppermute | solution.py:47
  (16 other events, 72.0 us)
where the time goes:
time: 443 us; the launch traced here: 441 us
  Pallas kernels  315 us (71%)
  starting transfers between devices  72.8 us (16%)
  waiting for transfers between devices  38.4 us (9%)
  local copies, waits for them, and re-layouts  13.7 us (3%)
    pallas_call x22, Pallas kernels, call(): pl.pallas_call(body, grid_spec=pltpu.PrefetchScalarGridSpec(num_scalar_pr...  315 us
    ppermute x27, starting transfers between devices, send(): return lax.ppermute(value, 'fsdp', way)  49.7 us
    ppermute x27, waiting for transfers between devices, send(): return lax.ppermute(value, 'fsdp', way)  26.2 us
    all_to_all x1, starting transfers between devices, sum_all(): return jnp.sum(lax.all_to_all(copies, ('fsdp', 'tp'), 0, 0), axis=0)  11.6 us
    all_to_all x1, waiting for transfers between devices, sum_all(): return jnp.sum(lax.all_to_all(copies, ('fsdp', 'tp'), 0, 0), axis=0)  9.85 us
    unnamed x37, local copies, waits for them, and re-layouts  9.14 us
  transfers between devices with their start and end apart: 30, of which 8 were waited for; matrix products, arithmetic and copies ran while one was open for 1% of the time, Pallas kernels for 12%

commit v1 on v0

--- a/solution.py
+++ b/solution.py
@@ -137,14 +137,14 @@
             whole[pl.ds(row, ROWS), :] = blocks[dc * NY + dy]
 
 
-def project_kernel(n, first, place_ref, *refs):
-    xs, refs = refs[:n], refs[n:]
+def project_kernel(n, extra, first, place_ref, *refs):
+    xs, refs = refs[: n + extra], refs[n + extra :]
     vs, refs = refs[:n], refs[n:]
     ws, refs = refs[:n], refs[n:]
     if first:
-        sum_out, val_out, *whole = refs
+        sum_out, val_out, pick_out, *whole = refs
     else:
-        sum_in, val_in, sum_out, val_out, *whole = refs
+        sum_in, val_in, sum_out, val_out, pick_out, *whole = refs
 
     @pl.when(pl.program_id(0) == 0)
     def _():
@@ -155,29 +155,39 @@
 
     total = sum(dot(xs[j][...], whole[j][...]) for j in range(n))
     sum_out[...] = total if first else total + sum_in[...]
+    for j, x_ref in enumerate(xs[n if extra else 0 :]):
+        for y in range(NY):
+            column = pl.multiple_of((y * 2 + 1 - place_ref[2]) * ROWS, ROWS)
+            pick_out[j, :, y * ROWS : (y + 1) * ROWS] = x_ref[:, pl.ds(column, ROWS)]
 
 
 WIDE = NY * NC * ROWS
 TILE = 512
 
 
-def project(where, train_x, val_x, zs, weights, sums, waits=()):
-    n = len(zs)
+def project(where, train_x, val_x, zs, weights, sums, waits=(), others=()):
+    n, extra = len(zs), len(others)
     rows = train_x.shape[0]
     sum_specs = [pl.BlockSpec((TILE, HD), lambda i, p: (i, 0)), vmem((VSEQ, HD))]
     first = sums is None
-    return call(
-        functools.partial(project_kernel, n, first),
+    picks = extra or n
+    pick_spec = pl.BlockSpec((picks, TILE, NY * ROWS), lambda i, p: (0, i, 0))
+    return call(
+        functools.partial(project_kernel, n, extra, first),
         (where,),
-        (*[train_x] * n, *[val_x] * n, *weights, *([] if first else sums)),
+        (*[train_x] * (n + extra), *[val_x] * n, *weights, *([] if first else sums)),
         waits,
         (rows // TILE,),
-        [pl.BlockSpec((TILE, WIDE), lambda i, p, dz=dz: (i, z_of(p, dz))) for dz in zs]
+        [pl.BlockSpec((TILE, WIDE), lambda i, p, dz=dz: (i, z_of(p, dz))) for dz in (*zs, *others)]
         + [pl.BlockSpec((VSEQ, WIDE), lambda i, p, dz=dz: (0, z_of(p, dz))) for dz in zs]
         + [vmem((NC * NY, ROWS, HD))] * n
         + ([] if first else sum_specs),
-        sum_specs,
-        [jax.ShapeDtypeStruct((rows, HD), f32), jax.ShapeDtypeStruct((VSEQ, HD), f32)],
+        sum_specs + [pick_spec],
+        [
+            jax.ShapeDtypeStruct((rows, HD), f32),
+            jax.ShapeDtypeStruct((VSEQ, HD), f32),
+            jax.ShapeDtypeStruct((picks, rows, NY * ROWS), bf16),
+        ],
         cost(2 * rows * n * WIDE * HD, 2 * rows * n * WIDE),
         [pltpu.VMEM((WIDE, HD), bf16)] * n,
     )
@@ -256,38 +266,9 @@
     )
 
 
-def pick_kernel(place_ref, x_ref, out_ref, sems):
-    copies = []
-    for i in range(NZ * NY):
-        column = pl.multiple_of((2 * i + 1 - place_ref[2]) * ROWS, ROWS)
-        source = x_ref.at[:, pl.ds(column, ROWS)]
-        copies.append(pltpu.make_async_copy(source, out_ref.at[:, i * ROWS : (i + 1) * ROWS], sems.at[i]))
-    for copy in copies:
-        copy.start()
-    for copy in copies:
-        copy.wait()
-
-
-def other_core_columns(where, train_x, waits=()):
-    rows, columns = train_x.shape
-    anywhere = pl.BlockSpec(memory_space=pl.ANY)
-    return call(
-        pick_kernel,
-        (where,),
-        (train_x,),
-        waits,
-        (1,),
-        [anywhere],
-        anywhere,
-        jax.ShapeDtypeStruct((rows, columns // NC), bf16),
-        cost(0, 2 * rows * columns),
-        [pltpu.SemaphoreType.DMA((NZ * NY,))],
-    )
-
-
 def skills_kernel(place_ref, own_x, other_x, own_grads, other_grads, out_ref, total):
     total[...] = jnp.zeros_like(total)
-    for k, (x_ref, grads_ref) in enumerate(((own_x, own_grads), (other_x, other_grads))):
+    for k, (x_ref, grads_ref) in enumerate(((own_x, own_grads), (other_x.at[0], other_grads))):
         for m in range(MEMBERS):
             tokens = slice(m * SEQ, (m + 1) * SEQ)
             total[place_ref[3 + k * MEMBERS + m]] += dot(grads_ref[:, tokens], x_ref[tokens, :])
@@ -309,7 +290,7 @@
         (len(zs), NY),
         [
             pl.BlockSpec((rows, ROWS), lambda i, j, p: (0, pair_of(i, j, p) * 2 + p[2])),
-            pl.BlockSpec((rows, ROWS), lambda i, j, p: (0, pair_of(i, j, p))),
+            pl.BlockSpec((1, rows, ROWS), lambda i, j, p: (i, 0, lax.rem(p[1] + j, NY))),
             pl.BlockSpec((HD, rows), lambda i, j, p: (0, 0)),
             pl.BlockSpec((HD, rows), lambda i, j, p: (0, 0)),
         ],
@@ -370,17 +351,35 @@
         refs[-1][i] = ref[...]
 
 
-def stacked(arrays):
+def stacked(arrays, waits=()):
     tails = [pl.BlockSpec((HD, ROWS), lambda i, n=a.shape[0] // HD - 1: (n, 0)) for a in arrays]
     return call(
         stack_kernel,
         (),
         arrays,
-        (),
+        waits,
         (1,),
         tails,
         vmem((len(arrays), HD, ROWS)),
         jax.ShapeDtypeStruct((len(arrays), HD, ROWS), bf16),
+        cost(0, 2**20),
+    )
+
+
+def copies_kernel(from_ref, to_ref):
+    to_ref[0] = from_ref[...]
+
+
+def copies(array, count, waits):
+    return call(
+        copies_kernel,
+        (),
+        (array,),
+        waits,
+        (count,),
+        [vmem(array.shape)],
+        pl.BlockSpec((1,) + array.shape, lambda i: (i, 0, 0, 0)),
+        jax.ShapeDtypeStruct((count,) + array.shape, array.dtype),
         cost(0, 2**20),
     )
 
@@ -486,7 +485,6 @@
     part = VSEQ // 8
     own_tokens = lax.dynamic_slice_in_dim(val_x, t * part, part).reshape(part, 32, ROWS)
     crossed = lax.all_to_all(own_tokens.transpose(1, 0, 2), "fsdp", 0, 0)
-    columns = lax.all_to_all(jnp.broadcast_to(crossed, (8,) + crossed.shape), "tp", 0, 0)
 
     own = value_weight
     quad = jnp.stack([own, send(own, YHI), send(own, CORE), send(own, DIAGONAL)])
@@ -495,16 +493,18 @@
     up1, down1 = send(quad, UP), send(quad, DOWN)
     up1, down1 = joined((up1, down1), (attention,))
     up2, down2 = send(up1, UP), send(down1, DOWN)
-    sums = project(where, train_x, val_x, (0,), [quad], None, (attention, up1))
-    picked = other_core_columns(where, train_x, (up1,))
-    other_x = send(picked, CORE)
-    up2, down2 = joined((up2, down2), (sums[1], picked))
+    *sums, picked = project(where, train_x, val_x, (0,), [quad], None, (attention, up1), (4, 0))
+    other_x = {(4,): send(picked[:1], CORE), (0,): send(picked[1:], CORE)}
+    up2, down2 = joined((up2, down2), (sums[1],))
     up3, down3 = send(up2, UP), send(down2, DOWN)
-    sums = project(where, train_x, val_x, (1, 7), [down1, up1], sums)
+    *sums, picked = project(where, train_x, val_x, (1, 7), [down1, up1], sums)
+    other_x[1, 7] = send(picked, CORE)
     up3, down3 = joined((up3, down3), (sums[1], crossed))
     last = jnp.concatenate([send(up3[:2], UP), send(down3[2:], DOWN)])
-    sums = project(where, train_x, val_x, (2, 6), [down2, up2], sums)
-    sums = project(where, train_x, val_x, (3, 5), [down3, up3], sums)
+    *sums, picked = project(where, train_x, val_x, (2, 6), [down2, up2], sums)
+    other_x[2, 6] = send(picked, CORE)
+    *sums, picked = project(where, train_x, val_x, (3, 5), [down3, up3], sums)
+    other_x[3, 5] = send(picked, CORE)
     own_pull = val_pulls(where, val_x, last, sums[1], val_attention, val_target)
     pull = jnp.concatenate([own_pull, send(own_pull, YHI)], axis=1)
     p_up, p_down = send(pull, UP), send(pull, DOWN)
@@ -512,11 +512,12 @@
     grads = (grads, send(grads, CORE))
 
     def terms(zs, *waits):
-        return skill_terms(where, train_x, other_x, grads, zs, waits)
+        return skill_terms(where, train_x, other_x[zs], grads, zs, waits)
 
     pulls = {0: pull, 1: p_down, 7: p_up}
     sent, (up, down) = ring_step(1, terms((4,)), p_up, p_down)
     mine = terms((3, 5), sent)
+    columns = lax.all_to_all(copies(crossed, NX * NL, (sent,)), "tp", 0, 0)
     pulls[6], pulls[2] = up, down
     sent, (up, down) = ring_step(2, mine, up, down)
     mine = terms((2, 6), sent)
@@ -525,7 +526,7 @@
     mine = terms((1, 7), sent)
     pulls[4] = up
     sent, (up, down) = ring_step(4, mine, up, down)
-    near_pulls = stacked([pulls[dz] for dz in range(NZ)])
+    near_pulls = stacked([pulls[dz] for dz in range(NZ)], (sent,))
     here = directions_of(where, val_skill, near_pulls, send(near_pulls, CORE), columns)
     there = send(here.astype(bf16), YHI)
     keep, give, local = local_transfer(terms((0,), sent, here), up, down, here, there)

time: 443 us -> 186 us (0.42)
  Pallas kernels: 315 us -> 62.6 us
  waiting for transfers between devices: 38.4 us -> 32.9 us
    pallas_call x22, Pallas kernels: 315 us -> 62.6 us  [call(): pl.pallas_call(body, grid_spec=pltpu.PrefetchScalarGridSpec(num_scalar_pr...]
    ppermute x27 -> x31, waiting for transfers between devices: 26.2 us -> 23 us  [send(): return lax.ppermute(value, 'fsdp', way)]
    ppermute x27 -> x31, starting transfers between devices: 49.7 us -> 51.6 us  [send(): return lax.ppermute(value, 'fsdp', way)]
    unnamed x37 -> x41, local copies, waits for them, and re-layouts: 9.14 us -> 9.66 us
  transfers between devices with their start and end apart: 30 -> 34, of which waited for: 8 -> 9; matrix products, arithmetic and copies ran while one was open for 1% -> 2% of each run, Pallas kernels for 12% -> 29%
where the time goes in v1:
time: 186 us; the launch traced here: 185 us
  starting transfers between devices  73.4 us (39%)
  Pallas kernels  62.6 us (34%)
  waiting for transfers between devices  32.9 us (18%)
  local copies, waits for them, and re-layouts  14.1 us (8%)
    pallas_call x22, Pallas kernels, call(): pl.pallas_call(body, grid_spec=pltpu.PrefetchScalarGridSpec(num_scalar_pr...  62.6 us
    ppermute x31, starting transfers between devices, send(): return lax.ppermute(value, 'fsdp', way)  51.6 us
    ppermute x31, waiting for transfers between devices, send(): return lax.ppermute(value, 'fsdp', way)  23 us
    all_to_all x1, starting transfers between devices, sum_all(): return jnp.sum(lax.all_to_all(copies, ('fsdp', 'tp'), 0, 0), axis=0)  10.2 us
    all_to_all x1, waiting for transfers between devices, sum_all(): return jnp.sum(lax.all_to_all(copies, ('fsdp', 'tp'), 0, 0), axis=0)  9.85 us
    unnamed x41, local copies, waits for them, and re-layouts  9.66 us
    all_to_all x1, starting transfers between devices, on_device(): crossed = lax.all_to_all(own_tokens.transpose(1, 0, 2), 'fsdp', 0, 0)  7.25 us
    all_to_all x1, starting transfers between devices, on_device(): columns = lax.all_to_all(copies(crossed, NX * NL, (sent,)), 'tp', 0, 0)  4.41 us
  transfers between devices with their start and end apart: 34, of which 9 were waited for; matrix products, arithmetic and copies ran while one was open for 2% of the time, Pallas kernels for 29%

profile of v1, /device:TPU:1, one launch (start us, length us, event | category | flops | bytes accessed | tf_op | source)
XLA Modules:
  0.0 185.1 jit_solution(5717473751168525631)
XLA Ops:
  0.6 3.8 %collective-permute-start = (bf16[256,128]{1,0:T(8,128)(2,1)}, bf16[256,128]{1,0:T(8,128)(2,1)S(1)}, u32[]{:S(2)}, u32[]{:S(2)}) collective-permute-start(bf16[256,128]{1,0:T(8,128)(2,1)} %param.16), channel_id=1, source_target_pairs={{0,16},{8,24},{16,0},{24,8},{32,48},{40,56},{48,32},{56,40},{64,80... | collective-permute-start | bytes 196616 | tf_op jit(solution)/shard_map/ppermute | solution.py:47
  7.1 3.7 %collective-permute-done.2 = bf16[256,128]{1,0:T(8,128)(2,1)S(1)} collective-permute-done((bf16[256,128]{1,0:T(8,128)(2,1)}, bf16[256,128]{1,0:T(8,128)(2,1)S(1)}, u32[]{:S(2)}, u32[]{:S(2)}) %collective-permute-start.2) | collective-permute-done | bytes 65568 | tf_op jit(solution)/shard_map/ppermute | solution.py:47
  13.4 4.0 %collective-permute-start.4 = (bf16[4,256,128]{2,1,0:T(8,128)(2,1)S(1)}, bf16[4,256,128]{2,1,0:T(8,128)(2,1)S(1)}, u32[]{:S(2)}, u32[]{:S(2)}) collective-permute-start(bf16[4,256,128]{2,1,0:T(8,128)(2,1)S(1)} %pad_maximum_fusion.refs_3_.refs_5_), channel_id=1, source_target_pairs={{0,224},{8,232},{16,240},{24,248},{32,0},{40,8},{48,16},{56,24},{6... | collective-permute-start | bytes 786440 | tf_op jit(solution)/shard_map/ppermute | solution.py:47
  22.3 4.6 %shard_map.123.refs_2_.refs_6_.refs_4_ = bf16[4,8,256,256]{3,2,1,0:T(8,128)(2,1)} custom-call(bf16[1024,1024]{1,0:T(8,128)(2,1)S(1)} %copy-done.4, bf16[1024,128]{1,0:T(8,128)(2,1)S(1)} %copy-done.10, bf16[1,8,128,128]{3,2,1,0:T(8,128)(2,1)S(1)} %shard_map.122.refs_2_.refs_4_, bf16[4,256,128]{2,1,0:T(8,128)(2,1)S(1)} %pad_maximum_fusion.refs_3_.refs_5_), custom_call_target="tpu_custom_call" | custom-call | flops 8388608 | bytes 131072 | tf_op jit(solution)/shard_map/pallas_call | solution.py:56
  27.0 2.7 %collective-permute-start.7 = (bf16[4,256,128]{2,1,0:T(8,128)(2,1)S(1)}, bf16[4,256,128]{2,1,0:T(8,128)(2,1)S(1)}, u32[]{:S(2)}, u32[]{:S(2)}) collective-permute-start(bf16[4,256,128]{2,1,0:T(8,128)(2,1)S(1)} %get-tuple-element.33.refs_5_), channel_id=1, source_target_pairs={{0,224},{8,232},{16,240},{24,248},{32,0},{40,8},{48,16},{56,24},{6... | collective-permute-start | bytes 786440 | tf_op jit(solution)/shard_map/ppermute | solution.py:47
  31.4 7.3 %all-to-all-start = ((bf16[32,16,256]{2,1,0:T(8,128)(2,1)}), bf16[32,16,256]{2,1,0:T(8,128)(2,1)S(1)}, u32[]{:S(2)}, u32[]{:S(2)}) async-start(bf16[32,16,256]{2,1,0:T(8,128)(2,1)} %bitcast.16), calls=%async_computation | async-start | bytes 524288 | tf_op jit(solution)/shard_map/all_to_all | solution.py:487
  38.9 4.2 %shard_map.125 = (f32[1024,128]{1,0:T(8,128)S(1)}, f32[128,128]{1,0:T(8,128)S(1)}, bf16[2,1024,512]{2,1,0:T(8,128)(2,1)S(1)}) custom-call(s32[11]{0:T(128)S(1)} %concatenate.9.refs_0_, bf16[1024,8192]{1,0:T(8,128)(2,1)} %refs_1_.27, bf16[1024,8192]{1,0:T(8,128)(2,1)} %refs_1_.27, bf16[1024,8192]{1,0:T(8,128)(2,1)} %refs_1_.27, bf16[128,8192]{1,0:T(8,128)(2,1)} %refs_1_.20, ...), custom_call_target="tpu_custom_call" | custom-call | flops 4194304 | bytes 32768 | tf_op jit(solution)/shard_map/pallas_call | solution.py:56
  47.2 5.2 %shard_map.127 = (f32[1024,128]{1,0:T(8,128)S(1)}, f32[128,128]{1,0:T(8,128)S(1)}, bf16[2,1024,512]{2,1,0:T(8,128)(2,1)}) custom-call(s32[11]{0:T(128)S(1)} %concatenate.9.refs_0_, bf16[1024,8192]{1,0:T(8,128)(2,1)} %refs_1_.27, bf16[1024,8192]{1,0:T(8,128)(2,1)} %refs_1_.27, bf16[128,8192]{1,0:T(8,128)(2,1)} %refs_1_.20, bf16[128,8192]{1,0:T(8,128)(2,1)} %refs_1_.20, ...), custom_call_target="tpu_custom_call" | custom-call | flops 8388608 | bytes 65536 | tf_op jit(solution)/shard_map/pallas_call | solution.py:56
  52.4 5.2 %shard_map.129 = (f32[1024,128]{1,0:T(8,128)S(1)}, f32[128,128]{1,0:T(8,128)S(1)}, bf16[2,1024,512]{2,1,0:T(8,128)(2,1)}) custom-call(s32[11]{0:T(128)S(1)} %concatenate.9.refs_0_, bf16[1024,8192]{1,0:T(8,128)(2,1)} %refs_1_.27, bf16[1024,8192]{1,0:T(8,128)(2,1)} %refs_1_.27, bf16[128,8192]{1,0:T(8,128)(2,1)} %refs_1_.20, bf16[128,8192]{1,0:T(8,128)(2,1)} %refs_1_.20, ...), custom_call_target="tpu_custom_call" | custom-call | flops 8388608 | bytes 65536 | tf_op jit(solution)/shard_map/pallas_call | solution.py:56
  57.7 5.2 %shard_map.130 = (f32[1024,128]{1,0:T(8,128)S(1)}, f32[128,128]{1,0:T(8,128)S(1)}, bf16[2,1024,512]{2,1,0:T(8,128)(2,1)}) custom-call(s32[11]{0:T(128)S(1)} %concatenate.9.refs_0_, bf16[1024,8192]{1,0:T(8,128)(2,1)} %refs_1_.27, bf16[1024,8192]{1,0:T(8,128)(2,1)} %refs_1_.27, bf16[128,8192]{1,0:T(8,128)(2,1)} %refs_1_.20, bf16[128,8192]{1,0:T(8,128)(2,1)} %refs_1_.20, ...), custom_call_target="tpu_custom_call" | custom-call | flops 8388608 | bytes 65536 | tf_op jit(solution)/shard_map/pallas_call | solution.py:56
  65.7 2.5 %collective-permute-start.11 = (bf16[2,256,128]{2,1,0:T(8,128)(2,1)S(1)}, bf16[2,256,128]{2,1,0:T(8,128)(2,1)S(1)}, u32[]{:S(2)}, u32[]{:S(2)}) collective-permute-start(bf16[2,256,128]{2,1,0:T(8,128)(2,1)S(1)} %slice.17), channel_id=1, source_target_pairs={{0,224},{8,232},{16,240},{24,248},{32,0},{40,8},{48,16},{56,24},{6... | collective-permute-start | bytes 393224 | tf_op jit(solution)/shard_map/ppermute | solution.py:47
  68.2 3.6 %collective-permute-done.10 = bf16[2,256,128]{2,1,0:T(8,128)(2,1)S(1)} collective-permute-done((bf16[2,256,128]{2,1,0:T(8,128)(2,1)S(1)}, bf16[2,256,128]{2,1,0:T(8,128)(2,1)S(1)}, u32[]{:S(2)}, u32[]{:S(2)}) %collective-permute-start.10) | collective-permute-done | bytes 131104 | tf_op jit(solution)/shard_map/ppermute | solution.py:47
  73.9 3.1 %collective-permute-start.17 = (bf16[128,128]{1,0:T(8,128)(2,1)S(1)}, bf16[128,128]{1,0:T(8,128)(2,1)S(1)}, u32[]{:S(2)}, u32[]{:S(2)}) collective-permute-start(bf16[128,128]{1,0:T(8,128)(2,1)S(1)} %shard_map.131.refs_6_), channel_id=1, source_target_pairs={{0,16},{8,24},{16,0},{24,8},{32,48},{40,56},{48,32},{56,40},{64,80... | collective-permute-start | bytes 98312 | tf_op jit(solution)/shard_map/ppermute | solution.py:47
  77.0 6.8 %shard_map.132.refs_3_ = bf16[128,1024]{1,0:T(8,128)(2,1)S(1)} custom-call(s32[11]{0:T(128)S(1)} %concatenate.9.refs_0_, bf16[1024,8192]{1,0:T(8,128)(2,1)} %refs_1_.27, bf16[4,256,128]{2,1,0:T(8,128)(2,1)S(1)} %constant_dynamic-update-slice_fusion.refs_2_, f32[1024,128]{1,0:T(8,128)S(1)} %get-tuple-element.44.refs_3_, ...), custom_call_target="tpu_custom_call" | custom-call | flops 16777216 | bytes 131072 | tf_op jit(solution)/shard_map/pallas_call | solution.py:56
  85.7 2.4 %collective-permute-start.19 = (bf16[128,256]{1,0:T(8,128)(2,1)S(1)}, bf16[128,256]{1,0:T(8,128)(2,1)S(1)}, u32[]{:S(2)}, u32[]{:S(2)}) collective-permute-start(bf16[128,256]{1,0:T(8,128)(2,1)S(1)} %pad_maximum_fusion.1.refs_0_), channel_id=1, source_target_pairs={{0,224},{8,232},{16,240},{24,248},{32,0},{40,8},{48,16},{56,24},{6... | collective-permute-start | bytes 196616 | tf_op jit(solution)/shard_map/ppermute | solution.py:47
  88.1 2.4 %shard_map.133.refs_0_ = f32[1,2,512,256]{3,2,1,0:T(8,128)S(1)} custom-call(s32[11]{0:T(128)S(1)} %concatenate.9.refs_0_, bf16[1024,8192]{1,0:T(8,128)(2,1)} %refs_1_.27, bf16[1,1024,512]{2,1,0:T(8,128)(2,1)S(1)} %collective-permute-done.16.refs_2_, bf16[128,1024]{1,0:T(8,128)(2,1)S(1)} %shard_map.132.refs_3_, ...), custom_call_target="tpu_custom_call" | custom-call | flops 4194304 | bytes 81920 | tf_op jit(solution)/shard_map/pallas_call | solution.py:56
  91.5 2.4 %collective-permute-start.20 = (bf16[640,256]{1,0:T(8,128)(2,1)}, bf16[640,256]{1,0:T(8,128)(2,1)S(1)}, u32[]{:S(2)}, u32[]{:S(2)}) collective-permute-start(bf16[640,256]{1,0:T(8,128)(2,1)} %get-tuple-element.49.refs_5_.refs_1_), channel_id=1, source_target_pairs={{0,32},{8,40},{16,48},{24,56},{32,64},{40,72},{48,80},{56,88},{64,... | collective-permute-start | bytes 983048 | tf_op jit(solution)/shard_map/ppermute | solution.py:47
  95.8 4.4 %all-to-all-start.1 = ((bf16[8,32,16,256]{3,2,1,0:T(8,128)(2,1)}), bf16[8,32,16,256]{3,2,1,0:T(8,128)(2,1)S(1)}, u32[]{:S(2)}, u32[]{:S(2)}) async-start(bf16[8,32,16,256]{3,2,1,0:T(8,128)(2,1)} %copy-done.3), calls=%async_computation.1 | async-start | bytes 4194304 | tf_op jit(solution)/shard_map/all_to_all | solution.py:520
  100.2 4.2 %shard_map.135.refs_0_ = f32[2,2,512,256]{3,2,1,0:T(8,128)S(1)} custom-call(s32[11]{0:T(128)S(1)} %concatenate.9.refs_0_, bf16[1024,8192]{1,0:T(8,128)(2,1)} %refs_1_.27, bf16[2,1024,512]{2,1,0:T(8,128)(2,1)} %collective-permute-done.15.refs_2_, bf16[128,1024]{1,0:T(8,128)(2,1)S(1)} %shard_map.132.refs_3_, ...), custom_call_target="tpu_custom_call" | custom-call | flops 8388608 | bytes 163840 | tf_op jit(solution)/shard_map/pallas_call | solution.py:56
  107.4 4.2 %shard_map.137.refs_0_ = f32[2,2,512,256]{3,2,1,0:T(8,128)S(1)} custom-call(s32[11]{0:T(128)S(1)} %concatenate.9.refs_0_, bf16[1024,8192]{1,0:T(8,128)(2,1)} %refs_1_.27, bf16[2,1024,512]{2,1,0:T(8,128)(2,1)} %collective-permute-done.14.refs_2_, bf16[128,1024]{1,0:T(8,128)(2,1)S(1)} %shard_map.132.refs_3_, ...), custom_call_target="tpu_custom_call" | custom-call | flops 8388608 | bytes 163840 | tf_op jit(solution)/shard_map/pallas_call | solution.py:56
  113.0 5.7 %collective-permute-done.22.refs_1_.refs_5_ = bf16[1152,256]{1,0:T(8,128)(2,1)S(1)} collective-permute-done((bf16[1152,256]{1,0:T(8,128)(2,1)S(1)}, bf16[1152,256]{1,0:T(8,128)(2,1)S(1)}, u32[]{:S(2)}, u32[]{:S(2)}) %collective-permute-start.22) | collective-permute-done | bytes 589856 | tf_op jit(solution)/shard_map/ppermute | solution.py:47
  123.2 3.5 %collective-permute-start.5 = (bf16[1,1024,512]{2,1,0:T(8,128)(2,1)}, bf16[1,1024,512]{2,1,0:T(8,128)(2,1)}, u32[]{:S(2)}, u32[]{:S(2)}) collective-permute-start(bf16[1,1024,512]{2,1,0:T(8,128)(2,1)} %get-tuple-element.61), channel_id=1, source_target_pairs={{0,8},{8,0},{16,24},{24,16},{32,40},{40,32},{48,56},{56,48},{64,72... | collective-permute-start | bytes 3145736 | tf_op jit(solution)/shard_map/ppermute | solution.py:47
  126.8 4.2 %shard_map.139.refs_0_ = f32[2,2,512,256]{3,2,1,0:T(8,128)S(1)} custom-call(s32[11]{0:T(128)S(1)} %concatenate.9.refs_0_, bf16[1024,8192]{1,0:T(8,128)(2,1)} %refs_1_.27, bf16[2,1024,512]{2,1,0:T(8,128)(2,1)} %collective-permute-done.13.refs_2_, bf16[128,1024]{1,0:T(8,128)(2,1)S(1)} %shard_map.132.refs_3_, ...), custom_call_target="tpu_custom_call" | custom-call | flops 8388608 | bytes 163840 | tf_op jit(solution)/shard_map/pallas_call | solution.py:56
  133.6 2.5 %shard_map.140 = (bf16[1024,256]{1,0:T(8,128)(2,1)S(1)}, bf16[1024,256]{1,0:T(8,128)(2,1)}) custom-call(f32[2,2,512,256]{3,2,1,0:T(8,128)} %copy-done.1, bf16[1152,256]{1,0:T(8,128)(2,1)S(1)} %collective-permute-done.24.refs_1_.refs_4_, bf16[1152,256]{1,0:T(8,128)(2,1)S(1)} %collective-permute-done.25.refs_2_), custom_call_target="tpu_custom_call" | custom-call | flops 16384 | bytes 65536 | tf_op jit(solution)/shard_map/pallas_call | solution.py:56
  137.0 4.2 %collective-permute-start.26 = (bf16[8,128,256]{2,1,0:T(8,128)(2,1)}, bf16[8,128,256]{2,1,0:T(8,128)(2,1)}, u32[]{:S(2)}, u32[]{:S(2)}) collective-permute-start(bf16[8,128,256]{2,1,0:T(8,128)(2,1)} %shard_map.141.refs_2_), channel_id=1, source_target_pairs={{0,8},{8,0},{16,24},{24,16},{32,40},{40,32},{48,56},{56,48},{64,72... | collective-permute-start | bytes 1572872 | tf_op jit(solution)/shard_map/ppermute | solution.py:47
  141.2 3.0 %collective-permute-start.27 = (bf16[1024,256]{1,0:T(8,128)(2,1)S(1)}, bf16[1024,256]{1,0:T(8,128)(2,1)}, u32[]{:S(2)}, u32[]{:S(2)}) collective-permute-start(bf16[1024,256]{1,0:T(8,128)(2,1)S(1)} %get-tuple-element.55.refs_8_.refs_5_), channel_id=1, source_target_pairs={{0,32},{8,40},{16,48},{24,56},{32,64},{40,72},{48,80},{56,88},{64,... | collective-permute-start | bytes 1572872 | tf_op jit(solution)/shard_map/ppermute | solution.py:47
  144.2 2.5 %shard_map.143.refs_6_.refs_3_ = f32[4,128,256]{2,1,0:T(8,128)S(1)} custom-call(s32[11]{0:T(128)S(1)} %concatenate.9.refs_0_, s32[32]{0:T(128)S(1)} %copy-done.18, bf16[8,128,256]{2,1,0:T(8,128)(2,1)} %shard_map.141.refs_2_, bf16[8,128,256]{2,1,0:T(8,128)(2,1)} %collective-permute-done.26.refs_3_, bf16[8,32,16,256]{3,2,1,0:T(8,128)(2,1)S(1)} %all-to-all-done.1.refs_4_), custom_call_target="tpu_custom_call" | custom-call | flops 4194304 | bytes 65536 | tf_op jit(solution)/shard_map/pallas_call | solution.py:56
  147.7 2.5 %shard_map.144.refs_0_ = f32[1,2,512,256]{3,2,1,0:T(8,128)S(1)} custom-call(s32[11]{0:T(128)S(1)} %concatenate.9.refs_0_, bf16[1024,8192]{1,0:T(8,128)(2,1)} %refs_1_.27, bf16[1,1024,512]{2,1,0:T(8,128)(2,1)} %collective-permute-done.5.refs_2_, bf16[128,1024]{1,0:T(8,128)(2,1)S(1)} %shard_map.132.refs_3_, ...), custom_call_target="tpu_custom_call" | custom-call | flops 4194304 | bytes 81920 | tf_op jit(solution)/shard_map/pallas_call | solution.py:56
  150.3 5.8 %collective-permute-done.27.refs_1_ = bf16[1024,256]{1,0:T(8,128)(2,1)} collective-permute-done((bf16[1024,256]{1,0:T(8,128)(2,1)S(1)}, bf16[1024,256]{1,0:T(8,128)(2,1)}, u32[]{:S(2)}, u32[]{:S(2)}) %collective-permute-start.27) | collective-permute-done | bytes 524320 | tf_op jit(solution)/shard_map/ppermute | solution.py:47
  160.5 10.2 %all-to-all-start.2 = ((f32[256,1,128]{2,1,0:T(1,128)}), f32[256,1,128]{2,1,0:T(1,128)S(1)}, u32[]{:S(2)}, u32[]{:S(2)}) async-start(f32[256,1,128]{2,1,0:T(1,128)} %broadcast_in_dim.3), calls=%async_computation.2 | async-start | bytes 262144 | tf_op jit(solution)/shard_map/all_to_all | solution.py:473
  170.7 3.0 %collective-permute-start.30 = (bf16[512,256]{1,0:T(8,128)(2,1)S(1)}, bf16[512,256]{1,0:T(8,128)(2,1)S(1)}, u32[]{:S(2)}, u32[]{:S(2)}) collective-permute-start(bf16[512,256]{1,0:T(8,128)(2,1)S(1)} %get-tuple-element.58), channel_id=1, source_target_pairs={{0,16},{8,24},{16,0},{24,8},{32,48},{40,56},{48,32},{56,40},{64,80... | collective-permute-start | bytes 786440 | tf_op jit(solution)/shard_map/ppermute | solution.py:47
  173.7 9.8 %all-to-all-done.2 = f32[256,1,128]{2,1,0:T(1,128)S(1)} async-done(((f32[256,1,128]{2,1,0:T(1,128)}), f32[256,1,128]{2,1,0:T(1,128)S(1)}, u32[]{:S(2)}, u32[]{:S(2)}) %all-to-all-start.2) | async-done | bytes 131104 | tf_op jit(solution)/shard_map/all_to_all | solution.py:473
  (117 shorter events, 45.1 us)
Async XLA Ops:
  0.6 6.5 %collective-permute-start = (bf16[256,128]{1,0:T(8,128)(2,1)}, bf16[256,128]{1,0:T(8,128)(2,1)S(1)}, u32[]{:S(2)}, u32[]{:S(2)}) collective-permute-start(bf16[256,128]{1,0:T(8,128)(2,1)} %param.16), channel_id=1, source_target_pairs={{0,16},{8,24},{16,0},{24,8},{32,48},{40,56},{48,32},{56,40},{64,80... | collective-permute-start | bytes 196616 | tf_op jit(solution)/shard_map/ppermute | solution.py:47
  5.4 5.4 %collective-permute-start.2 = (bf16[256,128]{1,0:T(8,128)(2,1)}, bf16[256,128]{1,0:T(8,128)(2,1)S(1)}, u32[]{:S(2)}, u32[]{:S(2)}) collective-permute-start(bf16[256,128]{1,0:T(8,128)(2,1)} %param.16), channel_id=1, source_target_pairs={{0,24},{8,16},{16,8},{24,0},{32,56},{40,48},{48,40},{56,32},{64,88... | collective-permute-start | bytes 196616 | tf_op jit(solution)/shard_map/ppermute | solution.py:47
  11.7 15.2 %collective-permute-start.3 = (bf16[4,256,128]{2,1,0:T(8,128)(2,1)S(1)}, bf16[4,256,128]{2,1,0:T(8,128)(2,1)S(1)}, u32[]{:S(2)}, u32[]{:S(2)}) collective-permute-start(bf16[4,256,128]{2,1,0:T(8,128)(2,1)S(1)} %pad_maximum_fusion.refs_3_.refs_5_), channel_id=1, source_target_pairs={{0,32},{8,40},{16,48},{24,56},{32,64},{40,72},{48,80},{56,88},{64,... | collective-permute-start | bytes 786440 | tf_op jit(solution)/shard_map/ppermute | solution.py:47
  13.4 13.5 %collective-permute-start.4 = (bf16[4,256,128]{2,1,0:T(8,128)(2,1)S(1)}, bf16[4,256,128]{2,1,0:T(8,128)(2,1)S(1)}, u32[]{:S(2)}, u32[]{:S(2)}) collective-permute-start(bf16[4,256,128]{2,1,0:T(8,128)(2,1)S(1)} %pad_maximum_fusion.refs_3_.refs_5_), channel_id=1, source_target_pairs={{0,224},{8,232},{16,240},{24,248},{32,0},{40,8},{48,16},{56,24},{6... | collective-permute-start | bytes 786440 | tf_op jit(solution)/shard_map/ppermute | solution.py:47
  26.9 17.5 %collective-permute-start.6 = (bf16[4,256,128]{2,1,0:T(8,128)(2,1)S(1)}, bf16[4,256,128]{2,1,0:T(8,128)(2,1)S(1)}, u32[]{:S(2)}, u32[]{:S(2)}) collective-permute-start(bf16[4,256,128]{2,1,0:T(8,128)(2,1)S(1)} %get-tuple-element.31.refs_7_.refs_6_), channel_id=1, source_target_pairs={{0,32},{8,40},{16,48},{24,56},{32,64},{40,72},{48,80},{56,88},{64,... | collective-permute-start | bytes 786440 | tf_op jit(solution)/shard_map/ppermute | solution.py:47
  27.0 17.4 %collective-permute-start.7 = (bf16[4,256,128]{2,1,0:T(8,128)(2,1)S(1)}, bf16[4,256,128]{2,1,0:T(8,128)(2,1)S(1)}, u32[]{:S(2)}, u32[]{:S(2)}) collective-permute-start(bf16[4,256,128]{2,1,0:T(8,128)(2,1)S(1)} %get-tuple-element.33.refs_5_), channel_id=1, source_target_pairs={{0,224},{8,232},{16,240},{24,248},{32,0},{40,8},{48,16},{56,24},{6... | collective-permute-start | bytes 786440 | tf_op jit(solution)/shard_map/ppermute | solution.py:47
  31.4 26.3 %all-to-all-start = ((bf16[32,16,256]{2,1,0:T(8,128)(2,1)}), bf16[32,16,256]{2,1,0:T(8,128)(2,1)S(1)}, u32[]{:S(2)}, u32[]{:S(2)}) async-start(bf16[32,16,256]{2,1,0:T(8,128)(2,1)} %bitcast.16), calls=%async_computation | async-start | bytes 524288 | tf_op jit(solution)/shard_map/all_to_all | solution.py:487
  44.4 13.2 %collective-permute-start.8 = (bf16[4,256,128]{2,1,0:T(8,128)(2,1)S(1)}, bf16[4,256,128]{2,1,0:T(8,128)(2,1)S(1)}, u32[]{:S(2)}, u32[]{:S(2)}) collective-permute-start(bf16[4,256,128]{2,1,0:T(8,128)(2,1)S(1)} %get-tuple-element.35.refs_6_), channel_id=1, source_target_pairs={{0,32},{8,40},{16,48},{24,56},{32,64},{40,72},{48,80},{56,88},{64,... | collective-permute-start | bytes 786440 | tf_op jit(solution)/shard_map/ppermute | solution.py:47
  45.8 11.8 %collective-permute-start.9 = (bf16[4,256,128]{2,1,0:T(8,128)(2,1)S(1)}, bf16[4,256,128]{2,1,0:T(8,128)(2,1)S(1)}, u32[]{:S(2)}, u32[]{:S(2)}) collective-permute-start(bf16[4,256,128]{2,1,0:T(8,128)(2,1)S(1)} %get-tuple-element.36.refs_5_), channel_id=1, source_target_pairs={{0,224},{8,232},{16,240},{24,248},{32,0},{40,8},{48,16},{56,24},{6... | collective-permute-start | bytes 786440 | tf_op jit(solution)/shard_map/ppermute | solution.py:47
  62.9 37.3 %collective-permute-start.15 = (bf16[2,1024,512]{2,1,0:T(8,128)(2,1)}, bf16[2,1024,512]{2,1,0:T(8,128)(2,1)}, u32[]{:S(2)}, u32[]{:S(2)}) collective-permute-start(bf16[2,1024,512]{2,1,0:T(8,128)(2,1)} %get-tuple-element.48), channel_id=1, source_target_pairs={{0,8},{8,0},{16,24},{24,16},{32,40},{40,32},{48,56},{56,48},{64,72... | collective-permute-start | bytes 6291464 | tf_op jit(solution)/shard_map/ppermute | solution.py:47
  63.6 43.8 %collective-permute-start.14 = (bf16[2,1024,512]{2,1,0:T(8,128)(2,1)}, bf16[2,1024,512]{2,1,0:T(8,128)(2,1)}, u32[]{:S(2)}, u32[]{:S(2)}) collective-permute-start(bf16[2,1024,512]{2,1,0:T(8,128)(2,1)} %get-tuple-element.47), channel_id=1, source_target_pairs={{0,8},{8,0},{16,24},{24,16},{32,40},{40,32},{48,56},{56,48},{64,72... | collective-permute-start | bytes 6291464 | tf_op jit(solution)/shard_map/ppermute | solution.py:47
  64.8 20.9 %collective-permute-start.16 = (bf16[1,1024,512]{2,1,0:T(8,128)(2,1)S(1)}, bf16[1,1024,512]{2,1,0:T(8,128)(2,1)S(1)}, u32[]{:S(2)}, u32[]{:S(2)}) collective-permute-start(bf16[1,1024,512]{2,1,0:T(8,128)(2,1)S(1)} %get-tuple-element.60), channel_id=1, source_target_pairs={{0,8},{8,0},{16,24},{24,16},{32,40},{40,32},{48,56},{56,48},{64,72... | collective-permute-start | bytes 3145736 | tf_op jit(solution)/shard_map/ppermute | solution.py:47
  65.3 6.4 %collective-permute-start.10 = (bf16[2,256,128]{2,1,0:T(8,128)(2,1)S(1)}, bf16[2,256,128]{2,1,0:T(8,128)(2,1)S(1)}, u32[]{:S(2)}, u32[]{:S(2)}) collective-permute-start(bf16[2,256,128]{2,1,0:T(8,128)(2,1)S(1)} %slice.16), channel_id=1, source_target_pairs={{0,32},{8,40},{16,48},{24,56},{32,64},{40,72},{48,80},{56,88},{64,... | collective-permute-start | bytes 393224 | tf_op jit(solution)/shard_map/ppermute | solution.py:47
  65.7 6.8 %collective-permute-start.11 = (bf16[2,256,128]{2,1,0:T(8,128)(2,1)S(1)}, bf16[2,256,128]{2,1,0:T(8,128)(2,1)S(1)}, u32[]{:S(2)}, u32[]{:S(2)}) collective-permute-start(bf16[2,256,128]{2,1,0:T(8,128)(2,1)S(1)} %slice.17), channel_id=1, source_target_pairs={{0,224},{8,232},{16,240},{24,248},{32,0},{40,8},{48,16},{56,24},{6... | collective-permute-start | bytes 393224 | tf_op jit(solution)/shard_map/ppermute | solution.py:47
  71.7 55.0 %collective-permute-start.13 = (bf16[2,1024,512]{2,1,0:T(8,128)(2,1)}, bf16[2,1024,512]{2,1,0:T(8,128)(2,1)}, u32[]{:S(2)}, u32[]{:S(2)}) collective-permute-start(bf16[2,1024,512]{2,1,0:T(8,128)(2,1)} %get-tuple-element.46), channel_id=1, source_target_pairs={{0,8},{8,0},{16,24},{24,16},{32,40},{40,32},{48,56},{56,48},{64,72... | collective-permute-start | bytes 6291464 | tf_op jit(solution)/shard_map/ppermute | solution.py:47
  73.9 9.9 %collective-permute-start.17 = (bf16[128,128]{1,0:T(8,128)(2,1)S(1)}, bf16[128,128]{1,0:T(8,128)(2,1)S(1)}, u32[]{:S(2)}, u32[]{:S(2)}) collective-permute-start(bf16[128,128]{1,0:T(8,128)(2,1)S(1)} %shard_map.131.refs_6_), channel_id=1, source_target_pairs={{0,16},{8,24},{16,0},{24,8},{32,48},{40,56},{48,32},{56,40},{64,80... | collective-permute-start | bytes 98312 | tf_op jit(solution)/shard_map/ppermute | solution.py:47
  85.4 5.1 %collective-permute-start.18 = (bf16[128,256]{1,0:T(8,128)(2,1)S(1)}, bf16[128,256]{1,0:T(8,128)(2,1)S(1)}, u32[]{:S(2)}, u32[]{:S(2)}) collective-permute-start(bf16[128,256]{1,0:T(8,128)(2,1)S(1)} %pad_maximum_fusion.1.refs_0_), channel_id=1, source_target_pairs={{0,32},{8,40},{16,48},{24,56},{32,64},{40,72},{48,80},{56,88},{64,... | collective-permute-start | bytes 196616 | tf_op jit(solution)/shard_map/ppermute | solution.py:47
  85.7 4.9 %collective-permute-start.19 = (bf16[128,256]{1,0:T(8,128)(2,1)S(1)}, bf16[128,256]{1,0:T(8,128)(2,1)S(1)}, u32[]{:S(2)}, u32[]{:S(2)}) collective-permute-start(bf16[128,256]{1,0:T(8,128)(2,1)S(1)} %pad_maximum_fusion.1.refs_0_), channel_id=1, source_target_pairs={{0,224},{8,232},{16,240},{24,248},{32,0},{40,8},{48,16},{56,24},{6... | collective-permute-start | bytes 196616 | tf_op jit(solution)/shard_map/ppermute | solution.py:47
  91.5 13.0 %collective-permute-start.20 = (bf16[640,256]{1,0:T(8,128)(2,1)}, bf16[640,256]{1,0:T(8,128)(2,1)S(1)}, u32[]{:S(2)}, u32[]{:S(2)}) collective-permute-start(bf16[640,256]{1,0:T(8,128)(2,1)} %get-tuple-element.49.refs_5_.refs_1_), channel_id=1, source_target_pairs={{0,32},{8,40},{16,48},{24,56},{32,64},{40,72},{48,80},{56,88},{64,... | collective-permute-start | bytes 983048 | tf_op jit(solution)/shard_map/ppermute | solution.py:47
  93.9 10.6 %collective-permute-start.21 = (bf16[640,256]{1,0:T(8,128)(2,1)}, bf16[640,256]{1,0:T(8,128)(2,1)S(1)}, u32[]{:S(2)}, u32[]{:S(2)}) collective-permute-start(bf16[640,256]{1,0:T(8,128)(2,1)} %get-tuple-element.50), channel_id=1, source_target_pairs={{0,224},{8,232},{16,240},{24,248},{32,0},{40,8},{48,16},{56,24},{6... | collective-permute-start | bytes 983048 | tf_op jit(solution)/shard_map/ppermute | solution.py:47
  95.8 48.4 %all-to-all-start.1 = ((bf16[8,32,16,256]{3,2,1,0:T(8,128)(2,1)}), bf16[8,32,16,256]{3,2,1,0:T(8,128)(2,1)S(1)}, u32[]{:S(2)}, u32[]{:S(2)}) async-start(bf16[8,32,16,256]{3,2,1,0:T(8,128)(2,1)} %copy-done.3), calls=%async_computation.1 | async-start | bytes 4194304 | tf_op jit(solution)/shard_map/all_to_all | solution.py:520
  104.7 14.0 %collective-permute-start.22 = (bf16[1152,256]{1,0:T(8,128)(2,1)S(1)}, bf16[1152,256]{1,0:T(8,128)(2,1)S(1)}, u32[]{:S(2)}, u32[]{:S(2)}) collective-permute-start(bf16[1152,256]{1,0:T(8,128)(2,1)S(1)} %get-tuple-element.51.refs_5_), channel_id=1, source_target_pairs={{0,32},{8,40},{16,48},{24,56},{32,64},{40,72},{48,80},{56,88},{64,... | collective-permute-start | bytes 1769480 | tf_op jit(solution)/shard_map/ppermute | solution.py:47
  105.9 12.8 %collective-permute-start.23 = (bf16[1152,256]{1,0:T(8,128)(2,1)S(1)}, bf16[1152,256]{1,0:T(8,128)(2,1)S(1)}, u32[]{:S(2)}, u32[]{:S(2)}) collective-permute-start(bf16[1152,256]{1,0:T(8,128)(2,1)S(1)} %get-tuple-element.52), channel_id=1, source_target_pairs={{0,224},{8,232},{16,240},{24,248},{32,0},{40,8},{48,16},{56,24},{6... | collective-permute-start | bytes 1769480 | tf_op jit(solution)/shard_map/ppermute | solution.py:47
  120.5 13.1 %collective-permute-start.24 = (bf16[1152,256]{1,0:T(8,128)(2,1)S(1)}, bf16[1152,256]{1,0:T(8,128)(2,1)S(1)}, u32[]{:S(2)}, u32[]{:S(2)}) collective-permute-start(bf16[1152,256]{1,0:T(8,128)(2,1)S(1)} %get-tuple-element.53.refs_5_), channel_id=1, source_target_pairs={{0,32},{8,40},{16,48},{24,56},{32,64},{40,72},{48,80},{56,88},{64,... | collective-permute-start | bytes 1769480 | tf_op jit(solution)/shard_map/ppermute | solution.py:47
  121.1 12.5 %collective-permute-start.25 = (bf16[1152,256]{1,0:T(8,128)(2,1)S(1)}, bf16[1152,256]{1,0:T(8,128)(2,1)S(1)}, u32[]{:S(2)}, u32[]{:S(2)}) collective-permute-start(bf16[1152,256]{1,0:T(8,128)(2,1)S(1)} %get-tuple-element.54), channel_id=1, source_target_pairs={{0,224},{8,232},{16,240},{24,248},{32,0},{40,8},{48,16},{56,24},{6... | collective-permute-start | bytes 1769480 | tf_op jit(solution)/shard_map/ppermute | solution.py:47
  123.2 24.5 %collective-permute-start.5 = (bf16[1,1024,512]{2,1,0:T(8,128)(2,1)}, bf16[1,1024,512]{2,1,0:T(8,128)(2,1)}, u32[]{:S(2)}, u32[]{:S(2)}) collective-permute-start(bf16[1,1024,512]{2,1,0:T(8,128)(2,1)} %get-tuple-element.61), channel_id=1, source_target_pairs={{0,8},{8,0},{16,24},{24,16},{32,40},{40,32},{48,56},{56,48},{64,72... | collective-permute-start | bytes 3145736 | tf_op jit(solution)/shard_map/ppermute | solution.py:47
  137.0 7.2 %collective-permute-start.26 = (bf16[8,128,256]{2,1,0:T(8,128)(2,1)}, bf16[8,128,256]{2,1,0:T(8,128)(2,1)}, u32[]{:S(2)}, u32[]{:S(2)}) collective-permute-start(bf16[8,128,256]{2,1,0:T(8,128)(2,1)} %shard_map.141.refs_2_), channel_id=1, source_target_pairs={{0,8},{8,0},{16,24},{24,16},{32,40},{40,32},{48,56},{56,48},{64,72... | collective-permute-start | bytes 1572872 | tf_op jit(solution)/shard_map/ppermute | solution.py:47
  141.2 14.9 %collective-permute-start.27 = (bf16[1024,256]{1,0:T(8,128)(2,1)S(1)}, bf16[1024,256]{1,0:T(8,128)(2,1)}, u32[]{:S(2)}, u32[]{:S(2)}) collective-permute-start(bf16[1024,256]{1,0:T(8,128)(2,1)S(1)} %get-tuple-element.55.refs_8_.refs_5_), channel_id=1, source_target_pairs={{0,32},{8,40},{16,48},{24,56},{32,64},{40,72},{48,80},{56,88},{64,... | collective-permute-start | bytes 1572872 | tf_op jit(solution)/shard_map/ppermute | solution.py:47
  144.2 13.6 %collective-permute-start.28 = (bf16[1024,256]{1,0:T(8,128)(2,1)}, bf16[1024,256]{1,0:T(8,128)(2,1)}, u32[]{:S(2)}, u32[]{:S(2)}) collective-permute-start(bf16[1024,256]{1,0:T(8,128)(2,1)} %get-tuple-element.56), channel_id=1, source_target_pairs={{0,224},{8,232},{16,240},{24,248},{32,0},{40,8},{48,16},{56,24},{6... | collective-permute-start | bytes 1572872 | tf_op jit(solution)/shard_map/ppermute | solution.py:47
  146.7 11.0 %collective-permute-start.29 = (bf16[4,128,256]{2,1,0:T(8,128)(2,1)S(1)}, bf16[4,128,256]{2,1,0:T(8,128)(2,1)S(1)}, u32[]{:S(2)}, u32[]{:S(2)}) collective-permute-start(bf16[4,128,256]{2,1,0:T(8,128)(2,1)S(1)} %convert_element_type.3), channel_id=1, source_target_pairs={{0,16},{8,24},{16,0},{24,8},{32,48},{40,56},{48,32},{56,40},{64,80... | collective-permute-start | bytes 786440 | tf_op jit(solution)/shard_map/ppermute | solution.py:47
  160.5 23.0 %all-to-all-start.2 = ((f32[256,1,128]{2,1,0:T(1,128)}), f32[256,1,128]{2,1,0:T(1,128)S(1)}, u32[]{:S(2)}, u32[]{:S(2)}) async-start(f32[256,1,128]{2,1,0:T(1,128)} %broadcast_in_dim.3), calls=%async_computation.2 | async-start | bytes 262144 | tf_op jit(solution)/shard_map/all_to_all | solution.py:473
  170.7 13.6 %collective-permute-start.30 = (bf16[512,256]{1,0:T(8,128)(2,1)S(1)}, bf16[512,256]{1,0:T(8,128)(2,1)S(1)}, u32[]{:S(2)}, u32[]{:S(2)}) collective-permute-start(bf16[512,256]{1,0:T(8,128)(2,1)S(1)} %get-tuple-element.58), channel_id=1, source_target_pairs={{0,16},{8,24},{16,0},{24,8},{32,48},{40,56},{48,32},{56,40},{64,80... | collective-permute-start | bytes 786440 | tf_op jit(solution)/shard_map/ppermute | solution.py:47
  (22 other events, 97.8 us)

commit v2 on v1

--- a/solution.py
+++ b/solution.py
@@ -85,7 +85,7 @@
 
 
 def cost(flops, moved, exps=0):
-    return pl.CostEstimate(flops=flops // 64, bytes_accessed=moved // 64, transcendentals=exps // 64)
+    return pl.CostEstimate(flops=flops // 4096, bytes_accessed=moved // 4096, transcendentals=exps // 4096)
 
 
 def dot(a, b, dims=((1,), (0,))):
@@ -468,9 +468,22 @@
     )
 
 
-def sum_all(row):
-    copies = jnp.broadcast_to(row, (NZ * NY * NC * NX * NL,) + row.shape)
-    return jnp.sum(lax.all_to_all(copies, ("fsdp", "tp"), 0, 0), axis=0)
+def rows_kernel(rows_ref, out_ref):
+    out_ref[...] = jnp.sum(rows_ref[...], axis=0)
+
+
+def sum_rows(rows, waits):
+    return call(
+        rows_kernel,
+        (),
+        (rows,),
+        waits,
+        (1,),
+        [vmem(rows.shape)],
+        vmem(rows.shape[1:]),
+        jax.ShapeDtypeStruct(rows.shape[1:], f32),
+        cost(2**20, 2**20),
+    )
 
 
 def on_device(
@@ -493,13 +506,13 @@
     up1, down1 = send(quad, UP), send(quad, DOWN)
     up1, down1 = joined((up1, down1), (attention,))
     up2, down2 = send(up1, UP), send(down1, DOWN)
-    *sums, picked = project(where, train_x, val_x, (0,), [quad], None, (attention, up1), (4, 0))
+    *sums, picked = project(where, train_x, val_x, (0,), [quad], None, (attention, up1, crossed), (4, 0))
     other_x = {(4,): send(picked[:1], CORE), (0,): send(picked[1:], CORE)}
     up2, down2 = joined((up2, down2), (sums[1],))
     up3, down3 = send(up2, UP), send(down2, DOWN)
     *sums, picked = project(where, train_x, val_x, (1, 7), [down1, up1], sums)
     other_x[1, 7] = send(picked, CORE)
-    up3, down3 = joined((up3, down3), (sums[1], crossed))
+    up3, down3 = joined((up3, down3), (sums[1],))
     last = jnp.concatenate([send(up3[:2], UP), send(down3[2:], DOWN)])
     *sums, picked = project(where, train_x, val_x, (2, 6), [down2, up2], sums)
     other_x[2, 6] = send(picked, CORE)
@@ -530,8 +543,10 @@
     here = directions_of(where, val_skill, near_pulls, send(near_pulls, CORE), columns)
     there = send(here.astype(bf16), YHI)
     keep, give, local = local_transfer(terms((0,), sent, here), up, down, here, there)
-    row = sum_all(local)
+    rows = jnp.broadcast_to(local, (NZ * NY * NC * NX * NL,) + local.shape)
+    rows = lax.all_to_all(rows, ("fsdp", "tp"), 0, 0)
     skill_grads = finish(keep, send(give, YHI))
+    row = sum_rows(rows, (skill_grads,))
     return (skill_grads, row[0, : SKILLS * SKILLS].reshape(SKILLS, SKILLS))
 
 

time: 186 us -> 187 us (level)
  waiting for transfers between devices: 32.9 us -> 37.5 us
  local copies, waits for them, and re-layouts: 14.1 us -> 11 us
    all_to_all x1, waiting for transfers between devices: 0.01 us -> 3.11 us  [on_device(): crossed = lax.all_to_all(own_tokens.transpose(1, 0, 2), 'fsdp', 0, 0)]
    unnamed x41 -> x39, local copies, waits for them, and re-layouts: 9.66 us -> 6.62 us
    all_to_all x1, waiting for transfers between devices: 9.85 us -> 12 us  [on_device(): rows = lax.all_to_all(rows, ('fsdp', 'tp'), 0, 0)]
    ppermute x31, starting transfers between devices: 51.6 us -> 49.5 us  [send(): return lax.ppermute(value, 'fsdp', way)]
    pallas_call x22 -> x23, Pallas kernels: 62.6 us -> 62.8 us  [call(): pl.pallas_call(body, grid_spec=pltpu.PrefetchScalarGridSpec(num_scalar_pr...]
  transfers between devices with their start and end apart: 34 -> 34, of which waited for: 9 -> 11; matrix products, arithmetic and copies ran while one was open for 2% -> 2% of each run, Pallas kernels for 29% -> 30%
where the time goes in v2:
time: 187 us; the launch traced here: 186 us
  starting transfers between devices  72.6 us (39%)
  Pallas kernels  62.8 us (34%)
  waiting for transfers between devices  37.5 us (20%)
  local copies, waits for them, and re-layouts  11 us (6%)
    pallas_call x23, Pallas kernels, call(): pl.pallas_call(body, grid_spec=pltpu.PrefetchScalarGridSpec(num_scalar_pr...  62.8 us
    ppermute x31, starting transfers between devices, send(): return lax.ppermute(value, 'fsdp', way)  49.5 us
    ppermute x31, waiting for transfers between devices, send(): return lax.ppermute(value, 'fsdp', way)  22.4 us
    all_to_all x1, waiting for transfers between devices, on_device(): rows = lax.all_to_all(rows, ('fsdp', 'tp'), 0, 0)  12 us
    all_to_all x1, starting transfers between devices, on_device(): rows = lax.all_to_all(rows, ('fsdp', 'tp'), 0, 0)  12 us
    all_to_all x1, starting transfers between devices, on_device(): crossed = lax.all_to_all(own_tokens.transpose(1, 0, 2), 'fsdp', 0, 0)  6.72 us
    unnamed x39, local copies, waits for them, and re-layouts  6.62 us
    all_to_all x1, starting transfers between devices, on_device(): columns = lax.all_to_all(copies(crossed, NX * NL, (sent,)), 'tp', 0, 0)  4.4 us
  transfers between devices with their start and end apart: 34, of which 11 were waited for; matrix products, arithmetic and copies ran while one was open for 2% of the time, Pallas kernels for 30%

profile of v2, /device:TPU:1, one launch (start us, length us, event | category | flops | bytes accessed | tf_op | source)
XLA Modules:
  0.0 186.0 jit_solution(12699449200188178305)
XLA Ops:
  0.7 3.8 %collective-permute-start = (bf16[256,128]{1,0:T(8,128)(2,1)}, bf16[256,128]{1,0:T(8,128)(2,1)S(1)}, u32[]{:S(2)}, u32[]{:S(2)}) collective-permute-start(bf16[256,128]{1,0:T(8,128)(2,1)} %param.16), channel_id=1, source_target_pairs={{0,16},{8,24},{16,0},{24,8},{32,48},{40,56},{48,32},{56,40},{64,80... | collective-permute-start | bytes 196616 | tf_op jit(solution)/shard_map/ppermute | solution.py:47
  7.1 3.7 %collective-permute-done.2 = bf16[256,128]{1,0:T(8,128)(2,1)S(1)} collective-permute-done((bf16[256,128]{1,0:T(8,128)(2,1)}, bf16[256,128]{1,0:T(8,128)(2,1)S(1)}, u32[]{:S(2)}, u32[]{:S(2)}) %collective-permute-start.2) | collective-permute-done | bytes 65568 | tf_op jit(solution)/shard_map/ppermute | solution.py:47
  13.5 4.0 %collective-permute-start.4 = (bf16[4,256,128]{2,1,0:T(8,128)(2,1)S(1)}, bf16[4,256,128]{2,1,0:T(8,128)(2,1)S(1)}, u32[]{:S(2)}, u32[]{:S(2)}) collective-permute-start(bf16[4,256,128]{2,1,0:T(8,128)(2,1)S(1)} %pad_maximum_fusion.refs_3_.refs_5_), channel_id=1, source_target_pairs={{0,224},{8,232},{16,240},{24,248},{32,0},{40,8},{48,16},{56,24},{6... | collective-permute-start | bytes 786440 | tf_op jit(solution)/shard_map/ppermute | solution.py:47
  19.2 6.7 %all-to-all-start = ((bf16[32,16,256]{2,1,0:T(8,128)(2,1)}), bf16[32,16,256]{2,1,0:T(8,128)(2,1)S(1)}, u32[]{:S(2)}, u32[]{:S(2)}) async-start(bf16[32,16,256]{2,1,0:T(8,128)(2,1)} %bitcast.14), calls=%async_computation | async-start | bytes 524288 | tf_op jit(solution)/shard_map/all_to_all | solution.py:500
  28.1 4.6 %shard_map.123.refs_2_.refs_6_.refs_4_ = bf16[4,8,256,256]{3,2,1,0:T(8,128)(2,1)} custom-call(bf16[1024,1024]{1,0:T(8,128)(2,1)S(1)} %copy-done.4, bf16[1024,128]{1,0:T(8,128)(2,1)S(1)} %copy-done.9, bf16[1,8,128,128]{3,2,1,0:T(8,128)(2,1)S(1)} %shard_map.122.refs_2_.refs_4_, bf16[4,256,128]{2,1,0:T(8,128)(2,1)S(1)} %pad_maximum_fusion.refs_3_.refs_5_), custom_call_target="tpu_custom_call" | custom-call | flops 131072 | bytes 2048 | tf_op jit(solution)/shard_map/pallas_call | solution.py:56
  35.7 3.1 %all-to-all-done.refs_8_.refs_0_ = bf16[32,16,256]{2,1,0:T(8,128)(2,1)S(1)} async-done(((bf16[32,16,256]{2,1,0:T(8,128)(2,1)}), bf16[32,16,256]{2,1,0:T(8,128)(2,1)S(1)}, u32[]{:S(2)}, u32[]{:S(2)}) %all-to-all-start) | async-done | bytes 262176 | tf_op jit(solution)/shard_map/all_to_all | solution.py:500
  38.8 4.2 %shard_map.125 = (f32[1024,128]{1,0:T(8,128)S(1)}, f32[128,128]{1,0:T(8,128)S(1)}, bf16[2,1024,512]{2,1,0:T(8,128)(2,1)S(1)}) custom-call(s32[11]{0:T(128)S(1)} %concatenate.9.refs_0_, bf16[1024,8192]{1,0:T(8,128)(2,1)} %refs_1_.27, bf16[1024,8192]{1,0:T(8,128)(2,1)} %refs_1_.27, bf16[1024,8192]{1,0:T(8,128)(2,1)} %refs_1_.27, bf16[128,8192]{1,0:T(8,128)(2,1)} %refs_1_.20, ...), custom_call_target="tpu_custom_call" | custom-call | flops 65536 | bytes 512 | tf_op jit(solution)/shard_map/pallas_call | solution.py:56
  43.3 2.6 %collective-permute-start.9 = (bf16[4,256,128]{2,1,0:T(8,128)(2,1)S(1)}, bf16[4,256,128]{2,1,0:T(8,128)(2,1)S(1)}, u32[]{:S(2)}, u32[]{:S(2)}) collective-permute-start(bf16[4,256,128]{2,1,0:T(8,128)(2,1)S(1)} %get-tuple-element.36.refs_5_), channel_id=1, source_target_pairs={{0,224},{8,232},{16,240},{24,248},{32,0},{40,8},{48,16},{56,24},{6... | collective-permute-start | bytes 786440 | tf_op jit(solution)/shard_map/ppermute | solution.py:47
  45.9 5.2 %shard_map.127 = (f32[1024,128]{1,0:T(8,128)S(1)}, f32[128,128]{1,0:T(8,128)S(1)}, bf16[2,1024,512]{2,1,0:T(8,128)(2,1)}) custom-call(s32[11]{0:T(128)S(1)} %concatenate.9.refs_0_, bf16[1024,8192]{1,0:T(8,128)(2,1)} %refs_1_.27, bf16[1024,8192]{1,0:T(8,128)(2,1)} %refs_1_.27, bf16[128,8192]{1,0:T(8,128)(2,1)} %refs_1_.20, bf16[128,8192]{1,0:T(8,128)(2,1)} %refs_1_.20, ...), custom_call_target="tpu_custom_call" | custom-call | flops 131072 | bytes 1024 | tf_op jit(solution)/shard_map/pallas_call | solution.py:56
  51.1 5.2 %shard_map.129 = (f32[1024,128]{1,0:T(8,128)S(1)}, f32[128,128]{1,0:T(8,128)S(1)}, bf16[2,1024,512]{2,1,0:T(8,128)(2,1)}) custom-call(s32[11]{0:T(128)S(1)} %concatenate.9.refs_0_, bf16[1024,8192]{1,0:T(8,128)(2,1)} %refs_1_.27, bf16[1024,8192]{1,0:T(8,128)(2,1)} %refs_1_.27, bf16[128,8192]{1,0:T(8,128)(2,1)} %refs_1_.20, bf16[128,8192]{1,0:T(8,128)(2,1)} %refs_1_.20, ...), custom_call_target="tpu_custom_call" | custom-call | flops 131072 | bytes 1024 | tf_op jit(solution)/shard_map/pallas_call | solution.py:56
  56.3 5.2 %shard_map.130 = (f32[1024,128]{1,0:T(8,128)S(1)}, f32[128,128]{1,0:T(8,128)S(1)}, bf16[2,1024,512]{2,1,0:T(8,128)(2,1)}) custom-call(s32[11]{0:T(128)S(1)} %concatenate.9.refs_0_, bf16[1024,8192]{1,0:T(8,128)(2,1)} %refs_1_.27, bf16[1024,8192]{1,0:T(8,128)(2,1)} %refs_1_.27, bf16[128,8192]{1,0:T(8,128)(2,1)} %refs_1_.20, bf16[128,8192]{1,0:T(8,128)(2,1)} %refs_1_.20, ...), custom_call_target="tpu_custom_call" | custom-call | flops 131072 | bytes 1024 | tf_op jit(solution)/shard_map/pallas_call | solution.py:56
  64.4 2.6 %collective-permute-start.11 = (bf16[2,256,128]{2,1,0:T(8,128)(2,1)S(1)}, bf16[2,256,128]{2,1,0:T(8,128)(2,1)S(1)}, u32[]{:S(2)}, u32[]{:S(2)}) collective-permute-start(bf16[2,256,128]{2,1,0:T(8,128)(2,1)S(1)} %slice.17), channel_id=1, source_target_pairs={{0,224},{8,232},{16,240},{24,248},{32,0},{40,8},{48,16},{56,24},{6... | collective-permute-start | bytes 393224 | tf_op jit(solution)/shard_map/ppermute | solution.py:47
  67.0 3.6 %collective-permute-done.10 = bf16[2,256,128]{2,1,0:T(8,128)(2,1)S(1)} collective-permute-done((bf16[2,256,128]{2,1,0:T(8,128)(2,1)S(1)}, bf16[2,256,128]{2,1,0:T(8,128)(2,1)S(1)}, u32[]{:S(2)}, u32[]{:S(2)}) %collective-permute-start.10) | collective-permute-done | bytes 131104 | tf_op jit(solution)/shard_map/ppermute | solution.py:47
  72.7 2.3 %collective-permute-start.17 = (bf16[128,128]{1,0:T(8,128)(2,1)S(1)}, bf16[128,128]{1,0:T(8,128)(2,1)S(1)}, u32[]{:S(2)}, u32[]{:S(2)}) collective-permute-start(bf16[128,128]{1,0:T(8,128)(2,1)S(1)} %shard_map.131.refs_6_), channel_id=1, source_target_pairs={{0,16},{8,24},{16,0},{24,8},{32,48},{40,56},{48,32},{56,40},{64,80... | collective-permute-start | bytes 98312 | tf_op jit(solution)/shard_map/ppermute | solution.py:47
  75.1 6.8 %shard_map.132.refs_3_ = bf16[128,1024]{1,0:T(8,128)(2,1)S(1)} custom-call(s32[11]{0:T(128)S(1)} %concatenate.9.refs_0_, bf16[1024,8192]{1,0:T(8,128)(2,1)} %refs_1_.27, bf16[4,256,128]{2,1,0:T(8,128)(2,1)S(1)} %constant_dynamic-update-slice_fusion.refs_2_, f32[1024,128]{1,0:T(8,128)S(1)} %get-tuple-element.44.refs_3_, ...), custom_call_target="tpu_custom_call" | custom-call | flops 262144 | bytes 2048 | tf_op jit(solution)/shard_map/pallas_call | solution.py:56
  86.3 2.4 %shard_map.133.refs_0_ = f32[1,2,512,256]{3,2,1,0:T(8,128)S(1)} custom-call(s32[11]{0:T(128)S(1)} %concatenate.9.refs_0_, bf16[1024,8192]{1,0:T(8,128)(2,1)} %refs_1_.27, bf16[1,1024,512]{2,1,0:T(8,128)(2,1)S(1)} %collective-permute-done.16.refs_2_, bf16[128,1024]{1,0:T(8,128)(2,1)S(1)} %shard_map.132.refs_3_, ...), custom_call_target="tpu_custom_call" | custom-call | flops 65536 | bytes 1280 | tf_op jit(solution)/shard_map/pallas_call | solution.py:56
  89.6 2.1 %collective-permute-start.20 = (bf16[640,256]{1,0:T(8,128)(2,1)}, bf16[640,256]{1,0:T(8,128)(2,1)S(1)}, u32[]{:S(2)}, u32[]{:S(2)}) collective-permute-start(bf16[640,256]{1,0:T(8,128)(2,1)} %get-tuple-element.49.refs_5_.refs_1_), channel_id=1, source_target_pairs={{0,32},{8,40},{16,48},{24,56},{32,64},{40,72},{48,80},{56,88},{64,... | collective-permute-start | bytes 983048 | tf_op jit(solution)/shard_map/ppermute | solution.py:47
  93.9 4.4 %all-to-all-start.1 = ((bf16[8,32,16,256]{3,2,1,0:T(8,128)(2,1)}), bf16[8,32,16,256]{3,2,1,0:T(8,128)(2,1)S(1)}, u32[]{:S(2)}, u32[]{:S(2)}) async-start(bf16[8,32,16,256]{3,2,1,0:T(8,128)(2,1)} %copy-done.3), calls=%async_computation.1 | async-start | bytes 4194304 | tf_op jit(solution)/shard_map/all_to_all | solution.py:533
  98.3 4.2 %shard_map.135.refs_0_ = f32[2,2,512,256]{3,2,1,0:T(8,128)S(1)} custom-call(s32[11]{0:T(128)S(1)} %concatenate.9.refs_0_, bf16[1024,8192]{1,0:T(8,128)(2,1)} %refs_1_.27, bf16[2,1024,512]{2,1,0:T(8,128)(2,1)} %collective-permute-done.15.refs_2_, bf16[128,1024]{1,0:T(8,128)(2,1)S(1)} %shard_map.132.refs_3_, ...), custom_call_target="tpu_custom_call" | custom-call | flops 131072 | bytes 2560 | tf_op jit(solution)/shard_map/pallas_call | solution.py:56
  105.5 4.2 %shard_map.137.refs_0_ = f32[2,2,512,256]{3,2,1,0:T(8,128)S(1)} custom-call(s32[11]{0:T(128)S(1)} %concatenate.9.refs_0_, bf16[1024,8192]{1,0:T(8,128)(2,1)} %refs_1_.27, bf16[2,1024,512]{2,1,0:T(8,128)(2,1)} %collective-permute-done.14.refs_2_, bf16[128,1024]{1,0:T(8,128)(2,1)S(1)} %shard_map.132.refs_3_, ...), custom_call_target="tpu_custom_call" | custom-call | flops 131072 | bytes 2560 | tf_op jit(solution)/shard_map/pallas_call | solution.py:56
  111.1 5.4 %collective-permute-done.22.refs_1_.refs_5_ = bf16[1152,256]{1,0:T(8,128)(2,1)S(1)} collective-permute-done((bf16[1152,256]{1,0:T(8,128)(2,1)S(1)}, bf16[1152,256]{1,0:T(8,128)(2,1)S(1)}, u32[]{:S(2)}, u32[]{:S(2)}) %collective-permute-start.22) | collective-permute-done | bytes 589856 | tf_op jit(solution)/shard_map/ppermute | solution.py:47
  119.0 2.1 %collective-permute-start.25 = (bf16[1152,256]{1,0:T(8,128)(2,1)S(1)}, bf16[1152,256]{1,0:T(8,128)(2,1)S(1)}, u32[]{:S(2)}, u32[]{:S(2)}) collective-permute-start(bf16[1152,256]{1,0:T(8,128)(2,1)S(1)} %get-tuple-element.54), channel_id=1, source_target_pairs={{0,224},{8,232},{16,240},{24,248},{32,0},{40,8},{48,16},{56,24},{6... | collective-permute-start | bytes 1769480 | tf_op jit(solution)/shard_map/ppermute | solution.py:47
  121.0 3.8 %collective-permute-start.5 = (bf16[1,1024,512]{2,1,0:T(8,128)(2,1)}, bf16[1,1024,512]{2,1,0:T(8,128)(2,1)}, u32[]{:S(2)}, u32[]{:S(2)}) collective-permute-start(bf16[1,1024,512]{2,1,0:T(8,128)(2,1)} %get-tuple-element.61), channel_id=1, source_target_pairs={{0,8},{8,0},{16,24},{24,16},{32,40},{40,32},{48,56},{56,48},{64,72... | collective-permute-start | bytes 3145736 | tf_op jit(solution)/shard_map/ppermute | solution.py:47
  124.9 4.2 %shard_map.139.refs_0_ = f32[2,2,512,256]{3,2,1,0:T(8,128)S(1)} custom-call(s32[11]{0:T(128)S(1)} %concatenate.9.refs_0_, bf16[1024,8192]{1,0:T(8,128)(2,1)} %refs_1_.27, bf16[2,1024,512]{2,1,0:T(8,128)(2,1)} %collective-permute-done.13.refs_2_, bf16[128,1024]{1,0:T(8,128)(2,1)S(1)} %shard_map.132.refs_3_, ...), custom_call_target="tpu_custom_call" | custom-call | flops 131072 | bytes 2560 | tf_op jit(solution)/shard_map/pallas_call | solution.py:56
  131.4 2.5 %shard_map.140 = (bf16[1024,256]{1,0:T(8,128)(2,1)S(1)}, bf16[1024,256]{1,0:T(8,128)(2,1)}) custom-call(f32[2,2,512,256]{3,2,1,0:T(8,128)} %copy-done.1, bf16[1152,256]{1,0:T(8,128)(2,1)S(1)} %collective-permute-done.24.refs_1_.refs_4_, bf16[1152,256]{1,0:T(8,128)(2,1)S(1)} %collective-permute-done.25.refs_2_), custom_call_target="tpu_custom_call" | custom-call | flops 256 | bytes 1024 | tf_op jit(solution)/shard_map/pallas_call | solution.py:56
  134.8 4.2 %collective-permute-start.26 = (bf16[8,128,256]{2,1,0:T(8,128)(2,1)}, bf16[8,128,256]{2,1,0:T(8,128)(2,1)}, u32[]{:S(2)}, u32[]{:S(2)}) collective-permute-start(bf16[8,128,256]{2,1,0:T(8,128)(2,1)} %shard_map.141.refs_2_), channel_id=1, source_target_pairs={{0,8},{8,0},{16,24},{24,16},{32,40},{40,32},{48,56},{56,48},{64,72... | collective-permute-start | bytes 1572872 | tf_op jit(solution)/shard_map/ppermute | solution.py:47
  139.0 3.0 %collective-permute-start.27 = (bf16[1024,256]{1,0:T(8,128)(2,1)S(1)}, bf16[1024,256]{1,0:T(8,128)(2,1)}, u32[]{:S(2)}, u32[]{:S(2)}) collective-permute-start(bf16[1024,256]{1,0:T(8,128)(2,1)S(1)} %get-tuple-element.55.refs_8_.refs_5_), channel_id=1, source_target_pairs={{0,32},{8,40},{16,48},{24,56},{32,64},{40,72},{48,80},{56,88},{64,... | collective-permute-start | bytes 1572872 | tf_op jit(solution)/shard_map/ppermute | solution.py:47
  142.0 2.5 %shard_map.143.refs_6_.refs_3_ = f32[4,128,256]{2,1,0:T(8,128)S(1)} custom-call(s32[11]{0:T(128)S(1)} %concatenate.9.refs_0_, s32[32]{0:T(128)S(1)} %copy-done.17, bf16[8,128,256]{2,1,0:T(8,128)(2,1)} %shard_map.141.refs_2_, bf16[8,128,256]{2,1,0:T(8,128)(2,1)} %collective-permute-done.26.refs_3_, bf16[8,32,16,256]{3,2,1,0:T(8,128)(2,1)S(1)} %all-to-all-done.1.refs_4_), custom_call_target="tpu_custom_call" | custom-call | flops 65536 | bytes 1024 | tf_op jit(solution)/shard_map/pallas_call | solution.py:56
  145.5 2.5 %shard_map.144.refs_0_ = f32[1,2,512,256]{3,2,1,0:T(8,128)S(1)} custom-call(s32[11]{0:T(128)S(1)} %concatenate.9.refs_0_, bf16[1024,8192]{1,0:T(8,128)(2,1)} %refs_1_.27, bf16[1,1024,512]{2,1,0:T(8,128)(2,1)} %collective-permute-done.5.refs_2_, bf16[128,1024]{1,0:T(8,128)(2,1)S(1)} %shard_map.132.refs_3_, ...), custom_call_target="tpu_custom_call" | custom-call | flops 65536 | bytes 1280 | tf_op jit(solution)/shard_map/pallas_call | solution.py:56
  148.1 5.8 %collective-permute-done.27.refs_1_ = bf16[1024,256]{1,0:T(8,128)(2,1)} collective-permute-done((bf16[1024,256]{1,0:T(8,128)(2,1)S(1)}, bf16[1024,256]{1,0:T(8,128)(2,1)}, u32[]{:S(2)}, u32[]{:S(2)}) %collective-permute-start.27) | collective-permute-done | bytes 524320 | tf_op jit(solution)/shard_map/ppermute | solution.py:47
  159.3 12.0 %all-to-all-start.2 = ((f32[256,1,128]{2,1,0:T(1,128)}), f32[256,1,128]{2,1,0:T(1,128)S(1)}, u32[]{:S(2)}, u32[]{:S(2)}) async-start(f32[256,1,128]{2,1,0:T(1,128)} %broadcast_in_dim.3), calls=%async_computation.2 | async-start | bytes 262144 | tf_op jit(solution)/shard_map/all_to_all | solution.py:547
  172.1 12.0 %all-to-all-done.2.refs_0_ = f32[256,1,128]{2,1,0:T(1,128)S(1)} async-done(((f32[256,1,128]{2,1,0:T(1,128)}), f32[256,1,128]{2,1,0:T(1,128)S(1)}, u32[]{:S(2)}, u32[]{:S(2)}) %all-to-all-start.2) | async-done | bytes 131104 | tf_op jit(solution)/shard_map/all_to_all | solution.py:547
  (115 shorter events, 43.8 us)
Async XLA Ops:
  0.7 6.5 %collective-permute-start = (bf16[256,128]{1,0:T(8,128)(2,1)}, bf16[256,128]{1,0:T(8,128)(2,1)S(1)}, u32[]{:S(2)}, u32[]{:S(2)}) collective-permute-start(bf16[256,128]{1,0:T(8,128)(2,1)} %param.16), channel_id=1, source_target_pairs={{0,16},{8,24},{16,0},{24,8},{32,48},{40,56},{48,32},{56,40},{64,80... | collective-permute-start | bytes 196616 | tf_op jit(solution)/shard_map/ppermute | solution.py:47
  5.4 5.4 %collective-permute-start.2 = (bf16[256,128]{1,0:T(8,128)(2,1)}, bf16[256,128]{1,0:T(8,128)(2,1)S(1)}, u32[]{:S(2)}, u32[]{:S(2)}) collective-permute-start(bf16[256,128]{1,0:T(8,128)(2,1)} %param.16), channel_id=1, source_target_pairs={{0,24},{8,16},{16,8},{24,0},{32,56},{40,48},{48,40},{56,32},{64,88... | collective-permute-start | bytes 196616 | tf_op jit(solution)/shard_map/ppermute | solution.py:47
  11.7 21.0 %collective-permute-start.3 = (bf16[4,256,128]{2,1,0:T(8,128)(2,1)S(1)}, bf16[4,256,128]{2,1,0:T(8,128)(2,1)S(1)}, u32[]{:S(2)}, u32[]{:S(2)}) collective-permute-start(bf16[4,256,128]{2,1,0:T(8,128)(2,1)S(1)} %pad_maximum_fusion.refs_3_.refs_5_), channel_id=1, source_target_pairs={{0,32},{8,40},{16,48},{24,56},{32,64},{40,72},{48,80},{56,88},{64,... | collective-permute-start | bytes 786440 | tf_op jit(solution)/shard_map/ppermute | solution.py:47
  13.5 19.3 %collective-permute-start.4 = (bf16[4,256,128]{2,1,0:T(8,128)(2,1)S(1)}, bf16[4,256,128]{2,1,0:T(8,128)(2,1)S(1)}, u32[]{:S(2)}, u32[]{:S(2)}) collective-permute-start(bf16[4,256,128]{2,1,0:T(8,128)(2,1)S(1)} %pad_maximum_fusion.refs_3_.refs_5_), channel_id=1, source_target_pairs={{0,224},{8,232},{16,240},{24,248},{32,0},{40,8},{48,16},{56,24},{6... | collective-permute-start | bytes 786440 | tf_op jit(solution)/shard_map/ppermute | solution.py:47
  19.2 19.7 %all-to-all-start = ((bf16[32,16,256]{2,1,0:T(8,128)(2,1)}), bf16[32,16,256]{2,1,0:T(8,128)(2,1)S(1)}, u32[]{:S(2)}, u32[]{:S(2)}) async-start(bf16[32,16,256]{2,1,0:T(8,128)(2,1)} %bitcast.14), calls=%async_computation | async-start | bytes 524288 | tf_op jit(solution)/shard_map/all_to_all | solution.py:500
  32.7 10.4 %collective-permute-start.6 = (bf16[4,256,128]{2,1,0:T(8,128)(2,1)S(1)}, bf16[4,256,128]{2,1,0:T(8,128)(2,1)S(1)}, u32[]{:S(2)}, u32[]{:S(2)}) collective-permute-start(bf16[4,256,128]{2,1,0:T(8,128)(2,1)S(1)} %get-tuple-element.31.refs_7_.refs_6_), channel_id=1, source_target_pairs={{0,32},{8,40},{16,48},{24,56},{32,64},{40,72},{48,80},{56,88},{64,... | collective-permute-start | bytes 786440 | tf_op jit(solution)/shard_map/ppermute | solution.py:47
  34.2 8.9 %collective-permute-start.7 = (bf16[4,256,128]{2,1,0:T(8,128)(2,1)S(1)}, bf16[4,256,128]{2,1,0:T(8,128)(2,1)S(1)}, u32[]{:S(2)}, u32[]{:S(2)}) collective-permute-start(bf16[4,256,128]{2,1,0:T(8,128)(2,1)S(1)} %get-tuple-element.33.refs_5_), channel_id=1, source_target_pairs={{0,224},{8,232},{16,240},{24,248},{32,0},{40,8},{48,16},{56,24},{6... | collective-permute-start | bytes 786440 | tf_op jit(solution)/shard_map/ppermute | solution.py:47
  43.1 13.1 %collective-permute-start.8 = (bf16[4,256,128]{2,1,0:T(8,128)(2,1)S(1)}, bf16[4,256,128]{2,1,0:T(8,128)(2,1)S(1)}, u32[]{:S(2)}, u32[]{:S(2)}) collective-permute-start(bf16[4,256,128]{2,1,0:T(8,128)(2,1)S(1)} %get-tuple-element.35.refs_6_), channel_id=1, source_target_pairs={{0,32},{8,40},{16,48},{24,56},{32,64},{40,72},{48,80},{56,88},{64,... | collective-permute-start | bytes 786440 | tf_op jit(solution)/shard_map/ppermute | solution.py:47
  43.3 13.0 %collective-permute-start.9 = (bf16[4,256,128]{2,1,0:T(8,128)(2,1)S(1)}, bf16[4,256,128]{2,1,0:T(8,128)(2,1)S(1)}, u32[]{:S(2)}, u32[]{:S(2)}) collective-permute-start(bf16[4,256,128]{2,1,0:T(8,128)(2,1)S(1)} %get-tuple-element.36.refs_5_), channel_id=1, source_target_pairs={{0,224},{8,232},{16,240},{24,248},{32,0},{40,8},{48,16},{56,24},{6... | collective-permute-start | bytes 786440 | tf_op jit(solution)/shard_map/ppermute | solution.py:47
  61.5 36.8 %collective-permute-start.15 = (bf16[2,1024,512]{2,1,0:T(8,128)(2,1)}, bf16[2,1024,512]{2,1,0:T(8,128)(2,1)}, u32[]{:S(2)}, u32[]{:S(2)}) collective-permute-start(bf16[2,1024,512]{2,1,0:T(8,128)(2,1)} %get-tuple-element.48), channel_id=1, source_target_pairs={{0,8},{8,0},{16,24},{24,16},{32,40},{40,32},{48,56},{56,48},{64,72... | collective-permute-start | bytes 6291464 | tf_op jit(solution)/shard_map/ppermute | solution.py:47
  62.5 43.0 %collective-permute-start.14 = (bf16[2,1024,512]{2,1,0:T(8,128)(2,1)}, bf16[2,1024,512]{2,1,0:T(8,128)(2,1)}, u32[]{:S(2)}, u32[]{:S(2)}) collective-permute-start(bf16[2,1024,512]{2,1,0:T(8,128)(2,1)} %get-tuple-element.47), channel_id=1, source_target_pairs={{0,8},{8,0},{16,24},{24,16},{32,40},{40,32},{48,56},{56,48},{64,72... | collective-permute-start | bytes 6291464 | tf_op jit(solution)/shard_map/ppermute | solution.py:47
  63.6 21.7 %collective-permute-start.16 = (bf16[1,1024,512]{2,1,0:T(8,128)(2,1)S(1)}, bf16[1,1024,512]{2,1,0:T(8,128)(2,1)S(1)}, u32[]{:S(2)}, u32[]{:S(2)}) collective-permute-start(bf16[1,1024,512]{2,1,0:T(8,128)(2,1)S(1)} %get-tuple-element.60), channel_id=1, source_target_pairs={{0,8},{8,0},{16,24},{24,16},{32,40},{40,32},{48,56},{56,48},{64,72... | collective-permute-start | bytes 3145736 | tf_op jit(solution)/shard_map/ppermute | solution.py:47
  64.1 6.4 %collective-permute-start.10 = (bf16[2,256,128]{2,1,0:T(8,128)(2,1)S(1)}, bf16[2,256,128]{2,1,0:T(8,128)(2,1)S(1)}, u32[]{:S(2)}, u32[]{:S(2)}) collective-permute-start(bf16[2,256,128]{2,1,0:T(8,128)(2,1)S(1)} %slice.16), channel_id=1, source_target_pairs={{0,32},{8,40},{16,48},{24,56},{32,64},{40,72},{48,80},{56,88},{64,... | collective-permute-start | bytes 393224 | tf_op jit(solution)/shard_map/ppermute | solution.py:47
  64.4 6.9 %collective-permute-start.11 = (bf16[2,256,128]{2,1,0:T(8,128)(2,1)S(1)}, bf16[2,256,128]{2,1,0:T(8,128)(2,1)S(1)}, u32[]{:S(2)}, u32[]{:S(2)}) collective-permute-start(bf16[2,256,128]{2,1,0:T(8,128)(2,1)S(1)} %slice.17), channel_id=1, source_target_pairs={{0,224},{8,232},{16,240},{24,248},{32,0},{40,8},{48,16},{56,24},{6... | collective-permute-start | bytes 393224 | tf_op jit(solution)/shard_map/ppermute | solution.py:47
  70.6 54.3 %collective-permute-start.13 = (bf16[2,1024,512]{2,1,0:T(8,128)(2,1)}, bf16[2,1024,512]{2,1,0:T(8,128)(2,1)}, u32[]{:S(2)}, u32[]{:S(2)}) collective-permute-start(bf16[2,1024,512]{2,1,0:T(8,128)(2,1)} %get-tuple-element.46), channel_id=1, source_target_pairs={{0,8},{8,0},{16,24},{24,16},{32,40},{40,32},{48,56},{56,48},{64,72... | collective-permute-start | bytes 6291464 | tf_op jit(solution)/shard_map/ppermute | solution.py:47
  72.7 9.1 %collective-permute-start.17 = (bf16[128,128]{1,0:T(8,128)(2,1)S(1)}, bf16[128,128]{1,0:T(8,128)(2,1)S(1)}, u32[]{:S(2)}, u32[]{:S(2)}) collective-permute-start(bf16[128,128]{1,0:T(8,128)(2,1)S(1)} %shard_map.131.refs_6_), channel_id=1, source_target_pairs={{0,16},{8,24},{16,0},{24,8},{32,48},{40,56},{48,32},{56,40},{64,80... | collective-permute-start | bytes 98312 | tf_op jit(solution)/shard_map/ppermute | solution.py:47
  83.6 5.1 %collective-permute-start.18 = (bf16[128,256]{1,0:T(8,128)(2,1)S(1)}, bf16[128,256]{1,0:T(8,128)(2,1)S(1)}, u32[]{:S(2)}, u32[]{:S(2)}) collective-permute-start(bf16[128,256]{1,0:T(8,128)(2,1)S(1)} %pad_maximum_fusion.1.refs_0_), channel_id=1, source_target_pairs={{0,32},{8,40},{16,48},{24,56},{32,64},{40,72},{48,80},{56,88},{64,... | collective-permute-start | bytes 196616 | tf_op jit(solution)/shard_map/ppermute | solution.py:47
  85.3 3.4 %collective-permute-start.19 = (bf16[128,256]{1,0:T(8,128)(2,1)S(1)}, bf16[128,256]{1,0:T(8,128)(2,1)S(1)}, u32[]{:S(2)}, u32[]{:S(2)}) collective-permute-start(bf16[128,256]{1,0:T(8,128)(2,1)S(1)} %pad_maximum_fusion.1.refs_0_), channel_id=1, source_target_pairs={{0,224},{8,232},{16,240},{24,248},{32,0},{40,8},{48,16},{56,24},{6... | collective-permute-start | bytes 196616 | tf_op jit(solution)/shard_map/ppermute | solution.py:47
  89.6 12.9 %collective-permute-start.20 = (bf16[640,256]{1,0:T(8,128)(2,1)}, bf16[640,256]{1,0:T(8,128)(2,1)S(1)}, u32[]{:S(2)}, u32[]{:S(2)}) collective-permute-start(bf16[640,256]{1,0:T(8,128)(2,1)} %get-tuple-element.49.refs_5_.refs_1_), channel_id=1, source_target_pairs={{0,32},{8,40},{16,48},{24,56},{32,64},{40,72},{48,80},{56,88},{64,... | collective-permute-start | bytes 983048 | tf_op jit(solution)/shard_map/ppermute | solution.py:47
  91.8 10.8 %collective-permute-start.21 = (bf16[640,256]{1,0:T(8,128)(2,1)}, bf16[640,256]{1,0:T(8,128)(2,1)S(1)}, u32[]{:S(2)}, u32[]{:S(2)}) collective-permute-start(bf16[640,256]{1,0:T(8,128)(2,1)} %get-tuple-element.50), channel_id=1, source_target_pairs={{0,224},{8,232},{16,240},{24,248},{32,0},{40,8},{48,16},{56,24},{6... | collective-permute-start | bytes 983048 | tf_op jit(solution)/shard_map/ppermute | solution.py:47
  93.9 48.1 %all-to-all-start.1 = ((bf16[8,32,16,256]{3,2,1,0:T(8,128)(2,1)}), bf16[8,32,16,256]{3,2,1,0:T(8,128)(2,1)S(1)}, u32[]{:S(2)}, u32[]{:S(2)}) async-start(bf16[8,32,16,256]{3,2,1,0:T(8,128)(2,1)} %copy-done.3), calls=%async_computation.1 | async-start | bytes 4194304 | tf_op jit(solution)/shard_map/all_to_all | solution.py:533
  102.7 13.8 %collective-permute-start.22 = (bf16[1152,256]{1,0:T(8,128)(2,1)S(1)}, bf16[1152,256]{1,0:T(8,128)(2,1)S(1)}, u32[]{:S(2)}, u32[]{:S(2)}) collective-permute-start(bf16[1152,256]{1,0:T(8,128)(2,1)S(1)} %get-tuple-element.51.refs_5_), channel_id=1, source_target_pairs={{0,32},{8,40},{16,48},{24,56},{32,64},{40,72},{48,80},{56,88},{64,... | collective-permute-start | bytes 1769480 | tf_op jit(solution)/shard_map/ppermute | solution.py:47
  103.7 12.8 %collective-permute-start.23 = (bf16[1152,256]{1,0:T(8,128)(2,1)S(1)}, bf16[1152,256]{1,0:T(8,128)(2,1)S(1)}, u32[]{:S(2)}, u32[]{:S(2)}) collective-permute-start(bf16[1152,256]{1,0:T(8,128)(2,1)S(1)} %get-tuple-element.52), channel_id=1, source_target_pairs={{0,224},{8,232},{16,240},{24,248},{32,0},{40,8},{48,16},{56,24},{6... | collective-permute-start | bytes 1769480 | tf_op jit(solution)/shard_map/ppermute | solution.py:47
  118.3 12.8 %collective-permute-start.24 = (bf16[1152,256]{1,0:T(8,128)(2,1)S(1)}, bf16[1152,256]{1,0:T(8,128)(2,1)S(1)}, u32[]{:S(2)}, u32[]{:S(2)}) collective-permute-start(bf16[1152,256]{1,0:T(8,128)(2,1)S(1)} %get-tuple-element.53.refs_5_), channel_id=1, source_target_pairs={{0,32},{8,40},{16,48},{24,56},{32,64},{40,72},{48,80},{56,88},{64,... | collective-permute-start | bytes 1769480 | tf_op jit(solution)/shard_map/ppermute | solution.py:47
  119.0 12.5 %collective-permute-start.25 = (bf16[1152,256]{1,0:T(8,128)(2,1)S(1)}, bf16[1152,256]{1,0:T(8,128)(2,1)S(1)}, u32[]{:S(2)}, u32[]{:S(2)}) collective-permute-start(bf16[1152,256]{1,0:T(8,128)(2,1)S(1)} %get-tuple-element.54), channel_id=1, source_target_pairs={{0,224},{8,232},{16,240},{24,248},{32,0},{40,8},{48,16},{56,24},{6... | collective-permute-start | bytes 1769480 | tf_op jit(solution)/shard_map/ppermute | solution.py:47
  121.0 24.5 %collective-permute-start.5 = (bf16[1,1024,512]{2,1,0:T(8,128)(2,1)}, bf16[1,1024,512]{2,1,0:T(8,128)(2,1)}, u32[]{:S(2)}, u32[]{:S(2)}) collective-permute-start(bf16[1,1024,512]{2,1,0:T(8,128)(2,1)} %get-tuple-element.61), channel_id=1, source_target_pairs={{0,8},{8,0},{16,24},{24,16},{32,40},{40,32},{48,56},{56,48},{64,72... | collective-permute-start | bytes 3145736 | tf_op jit(solution)/shard_map/ppermute | solution.py:47
  134.8 7.2 %collective-permute-start.26 = (bf16[8,128,256]{2,1,0:T(8,128)(2,1)}, bf16[8,128,256]{2,1,0:T(8,128)(2,1)}, u32[]{:S(2)}, u32[]{:S(2)}) collective-permute-start(bf16[8,128,256]{2,1,0:T(8,128)(2,1)} %shard_map.141.refs_2_), channel_id=1, source_target_pairs={{0,8},{8,0},{16,24},{24,16},{32,40},{40,32},{48,56},{56,48},{64,72... | collective-permute-start | bytes 1572872 | tf_op jit(solution)/shard_map/ppermute | solution.py:47
  139.0 14.9 %collective-permute-start.27 = (bf16[1024,256]{1,0:T(8,128)(2,1)S(1)}, bf16[1024,256]{1,0:T(8,128)(2,1)}, u32[]{:S(2)}, u32[]{:S(2)}) collective-permute-start(bf16[1024,256]{1,0:T(8,128)(2,1)S(1)} %get-tuple-element.55.refs_8_.refs_5_), channel_id=1, source_target_pairs={{0,32},{8,40},{16,48},{24,56},{32,64},{40,72},{48,80},{56,88},{64,... | collective-permute-start | bytes 1572872 | tf_op jit(solution)/shard_map/ppermute | solution.py:47
  142.0 13.6 %collective-permute-start.28 = (bf16[1024,256]{1,0:T(8,128)(2,1)}, bf16[1024,256]{1,0:T(8,128)(2,1)}, u32[]{:S(2)}, u32[]{:S(2)}) collective-permute-start(bf16[1024,256]{1,0:T(8,128)(2,1)} %get-tuple-element.56), channel_id=1, source_target_pairs={{0,224},{8,232},{16,240},{24,248},{32,0},{40,8},{48,16},{56,24},{6... | collective-permute-start | bytes 1572872 | tf_op jit(solution)/shard_map/ppermute | solution.py:47
  144.6 11.0 %collective-permute-start.29 = (bf16[4,128,256]{2,1,0:T(8,128)(2,1)S(1)}, bf16[4,128,256]{2,1,0:T(8,128)(2,1)S(1)}, u32[]{:S(2)}, u32[]{:S(2)}) collective-permute-start(bf16[4,128,256]{2,1,0:T(8,128)(2,1)S(1)} %convert_element_type.3), channel_id=1, source_target_pairs={{0,16},{8,24},{16,0},{24,8},{32,48},{40,56},{48,32},{56,40},{64,80... | collective-permute-start | bytes 786440 | tf_op jit(solution)/shard_map/ppermute | solution.py:47
  157.6 13.6 %collective-permute-start.30 = (bf16[512,256]{1,0:T(8,128)(2,1)S(1)}, bf16[512,256]{1,0:T(8,128)(2,1)S(1)}, u32[]{:S(2)}, u32[]{:S(2)}) collective-permute-start(bf16[512,256]{1,0:T(8,128)(2,1)S(1)} %get-tuple-element.58), channel_id=1, source_target_pairs={{0,16},{8,24},{16,0},{24,8},{32,48},{40,56},{48,32},{56,40},{64,80... | collective-permute-start | bytes 786440 | tf_op jit(solution)/shard_map/ppermute | solution.py:47
  159.3 24.8 %all-to-all-start.2 = ((f32[256,1,128]{2,1,0:T(1,128)}), f32[256,1,128]{2,1,0:T(1,128)S(1)}, u32[]{:S(2)}, u32[]{:S(2)}) async-start(f32[256,1,128]{2,1,0:T(1,128)} %broadcast_in_dim.3), calls=%async_computation.2 | async-start | bytes 262144 | tf_op jit(solution)/shard_map/all_to_all | solution.py:547
  (21 other events, 154.6 us)

commit v3 on v2

--- a/solution.py
+++ b/solution.py
@@ -342,6 +342,7 @@
         [vmem(shape), vmem(shape)],
         [jax.ShapeDtypeStruct(shape, bf16)] * 2,
         cost(2**20, 4 * 2**20),
+        mib=16,
     )
     return up, (send(up, UP), send(down, DOWN))
 
@@ -363,6 +364,7 @@
         vmem((len(arrays), HD, ROWS)),
         jax.ShapeDtypeStruct((len(arrays), HD, ROWS), bf16),
         cost(0, 2**20),
+        mib=16,
     )
 
 
@@ -381,6 +383,7 @@
         pl.BlockSpec((1,) + array.shape, lambda i: (i, 0, 0, 0)),
         jax.ShapeDtypeStruct((count,) + array.shape, array.dtype),
         cost(0, 2**20),
+        mib=16,
     )
 
 
@@ -405,7 +408,11 @@
         vmem((SKILLS, HD, ROWS)),
         jax.ShapeDtypeStruct((SKILLS, HD, ROWS), f32),
         cost(2 * 4096 * ROWS * HD, 4 * 2**20),
-    )
+        mib=16,
+    )
+
+
+EVERY = NZ * NY * NC * NX * NL
 
 
 def local_kernel(mine_ref, up_ref, down_ref, here_ref, there_ref, keep_ref, give_ref, local_ref):
@@ -426,7 +433,7 @@
             product = jnp.sum(product, axis=0, keepdims=True)
             entry = step_size * jnp.sum(product, axis=1, keepdims=True)
             local = jnp.where(lane == s * SKILLS + v, entry, local)
-    local_ref[...] = local
+    local_ref[...] = jnp.broadcast_to(local, local_ref.shape)
 
 
 def local_transfer(mine, up, down, here, there):
@@ -438,13 +445,14 @@
         (),
         (1,),
         [vmem(o.shape) for o in operands],
-        [vmem((SKILLS * HD, ROWS)), vmem((SKILLS * HD, ROWS)), vmem((1, HD))],
+        [vmem((SKILLS * HD, ROWS)), vmem((SKILLS * HD, ROWS)), vmem((EVERY, 1, HD))],
         [
             jax.ShapeDtypeStruct((SKILLS * HD, ROWS), f32),
             jax.ShapeDtypeStruct((SKILLS * HD, ROWS), bf16),
-            jax.ShapeDtypeStruct((1, HD), f32),
+            jax.ShapeDtypeStruct((EVERY, 1, HD), f32),
         ],
         cost(2**22, 4 * 2**20),
+        mib=16,
     )
 
 
@@ -465,11 +473,14 @@
         vmem((SKILLS, ROWS, HD)),
         jax.ShapeDtypeStruct((SKILLS, ROWS, HD), bf16),
         cost(2**20, 2**20),
+        mib=16,
     )
 
 
 def rows_kernel(rows_ref, out_ref):
-    out_ref[...] = jnp.sum(rows_ref[...], axis=0)
+    row = jnp.sum(rows_ref[...], axis=0)
+    for s in range(SKILLS):
+        out_ref[s : s + 1, :] = row[:, s * SKILLS : (s + 1) * SKILLS]
 
 
 def sum_rows(rows, waits):
@@ -480,9 +491,10 @@
         waits,
         (1,),
         [vmem(rows.shape)],
-        vmem(rows.shape[1:]),
-        jax.ShapeDtypeStruct(rows.shape[1:], f32),
+        vmem((SKILLS, SKILLS)),
+        jax.ShapeDtypeStruct((SKILLS, SKILLS), f32),
         cost(2**20, 2**20),
+        mib=16,
     )
 
 
@@ -515,10 +527,9 @@
     up3, down3 = joined((up3, down3), (sums[1],))
     last = jnp.concatenate([send(up3[:2], UP), send(down3[2:], DOWN)])
     *sums, picked = project(where, train_x, val_x, (2, 6), [down2, up2], sums)
-    other_x[2, 6] = send(picked, CORE)
-    *sums, picked = project(where, train_x, val_x, (3, 5), [down3, up3], sums)
-    other_x[3, 5] = send(picked, CORE)
+    *sums, later = project(where, train_x, val_x, (3, 5), [down3, up3], sums)
     own_pull = val_pulls(where, val_x, last, sums[1], val_attention, val_target)
+    other_x[3, 5] = send(joined((later,), (own_pull,))[0], CORE)
     pull = jnp.concatenate([own_pull, send(own_pull, YHI)], axis=1)
     p_up, p_down = send(pull, UP), send(pull, DOWN)
     grads = value_grads(where, train_x, last, sums[0], attention, train_target, (own_pull,))
@@ -530,6 +541,7 @@
     pulls = {0: pull, 1: p_down, 7: p_up}
     sent, (up, down) = ring_step(1, terms((4,)), p_up, p_down)
     mine = terms((3, 5), sent)
+    other_x[2, 6] = send(joined((picked,), (sent,))[0], CORE)
     columns = lax.all_to_all(copies(crossed, NX * NL, (sent,)), "tp", 0, 0)
     pulls[6], pulls[2] = up, down
     sent, (up, down) = ring_step(2, mine, up, down)
@@ -543,11 +555,9 @@
     here = directions_of(where, val_skill, near_pulls, send(near_pulls, CORE), columns)
     there = send(here.astype(bf16), YHI)
     keep, give, local = local_transfer(terms((0,), sent, here), up, down, here, there)
-    rows = jnp.broadcast_to(local, (NZ * NY * NC * NX * NL,) + local.shape)
-    rows = lax.all_to_all(rows, ("fsdp", "tp"), 0, 0)
+    rows = lax.all_to_all(local, ("fsdp", "tp"), 0, 0)
     skill_grads = finish(keep, send(give, YHI))
-    row = sum_rows(rows, (skill_grads,))
-    return (skill_grads, row[0, : SKILLS * SKILLS].reshape(SKILLS, SKILLS))
+    return (skill_grads, sum_rows(rows, (skill_grads,)))
 
 
 def solution(mesh):

time: 187 us -> 186 us (level)
  waiting for transfers between devices: 37.5 us -> 41.6 us
  starting transfers between devices: 72.6 us -> 69.8 us
  local copies, waits for them, and re-layouts: 11 us -> 8.89 us
    ppermute x31, waiting for transfers between devices: 22.4 us -> 27.5 us  [send(): return lax.ppermute(value, 'fsdp', way)]
    all_to_all x1, starting transfers between devices: 12 us -> 9.15 us  [on_device(): rows = lax.all_to_all(local, ('fsdp', 'tp'), 0, 0)]
    unnamed x39 -> x31, local copies, waits for them, and re-layouts: 6.62 us -> 5.88 us
  transfers between devices with their start and end apart: 34 -> 34, of which waited for: 11 -> 13; matrix products, arithmetic and copies ran while one was open for 2% -> 2% of each run, Pallas kernels for 30% -> 32%
where the time goes in v3:
time: 186 us; the launch traced here: 185 us
  starting transfers between devices  69.8 us (38%)
  Pallas kernels  62.8 us (34%)
  waiting for transfers between devices  41.6 us (22%)
  local copies, waits for them, and re-layouts  8.89 us (5%)
    pallas_call x23, Pallas kernels, call(): pl.pallas_call(body, grid_spec=pltpu.PrefetchScalarGridSpec(num_scalar_pr...  62.8 us
    ppermute x31, starting transfers between devices, send(): return lax.ppermute(value, 'fsdp', way)  50 us
    ppermute x31, waiting for transfers between devices, send(): return lax.ppermute(value, 'fsdp', way)  27.5 us
    all_to_all x1, waiting for transfers between devices, on_device(): rows = lax.all_to_all(local, ('fsdp', 'tp'), 0, 0)  12 us
    all_to_all x1, starting transfers between devices, on_device(): rows = lax.all_to_all(local, ('fsdp', 'tp'), 0, 0)  9.15 us
    unnamed x31, local copies, waits for them, and re-layouts  5.88 us
    all_to_all x1, starting transfers between devices, on_device(): crossed = lax.all_to_all(own_tokens.transpose(1, 0, 2), 'fsdp', 0, 0)  5.77 us
    all_to_all x1, starting transfers between devices, on_device(): columns = lax.all_to_all(copies(crossed, NX * NL, (sent,)), 'tp', 0, 0)  4.93 us
  transfers between devices with their start and end apart: 34, of which 13 were waited for; matrix products, arithmetic and copies ran while one was open for 2% of the time, Pallas kernels for 32%

profile of v3, /device:TPU:1, one launch (start us, length us, event | category | flops | bytes accessed | tf_op | source)
XLA Modules:
  0.0 185.1 jit_solution(1035596846588323103)
XLA Ops:
  0.6 3.8 %collective-permute-start = (bf16[256,128]{1,0:T(8,128)(2,1)}, bf16[256,128]{1,0:T(8,128)(2,1)S(1)}, u32[]{:S(2)}, u32[]{:S(2)}) collective-permute-start(bf16[256,128]{1,0:T(8,128)(2,1)} %param.16), channel_id=1, source_target_pairs={{0,16},{8,24},{16,0},{24,8},{32,48},{40,56},{48,32},{56,40},{64,80... | collective-permute-start | bytes 196616 | tf_op jit(solution)/shard_map/ppermute | solution.py:47
  4.5 2.6 %collective-permute-start.2 = (bf16[256,128]{1,0:T(8,128)(2,1)}, bf16[256,128]{1,0:T(8,128)(2,1)S(1)}, u32[]{:S(2)}, u32[]{:S(2)}) collective-permute-start(bf16[256,128]{1,0:T(8,128)(2,1)} %param.16), channel_id=1, source_target_pairs={{0,24},{8,16},{16,8},{24,0},{32,56},{40,48},{48,40},{56,32},{64,88... | collective-permute-start | bytes 196616 | tf_op jit(solution)/shard_map/ppermute | solution.py:47
  7.1 3.7 %collective-permute-done.2 = bf16[256,128]{1,0:T(8,128)(2,1)S(1)} collective-permute-done((bf16[256,128]{1,0:T(8,128)(2,1)}, bf16[256,128]{1,0:T(8,128)(2,1)S(1)}, u32[]{:S(2)}, u32[]{:S(2)}) %collective-permute-start.2) | collective-permute-done | bytes 65568 | tf_op jit(solution)/shard_map/ppermute | solution.py:47
  11.7 5.5 %collective-permute-start.4 = (bf16[4,256,128]{2,1,0:T(8,128)(2,1)S(1)}, bf16[4,256,128]{2,1,0:T(8,128)(2,1)S(1)}, u32[]{:S(2)}, u32[]{:S(2)}) collective-permute-start(bf16[4,256,128]{2,1,0:T(8,128)(2,1)S(1)} %pad_maximum_fusion.refs_3_.refs_5_), channel_id=1, source_target_pairs={{0,224},{8,232},{16,240},{24,248},{32,0},{40,8},{48,16},{56,24},{6... | collective-permute-start | bytes 786440 | tf_op jit(solution)/shard_map/ppermute | solution.py:47
  18.8 5.8 %all-to-all-start = ((bf16[32,16,256]{2,1,0:T(8,128)(2,1)}), bf16[32,16,256]{2,1,0:T(8,128)(2,1)S(1)}, u32[]{:S(2)}, u32[]{:S(2)}) async-start(bf16[32,16,256]{2,1,0:T(8,128)(2,1)} %bitcast.13), calls=%async_computation | async-start | bytes 524288 | tf_op jit(solution)/shard_map/all_to_all | solution.py:512
  27.8 4.6 %shard_map.123.refs_2_.refs_6_.refs_4_ = bf16[4,8,256,256]{3,2,1,0:T(8,128)(2,1)} custom-call(bf16[1024,1024]{1,0:T(8,128)(2,1)S(1)} %copy-done.2, bf16[1024,128]{1,0:T(8,128)(2,1)S(1)} %copy-done.5, bf16[1,8,128,128]{3,2,1,0:T(8,128)(2,1)S(1)} %shard_map.122.refs_2_.refs_4_, bf16[4,256,128]{2,1,0:T(8,128)(2,1)S(1)} %pad_maximum_fusion.refs_3_.refs_5_), custom_call_target="tpu_custom_call" | custom-call | flops 131072 | bytes 2048 | tf_op jit(solution)/shard_map/pallas_call | solution.py:56
  32.5 2.7 %collective-permute-start.7 = (bf16[4,256,128]{2,1,0:T(8,128)(2,1)S(1)}, bf16[4,256,128]{2,1,0:T(8,128)(2,1)S(1)}, u32[]{:S(2)}, u32[]{:S(2)}) collective-permute-start(bf16[4,256,128]{2,1,0:T(8,128)(2,1)S(1)} %get-tuple-element.33.refs_5_), channel_id=1, source_target_pairs={{0,224},{8,232},{16,240},{24,248},{32,0},{40,8},{48,16},{56,24},{6... | collective-permute-start | bytes 786440 | tf_op jit(solution)/shard_map/ppermute | solution.py:47
  37.6 4.2 %shard_map.125 = (f32[1024,128]{1,0:T(8,128)S(1)}, f32[128,128]{1,0:T(8,128)S(1)}, bf16[2,1024,512]{2,1,0:T(8,128)(2,1)S(1)}) custom-call(s32[11]{0:T(128)S(1)} %concatenate.9.refs_0_, bf16[1024,8192]{1,0:T(8,128)(2,1)} %refs_1_.27, bf16[1024,8192]{1,0:T(8,128)(2,1)} %refs_1_.27, bf16[1024,8192]{1,0:T(8,128)(2,1)} %refs_1_.27, bf16[128,8192]{1,0:T(8,128)(2,1)} %refs_1_.20, ...), custom_call_target="tpu_custom_call" | custom-call | flops 65536 | bytes 512 | tf_op jit(solution)/shard_map/pallas_call | solution.py:56
  43.7 2.7 %collective-permute-start.9 = (bf16[4,256,128]{2,1,0:T(8,128)(2,1)S(1)}, bf16[4,256,128]{2,1,0:T(8,128)(2,1)S(1)}, u32[]{:S(2)}, u32[]{:S(2)}) collective-permute-start(bf16[4,256,128]{2,1,0:T(8,128)(2,1)S(1)} %get-tuple-element.36.refs_5_), channel_id=1, source_target_pairs={{0,224},{8,232},{16,240},{24,248},{32,0},{40,8},{48,16},{56,24},{6... | collective-permute-start | bytes 786440 | tf_op jit(solution)/shard_map/ppermute | solution.py:47
  49.5 5.2 %shard_map.127 = (f32[1024,128]{1,0:T(8,128)S(1)}, f32[128,128]{1,0:T(8,128)S(1)}, bf16[2,1024,512]{2,1,0:T(8,128)(2,1)}) custom-call(s32[11]{0:T(128)S(1)} %concatenate.9.refs_0_, bf16[1024,8192]{1,0:T(8,128)(2,1)} %refs_1_.27, bf16[1024,8192]{1,0:T(8,128)(2,1)} %refs_1_.27, bf16[128,8192]{1,0:T(8,128)(2,1)} %refs_1_.20, bf16[128,8192]{1,0:T(8,128)(2,1)} %refs_1_.20, ...), custom_call_target="tpu_custom_call" | custom-call | flops 131072 | bytes 1024 | tf_op jit(solution)/shard_map/pallas_call | solution.py:56
  54.9 2.9 %collective-permute-start.11 = (bf16[2,256,128]{2,1,0:T(8,128)(2,1)S(1)}, bf16[2,256,128]{2,1,0:T(8,128)(2,1)S(1)}, u32[]{:S(2)}, u32[]{:S(2)}) collective-permute-start(bf16[2,256,128]{2,1,0:T(8,128)(2,1)S(1)} %slice.14), channel_id=1, source_target_pairs={{0,224},{8,232},{16,240},{24,248},{32,0},{40,8},{48,16},{56,24},{6... | collective-permute-start | bytes 393224 | tf_op jit(solution)/shard_map/ppermute | solution.py:47
  57.8 5.2 %shard_map.129 = (f32[1024,128]{1,0:T(8,128)S(1)}, f32[128,128]{1,0:T(8,128)S(1)}, bf16[2,1024,512]{2,1,0:T(8,128)(2,1)}) custom-call(s32[11]{0:T(128)S(1)} %concatenate.9.refs_0_, bf16[1024,8192]{1,0:T(8,128)(2,1)} %refs_1_.27, bf16[1024,8192]{1,0:T(8,128)(2,1)} %refs_1_.27, bf16[128,8192]{1,0:T(8,128)(2,1)} %refs_1_.20, bf16[128,8192]{1,0:T(8,128)(2,1)} %refs_1_.20, ...), custom_call_target="tpu_custom_call" | custom-call | flops 131072 | bytes 1024 | tf_op jit(solution)/shard_map/pallas_call | solution.py:56
  63.0 5.3 %shard_map.130 = (f32[1024,128]{1,0:T(8,128)S(1)}, f32[128,128]{1,0:T(8,128)S(1)}, bf16[2,1024,512]{2,1,0:T(8,128)(2,1)}) custom-call(s32[11]{0:T(128)S(1)} %concatenate.9.refs_0_, bf16[1024,8192]{1,0:T(8,128)(2,1)} %refs_1_.27, bf16[1024,8192]{1,0:T(8,128)(2,1)} %refs_1_.27, bf16[128,8192]{1,0:T(8,128)(2,1)} %refs_1_.20, bf16[128,8192]{1,0:T(8,128)(2,1)} %refs_1_.20, ...), custom_call_target="tpu_custom_call" | custom-call | flops 131072 | bytes 1024 | tf_op jit(solution)/shard_map/pallas_call | solution.py:56
  71.3 6.8 %shard_map.132.refs_3_ = bf16[128,1024]{1,0:T(8,128)(2,1)S(1)} custom-call(s32[11]{0:T(128)S(1)} %concatenate.9.refs_0_, bf16[1024,8192]{1,0:T(8,128)(2,1)} %refs_1_.27, bf16[4,256,128]{2,1,0:T(8,128)(2,1)S(1)} %constant_dynamic-update-slice_fusion.refs_2_, f32[1024,128]{1,0:T(8,128)S(1)} %get-tuple-element.44.refs_3_, ...), custom_call_target="tpu_custom_call" | custom-call | flops 262144 | bytes 2048 | tf_op jit(solution)/shard_map/pallas_call | solution.py:56
  78.7 2.7 %collective-permute-start.15 = (bf16[128,128]{1,0:T(8,128)(2,1)S(1)}, bf16[128,128]{1,0:T(8,128)(2,1)S(1)}, u32[]{:S(2)}, u32[]{:S(2)}) collective-permute-start(bf16[128,128]{1,0:T(8,128)(2,1)S(1)} %shard_map.131.refs_6_.refs_1_), channel_id=1, source_target_pairs={{0,16},{8,24},{16,0},{24,8},{32,48},{40,56},{48,32},{56,40},{64,80... | collective-permute-start | bytes 98312 | tf_op jit(solution)/shard_map/ppermute | solution.py:47
  88.5 2.7 %collective-permute-start.18 = (bf16[2,1024,512]{2,1,0:T(8,128)(2,1)}, bf16[2,1024,512]{2,1,0:T(8,128)(2,1)}, u32[]{:S(2)}, u32[]{:S(2)}) collective-permute-start(bf16[2,1024,512]{2,1,0:T(8,128)(2,1)} %shard_map.135), channel_id=1, source_target_pairs={{0,8},{8,0},{16,24},{24,16},{32,40},{40,32},{48,56},{56,48},{64,72... | collective-permute-start | bytes 6291464 | tf_op jit(solution)/shard_map/ppermute | solution.py:47
  94.3 4.9 %all-to-all-start.1 = ((bf16[8,32,16,256]{3,2,1,0:T(8,128)(2,1)}), bf16[8,32,16,256]{3,2,1,0:T(8,128)(2,1)S(1)}, u32[]{:S(2)}, u32[]{:S(2)}) async-start(bf16[8,32,16,256]{3,2,1,0:T(8,128)(2,1)} %copy-done.1), calls=%async_computation.1 | async-start | bytes 4194304 | tf_op jit(solution)/shard_map/all_to_all | solution.py:545
  99.2 4.2 %shard_map.137.refs_0_ = f32[2,2,512,256]{3,2,1,0:T(8,128)S(1)} custom-call(s32[11]{0:T(128)S(1)} %concatenate.9.refs_0_, bf16[1024,8192]{1,0:T(8,128)(2,1)} %refs_1_.27, bf16[2,1024,512]{2,1,0:T(8,128)(2,1)} %collective-permute-done.19.refs_2_, bf16[128,1024]{1,0:T(8,128)(2,1)S(1)} %shard_map.132.refs_3_, ...), custom_call_target="tpu_custom_call" | custom-call | flops 131072 | bytes 2560 | tf_op jit(solution)/shard_map/pallas_call | solution.py:56
  106.1 4.2 %shard_map.139.refs_0_ = f32[2,2,512,256]{3,2,1,0:T(8,128)S(1)} custom-call(s32[11]{0:T(128)S(1)} %concatenate.9.refs_0_, bf16[1024,8192]{1,0:T(8,128)(2,1)} %refs_1_.27, bf16[2,1024,512]{2,1,0:T(8,128)(2,1)} %collective-permute-done.18.refs_2_, bf16[128,1024]{1,0:T(8,128)(2,1)S(1)} %shard_map.132.refs_3_, ...), custom_call_target="tpu_custom_call" | custom-call | flops 131072 | bytes 2560 | tf_op jit(solution)/shard_map/pallas_call | solution.py:56
  110.4 7.8 %collective-permute-done.23.refs_2_.refs_3_ = bf16[1152,256]{1,0:T(8,128)(2,1)S(1)} collective-permute-done((bf16[1152,256]{1,0:T(8,128)(2,1)S(1)}, bf16[1152,256]{1,0:T(8,128)(2,1)S(1)}, u32[]{:S(2)}, u32[]{:S(2)}) %collective-permute-start.23) | collective-permute-done | bytes 589856 | tf_op jit(solution)/shard_map/ppermute | solution.py:47
  122.1 3.0 %collective-permute-start.5 = (bf16[1,1024,512]{2,1,0:T(8,128)(2,1)}, bf16[1,1024,512]{2,1,0:T(8,128)(2,1)}, u32[]{:S(2)}, u32[]{:S(2)}) collective-permute-start(bf16[1,1024,512]{2,1,0:T(8,128)(2,1)} %get-tuple-element.61), channel_id=1, source_target_pairs={{0,8},{8,0},{16,24},{24,16},{32,40},{40,32},{48,56},{56,48},{64,72... | collective-permute-start | bytes 3145736 | tf_op jit(solution)/shard_map/ppermute | solution.py:47
  125.1 4.2 %shard_map.141.refs_0_ = f32[2,2,512,256]{3,2,1,0:T(8,128)S(1)} custom-call(s32[11]{0:T(128)S(1)} %concatenate.9.refs_0_, bf16[1024,8192]{1,0:T(8,128)(2,1)} %refs_1_.27, bf16[2,1024,512]{2,1,0:T(8,128)(2,1)} %collective-permute-done.13.refs_2_, bf16[128,1024]{1,0:T(8,128)(2,1)S(1)} %shard_map.132.refs_3_, ...), custom_call_target="tpu_custom_call" | custom-call | flops 131072 | bytes 2560 | tf_op jit(solution)/shard_map/pallas_call | solution.py:56
  129.4 3.6 %collective-permute-done.25.refs_2_ = bf16[1152,256]{1,0:T(8,128)(2,1)S(1)} collective-permute-done((bf16[1152,256]{1,0:T(8,128)(2,1)S(1)}, bf16[1152,256]{1,0:T(8,128)(2,1)S(1)}, u32[]{:S(2)}, u32[]{:S(2)}) %collective-permute-start.25) | collective-permute-done | bytes 589856 | tf_op jit(solution)/shard_map/ppermute | solution.py:47
  137.1 3.4 %collective-permute-start.26 = (bf16[8,128,256]{2,1,0:T(8,128)(2,1)}, bf16[8,128,256]{2,1,0:T(8,128)(2,1)}, u32[]{:S(2)}, u32[]{:S(2)}) collective-permute-start(bf16[8,128,256]{2,1,0:T(8,128)(2,1)} %shard_map.143.refs_2_), channel_id=1, source_target_pairs={{0,8},{8,0},{16,24},{24,16},{32,40},{40,32},{48,56},{56,48},{64,72... | collective-permute-start | bytes 1572872 | tf_op jit(solution)/shard_map/ppermute | solution.py:47
  142.4 2.5 %shard_map.145.refs_6_.refs_3_ = f32[4,128,256]{2,1,0:T(8,128)S(1)} custom-call(s32[11]{0:T(128)S(1)} %concatenate.9.refs_0_, s32[32]{0:T(128)S(1)} %copy-done.13, bf16[8,128,256]{2,1,0:T(8,128)(2,1)} %shard_map.143.refs_2_, bf16[8,128,256]{2,1,0:T(8,128)(2,1)} %collective-permute-done.26.refs_3_, bf16[8,32,16,256]{3,2,1,0:T(8,128)(2,1)S(1)} %all-to-all-done.1.refs_4_), custom_call_target="tpu_custom_call" | custom-call | flops 65536 | bytes 1024 | tf_op jit(solution)/shard_map/pallas_call | solution.py:56
  144.9 3.4 %collective-permute-start.29 = (bf16[4,128,256]{2,1,0:T(8,128)(2,1)S(1)}, bf16[4,128,256]{2,1,0:T(8,128)(2,1)S(1)}, u32[]{:S(2)}, u32[]{:S(2)}) collective-permute-start(bf16[4,128,256]{2,1,0:T(8,128)(2,1)S(1)} %convert_element_type.3), channel_id=1, source_target_pairs={{0,16},{8,24},{16,0},{24,8},{32,48},{40,56},{48,32},{56,40},{64,80... | collective-permute-start | bytes 786440 | tf_op jit(solution)/shard_map/ppermute | solution.py:47
  148.4 2.5 %shard_map.146.refs_0_ = f32[1,2,512,256]{3,2,1,0:T(8,128)S(1)} custom-call(s32[11]{0:T(128)S(1)} %concatenate.9.refs_0_, bf16[1024,8192]{1,0:T(8,128)(2,1)} %refs_1_.27, bf16[1,1024,512]{2,1,0:T(8,128)(2,1)} %collective-permute-done.5.refs_2_, bf16[128,1024]{1,0:T(8,128)(2,1)S(1)} %shard_map.132.refs_3_, ...), custom_call_target="tpu_custom_call" | custom-call | flops 65536 | bytes 1280 | tf_op jit(solution)/shard_map/pallas_call | solution.py:56
  150.9 3.4 %collective-permute-done.28.refs_2_ = bf16[1024,256]{1,0:T(8,128)(2,1)} collective-permute-done((bf16[1024,256]{1,0:T(8,128)(2,1)}, bf16[1024,256]{1,0:T(8,128)(2,1)}, u32[]{:S(2)}, u32[]{:S(2)}) %collective-permute-start.28) | collective-permute-done | bytes 524320 | tf_op jit(solution)/shard_map/ppermute | solution.py:47
  155.1 2.8 %shard_map.147 = (f32[512,256]{1,0:T(8,128)S(1)}, bf16[512,256]{1,0:T(8,128)(2,1)S(1)}, f32[256,1,128]{2,1,0:T(1,128)}) custom-call(f32[1,2,512,256]{3,2,1,0:T(8,128)S(1)} %shard_map.146.refs_0_, bf16[1024,256]{1,0:T(8,128)(2,1)} %collective-permute-done.27.refs_1_, bf16[1024,256]{1,0:T(8,128)(2,1)} %collective-permute-done.28.refs_2_, ...), custom_call_target="tpu_custom_call" | custom-call | flops 1024 | bytes 1024 | tf_op jit(solution)/shard_map/pallas_call | solution.py:56
  157.8 3.4 %collective-permute-start.30 = (bf16[512,256]{1,0:T(8,128)(2,1)S(1)}, bf16[512,256]{1,0:T(8,128)(2,1)S(1)}, u32[]{:S(2)}, u32[]{:S(2)}) collective-permute-start(bf16[512,256]{1,0:T(8,128)(2,1)S(1)} %get-tuple-element.58), channel_id=1, source_target_pairs={{0,16},{8,24},{16,0},{24,8},{32,48},{40,56},{48,32},{56,40},{64,80... | collective-permute-start | bytes 786440 | tf_op jit(solution)/shard_map/ppermute | solution.py:47
  161.2 9.1 %all-to-all-start.2 = ((f32[256,1,128]{2,1,0:T(1,128)}), f32[256,1,128]{2,1,0:T(1,128)S(1)}, u32[]{:S(2)}, u32[]{:S(2)}) async-start(f32[256,1,128]{2,1,0:T(1,128)} %get-tuple-element.59), calls=%async_computation.2 | async-start | bytes 262144 | tf_op jit(solution)/shard_map/all_to_all | solution.py:558
  171.2 12.0 %all-to-all-done.2.refs_0_ = f32[256,1,128]{2,1,0:T(1,128)S(1)} async-done(((f32[256,1,128]{2,1,0:T(1,128)}), f32[256,1,128]{2,1,0:T(1,128)S(1)}, u32[]{:S(2)}, u32[]{:S(2)}) %all-to-all-start.2) | async-done | bytes 131104 | tf_op jit(solution)/shard_map/all_to_all | solution.py:558
  (106 shorter events, 43.0 us)
Async XLA Ops:
  0.6 6.5 %collective-permute-start = (bf16[256,128]{1,0:T(8,128)(2,1)}, bf16[256,128]{1,0:T(8,128)(2,1)S(1)}, u32[]{:S(2)}, u32[]{:S(2)}) collective-permute-start(bf16[256,128]{1,0:T(8,128)(2,1)} %param.16), channel_id=1, source_target_pairs={{0,16},{8,24},{16,0},{24,8},{32,48},{40,56},{48,32},{56,40},{64,80... | collective-permute-start | bytes 196616 | tf_op jit(solution)/shard_map/ppermute | solution.py:47
  4.5 6.3 %collective-permute-start.2 = (bf16[256,128]{1,0:T(8,128)(2,1)}, bf16[256,128]{1,0:T(8,128)(2,1)S(1)}, u32[]{:S(2)}, u32[]{:S(2)}) collective-permute-start(bf16[256,128]{1,0:T(8,128)(2,1)} %param.16), channel_id=1, source_target_pairs={{0,24},{8,16},{16,8},{24,0},{32,56},{40,48},{48,40},{56,32},{64,88... | collective-permute-start | bytes 196616 | tf_op jit(solution)/shard_map/ppermute | solution.py:47
  11.7 20.8 %collective-permute-start.4 = (bf16[4,256,128]{2,1,0:T(8,128)(2,1)S(1)}, bf16[4,256,128]{2,1,0:T(8,128)(2,1)S(1)}, u32[]{:S(2)}, u32[]{:S(2)}) collective-permute-start(bf16[4,256,128]{2,1,0:T(8,128)(2,1)S(1)} %pad_maximum_fusion.refs_3_.refs_5_), channel_id=1, source_target_pairs={{0,224},{8,232},{16,240},{24,248},{32,0},{40,8},{48,16},{56,24},{6... | collective-permute-start | bytes 786440 | tf_op jit(solution)/shard_map/ppermute | solution.py:47
  17.1 15.3 %collective-permute-start.3 = (bf16[4,256,128]{2,1,0:T(8,128)(2,1)S(1)}, bf16[4,256,128]{2,1,0:T(8,128)(2,1)S(1)}, u32[]{:S(2)}, u32[]{:S(2)}) collective-permute-start(bf16[4,256,128]{2,1,0:T(8,128)(2,1)S(1)} %pad_maximum_fusion.refs_3_.refs_5_), channel_id=1, source_target_pairs={{0,32},{8,40},{16,48},{24,56},{32,64},{40,72},{48,80},{56,88},{64,... | collective-permute-start | bytes 786440 | tf_op jit(solution)/shard_map/ppermute | solution.py:47
  18.8 18.7 %all-to-all-start = ((bf16[32,16,256]{2,1,0:T(8,128)(2,1)}), bf16[32,16,256]{2,1,0:T(8,128)(2,1)S(1)}, u32[]{:S(2)}, u32[]{:S(2)}) async-start(bf16[32,16,256]{2,1,0:T(8,128)(2,1)} %bitcast.13), calls=%async_computation | async-start | bytes 524288 | tf_op jit(solution)/shard_map/all_to_all | solution.py:512
  32.5 9.3 %collective-permute-start.7 = (bf16[4,256,128]{2,1,0:T(8,128)(2,1)S(1)}, bf16[4,256,128]{2,1,0:T(8,128)(2,1)S(1)}, u32[]{:S(2)}, u32[]{:S(2)}) collective-permute-start(bf16[4,256,128]{2,1,0:T(8,128)(2,1)S(1)} %get-tuple-element.33.refs_5_), channel_id=1, source_target_pairs={{0,224},{8,232},{16,240},{24,248},{32,0},{40,8},{48,16},{56,24},{6... | collective-permute-start | bytes 786440 | tf_op jit(solution)/shard_map/ppermute | solution.py:47
  35.2 8.4 %collective-permute-start.6 = (bf16[4,256,128]{2,1,0:T(8,128)(2,1)S(1)}, bf16[4,256,128]{2,1,0:T(8,128)(2,1)S(1)}, u32[]{:S(2)}, u32[]{:S(2)}) collective-permute-start(bf16[4,256,128]{2,1,0:T(8,128)(2,1)S(1)} %get-tuple-element.31.refs_7_.refs_6_), channel_id=1, source_target_pairs={{0,32},{8,40},{16,48},{24,56},{32,64},{40,72},{48,80},{56,88},{64,... | collective-permute-start | bytes 786440 | tf_op jit(solution)/shard_map/ppermute | solution.py:47
  43.7 11.1 %collective-permute-start.8 = (bf16[4,256,128]{2,1,0:T(8,128)(2,1)S(1)}, bf16[4,256,128]{2,1,0:T(8,128)(2,1)S(1)}, u32[]{:S(2)}, u32[]{:S(2)}) collective-permute-start(bf16[4,256,128]{2,1,0:T(8,128)(2,1)S(1)} %get-tuple-element.35.refs_6_), channel_id=1, source_target_pairs={{0,32},{8,40},{16,48},{24,56},{32,64},{40,72},{48,80},{56,88},{64,... | collective-permute-start | bytes 786440 | tf_op jit(solution)/shard_map/ppermute | solution.py:47
  43.7 11.1 %collective-permute-start.9 = (bf16[4,256,128]{2,1,0:T(8,128)(2,1)S(1)}, bf16[4,256,128]{2,1,0:T(8,128)(2,1)S(1)}, u32[]{:S(2)}, u32[]{:S(2)}) collective-permute-start(bf16[4,256,128]{2,1,0:T(8,128)(2,1)S(1)} %get-tuple-element.36.refs_5_), channel_id=1, source_target_pairs={{0,224},{8,232},{16,240},{24,248},{32,0},{40,8},{48,16},{56,24},{6... | collective-permute-start | bytes 786440 | tf_op jit(solution)/shard_map/ppermute | solution.py:47
  47.5 37.1 %collective-permute-start.14 = (bf16[1,1024,512]{2,1,0:T(8,128)(2,1)S(1)}, bf16[1,1024,512]{2,1,0:T(8,128)(2,1)S(1)}, u32[]{:S(2)}, u32[]{:S(2)}) collective-permute-start(bf16[1,1024,512]{2,1,0:T(8,128)(2,1)S(1)} %get-tuple-element.60), channel_id=1, source_target_pairs={{0,8},{8,0},{16,24},{24,16},{32,40},{40,32},{48,56},{56,48},{64,72... | collective-permute-start | bytes 3145736 | tf_op jit(solution)/shard_map/ppermute | solution.py:47
  54.8 13.5 %collective-permute-start.10 = (bf16[2,256,128]{2,1,0:T(8,128)(2,1)S(1)}, bf16[2,256,128]{2,1,0:T(8,128)(2,1)S(1)}, u32[]{:S(2)}, u32[]{:S(2)}) collective-permute-start(bf16[2,256,128]{2,1,0:T(8,128)(2,1)S(1)} %slice.13), channel_id=1, source_target_pairs={{0,32},{8,40},{16,48},{24,56},{32,64},{40,72},{48,80},{56,88},{64,... | collective-permute-start | bytes 393224 | tf_op jit(solution)/shard_map/ppermute | solution.py:47
  54.9 13.4 %collective-permute-start.11 = (bf16[2,256,128]{2,1,0:T(8,128)(2,1)S(1)}, bf16[2,256,128]{2,1,0:T(8,128)(2,1)S(1)}, u32[]{:S(2)}, u32[]{:S(2)}) collective-permute-start(bf16[2,256,128]{2,1,0:T(8,128)(2,1)S(1)} %slice.14), channel_id=1, source_target_pairs={{0,224},{8,232},{16,240},{24,248},{32,0},{40,8},{48,16},{56,24},{6... | collective-permute-start | bytes 393224 | tf_op jit(solution)/shard_map/ppermute | solution.py:47
  69.7 29.5 %collective-permute-start.19 = (bf16[2,1024,512]{2,1,0:T(8,128)(2,1)}, bf16[2,1024,512]{2,1,0:T(8,128)(2,1)}, u32[]{:S(2)}, u32[]{:S(2)}) collective-permute-start(bf16[2,1024,512]{2,1,0:T(8,128)(2,1)} %shard_map.136), channel_id=1, source_target_pairs={{0,8},{8,0},{16,24},{24,16},{32,40},{40,32},{48,56},{56,48},{64,72... | collective-permute-start | bytes 6291464 | tf_op jit(solution)/shard_map/ppermute | solution.py:47
  78.1 6.5 %collective-permute-start.12 = (bf16[128,1024]{1,0:T(8,128)(2,1)S(1)}, bf16[128,1024]{1,0:T(8,128)(2,1)S(1)}, u32[]{:S(2)}, u32[]{:S(2)}) collective-permute-start(bf16[128,1024]{1,0:T(8,128)(2,1)S(1)} %shard_map.132.refs_3_), channel_id=1, source_target_pairs={{0,8},{8,0},{16,24},{24,16},{32,40},{40,32},{48,56},{56,48},{64,72... | collective-permute-start | bytes 786440 | tf_op jit(solution)/shard_map/ppermute | solution.py:47
  78.7 4.3 %collective-permute-start.15 = (bf16[128,128]{1,0:T(8,128)(2,1)S(1)}, bf16[128,128]{1,0:T(8,128)(2,1)S(1)}, u32[]{:S(2)}, u32[]{:S(2)}) collective-permute-start(bf16[128,128]{1,0:T(8,128)(2,1)S(1)} %shard_map.131.refs_6_.refs_1_), channel_id=1, source_target_pairs={{0,16},{8,24},{16,0},{24,8},{32,48},{40,56},{48,32},{56,40},{64,80... | collective-permute-start | bytes 98312 | tf_op jit(solution)/shard_map/ppermute | solution.py:47
  83.4 4.3 %collective-permute-start.16 = (bf16[128,256]{1,0:T(8,128)(2,1)S(1)}, bf16[128,256]{1,0:T(8,128)(2,1)S(1)}, u32[]{:S(2)}, u32[]{:S(2)}) collective-permute-start(bf16[128,256]{1,0:T(8,128)(2,1)S(1)} %pad_maximum_fusion.1.refs_0_), channel_id=1, source_target_pairs={{0,32},{8,40},{16,48},{24,56},{32,64},{40,72},{48,80},{56,88},{64,... | collective-permute-start | bytes 196616 | tf_op jit(solution)/shard_map/ppermute | solution.py:47
  88.5 17.6 %collective-permute-start.18 = (bf16[2,1024,512]{2,1,0:T(8,128)(2,1)}, bf16[2,1024,512]{2,1,0:T(8,128)(2,1)}, u32[]{:S(2)}, u32[]{:S(2)}) collective-permute-start(bf16[2,1024,512]{2,1,0:T(8,128)(2,1)} %shard_map.135), channel_id=1, source_target_pairs={{0,8},{8,0},{16,24},{24,16},{32,40},{40,32},{48,56},{56,48},{64,72... | collective-permute-start | bytes 6291464 | tf_op jit(solution)/shard_map/ppermute | solution.py:47
  91.2 33.9 %collective-permute-start.13 = (bf16[2,1024,512]{2,1,0:T(8,128)(2,1)}, bf16[2,1024,512]{2,1,0:T(8,128)(2,1)}, u32[]{:S(2)}, u32[]{:S(2)}) collective-permute-start(bf16[2,1024,512]{2,1,0:T(8,128)(2,1)} %get-tuple-element.46), channel_id=1, source_target_pairs={{0,8},{8,0},{16,24},{24,16},{32,40},{40,32},{48,56},{56,48},{64,72... | collective-permute-start | bytes 6291464 | tf_op jit(solution)/shard_map/ppermute | solution.py:47
  91.2 12.3 %collective-permute-start.21 = (bf16[640,256]{1,0:T(8,128)(2,1)}, bf16[640,256]{1,0:T(8,128)(2,1)S(1)}, u32[]{:S(2)}, u32[]{:S(2)}) collective-permute-start(bf16[640,256]{1,0:T(8,128)(2,1)} %get-tuple-element.50), channel_id=1, source_target_pairs={{0,224},{8,232},{16,240},{24,248},{32,0},{40,8},{48,16},{56,24},{6... | collective-permute-start | bytes 983048 | tf_op jit(solution)/shard_map/ppermute | solution.py:47
  91.2 12.3 %collective-permute-start.20 = (bf16[640,256]{1,0:T(8,128)(2,1)S(1)}, bf16[640,256]{1,0:T(8,128)(2,1)}, u32[]{:S(2)}, u32[]{:S(2)}) collective-permute-start(bf16[640,256]{1,0:T(8,128)(2,1)S(1)} %get-tuple-element.48.refs_1_.refs_5_), channel_id=1, source_target_pairs={{0,32},{8,40},{16,48},{24,56},{32,64},{40,72},{48,80},{56,88},{64,... | collective-permute-start | bytes 983048 | tf_op jit(solution)/shard_map/ppermute | solution.py:47
  94.3 47.7 %all-to-all-start.1 = ((bf16[8,32,16,256]{3,2,1,0:T(8,128)(2,1)}), bf16[8,32,16,256]{3,2,1,0:T(8,128)(2,1)S(1)}, u32[]{:S(2)}, u32[]{:S(2)}) async-start(bf16[8,32,16,256]{3,2,1,0:T(8,128)(2,1)} %copy-done.1), calls=%async_computation.1 | async-start | bytes 4194304 | tf_op jit(solution)/shard_map/all_to_all | solution.py:545
  104.6 13.6 %collective-permute-start.23 = (bf16[1152,256]{1,0:T(8,128)(2,1)S(1)}, bf16[1152,256]{1,0:T(8,128)(2,1)S(1)}, u32[]{:S(2)}, u32[]{:S(2)}) collective-permute-start(bf16[1152,256]{1,0:T(8,128)(2,1)S(1)} %get-tuple-element.52), channel_id=1, source_target_pairs={{0,224},{8,232},{16,240},{24,248},{32,0},{40,8},{48,16},{56,24},{6... | collective-permute-start | bytes 1769480 | tf_op jit(solution)/shard_map/ppermute | solution.py:47
  105.9 14.5 %collective-permute-start.22 = (bf16[1152,256]{1,0:T(8,128)(2,1)S(1)}, bf16[1152,256]{1,0:T(8,128)(2,1)S(1)}, u32[]{:S(2)}, u32[]{:S(2)}) collective-permute-start(bf16[1152,256]{1,0:T(8,128)(2,1)S(1)} %get-tuple-element.51.refs_5_), channel_id=1, source_target_pairs={{0,32},{8,40},{16,48},{24,56},{32,64},{40,72},{48,80},{56,88},{64,... | collective-permute-start | bytes 1769480 | tf_op jit(solution)/shard_map/ppermute | solution.py:47
  120.6 12.4 %collective-permute-start.25 = (bf16[1152,256]{1,0:T(8,128)(2,1)S(1)}, bf16[1152,256]{1,0:T(8,128)(2,1)S(1)}, u32[]{:S(2)}, u32[]{:S(2)}) collective-permute-start(bf16[1152,256]{1,0:T(8,128)(2,1)S(1)} %get-tuple-element.54), channel_id=1, source_target_pairs={{0,224},{8,232},{16,240},{24,248},{32,0},{40,8},{48,16},{56,24},{6... | collective-permute-start | bytes 1769480 | tf_op jit(solution)/shard_map/ppermute | solution.py:47
  120.9 13.6 %collective-permute-start.24 = (bf16[1152,256]{1,0:T(8,128)(2,1)S(1)}, bf16[1152,256]{1,0:T(8,128)(2,1)S(1)}, u32[]{:S(2)}, u32[]{:S(2)}) collective-permute-start(bf16[1152,256]{1,0:T(8,128)(2,1)S(1)} %get-tuple-element.53.refs_5_), channel_id=1, source_target_pairs={{0,32},{8,40},{16,48},{24,56},{32,64},{40,72},{48,80},{56,88},{64,... | collective-permute-start | bytes 1769480 | tf_op jit(solution)/shard_map/ppermute | solution.py:47
  122.1 26.3 %collective-permute-start.5 = (bf16[1,1024,512]{2,1,0:T(8,128)(2,1)}, bf16[1,1024,512]{2,1,0:T(8,128)(2,1)}, u32[]{:S(2)}, u32[]{:S(2)}) collective-permute-start(bf16[1,1024,512]{2,1,0:T(8,128)(2,1)} %get-tuple-element.61), channel_id=1, source_target_pairs={{0,8},{8,0},{16,24},{24,16},{32,40},{40,32},{48,56},{56,48},{64,72... | collective-permute-start | bytes 3145736 | tf_op jit(solution)/shard_map/ppermute | solution.py:47
  137.1 5.3 %collective-permute-start.26 = (bf16[8,128,256]{2,1,0:T(8,128)(2,1)}, bf16[8,128,256]{2,1,0:T(8,128)(2,1)}, u32[]{:S(2)}, u32[]{:S(2)}) collective-permute-start(bf16[8,128,256]{2,1,0:T(8,128)(2,1)} %shard_map.143.refs_2_), channel_id=1, source_target_pairs={{0,8},{8,0},{16,24},{24,16},{32,40},{40,32},{48,56},{56,48},{64,72... | collective-permute-start | bytes 1572872 | tf_op jit(solution)/shard_map/ppermute | solution.py:47
  140.5 13.9 %collective-permute-start.28 = (bf16[1024,256]{1,0:T(8,128)(2,1)}, bf16[1024,256]{1,0:T(8,128)(2,1)}, u32[]{:S(2)}, u32[]{:S(2)}) collective-permute-start(bf16[1024,256]{1,0:T(8,128)(2,1)} %get-tuple-element.56), channel_id=1, source_target_pairs={{0,224},{8,232},{16,240},{24,248},{32,0},{40,8},{48,16},{56,24},{6... | collective-permute-start | bytes 1572872 | tf_op jit(solution)/shard_map/ppermute | solution.py:47
  140.5 14.6 %collective-permute-start.27 = (bf16[1024,256]{1,0:T(8,128)(2,1)S(1)}, bf16[1024,256]{1,0:T(8,128)(2,1)}, u32[]{:S(2)}, u32[]{:S(2)}) collective-permute-start(bf16[1024,256]{1,0:T(8,128)(2,1)S(1)} %get-tuple-element.55.refs_8_.refs_5_), channel_id=1, source_target_pairs={{0,32},{8,40},{16,48},{24,56},{32,64},{40,72},{48,80},{56,88},{64,... | collective-permute-start | bytes 1572872 | tf_op jit(solution)/shard_map/ppermute | solution.py:47
  144.9 10.1 %collective-permute-start.29 = (bf16[4,128,256]{2,1,0:T(8,128)(2,1)S(1)}, bf16[4,128,256]{2,1,0:T(8,128)(2,1)S(1)}, u32[]{:S(2)}, u32[]{:S(2)}) collective-permute-start(bf16[4,128,256]{2,1,0:T(8,128)(2,1)S(1)} %convert_element_type.3), channel_id=1, source_target_pairs={{0,16},{8,24},{16,0},{24,8},{32,48},{40,56},{48,32},{56,40},{64,80... | collective-permute-start | bytes 786440 | tf_op jit(solution)/shard_map/ppermute | solution.py:47
  157.8 12.5 %collective-permute-start.30 = (bf16[512,256]{1,0:T(8,128)(2,1)S(1)}, bf16[512,256]{1,0:T(8,128)(2,1)S(1)}, u32[]{:S(2)}, u32[]{:S(2)}) collective-permute-start(bf16[512,256]{1,0:T(8,128)(2,1)S(1)} %get-tuple-element.58), channel_id=1, source_target_pairs={{0,16},{8,24},{16,0},{24,8},{32,48},{40,56},{48,32},{56,40},{64,80... | collective-permute-start | bytes 786440 | tf_op jit(solution)/shard_map/ppermute | solution.py:47
  161.2 22.0 %all-to-all-start.2 = ((f32[256,1,128]{2,1,0:T(1,128)}), f32[256,1,128]{2,1,0:T(1,128)S(1)}, u32[]{:S(2)}, u32[]{:S(2)}) async-start(f32[256,1,128]{2,1,0:T(1,128)} %get-tuple-element.59), calls=%async_computation.2 | async-start | bytes 262144 | tf_op jit(solution)/shard_map/all_to_all | solution.py:558
  (17 other events, 77.8 us)

commit v4 on v3

--- a/solution.py
+++ b/solution.py
@@ -526,10 +526,10 @@
     other_x[1, 7] = send(picked, CORE)
     up3, down3 = joined((up3, down3), (sums[1],))
     last = jnp.concatenate([send(up3[:2], UP), send(down3[2:], DOWN)])
+    *sums, picked = project(where, train_x, val_x, (3, 5), [down3, up3], sums)
+    other_x[3, 5] = send(picked, CORE)
     *sums, picked = project(where, train_x, val_x, (2, 6), [down2, up2], sums)
-    *sums, later = project(where, train_x, val_x, (3, 5), [down3, up3], sums)
     own_pull = val_pulls(where, val_x, last, sums[1], val_attention, val_target)
-    other_x[3, 5] = send(joined((later,), (own_pull,))[0], CORE)
     pull = jnp.concatenate([own_pull, send(own_pull, YHI)], axis=1)
     p_up, p_down = send(pull, UP), send(pull, DOWN)
     grads = value_grads(where, train_x, last, sums[0], attention, train_target, (own_pull,))

time: 186 us -> 188 us (1.011)
  waiting for transfers between devices: 41.6 us -> 47 us
  starting transfers between devices: 69.8 us -> 66.6 us
    ppermute x31, starting transfers between devices: 50 us -> 39.5 us  [send(): return lax.ppermute(value, 'fsdp', way)]
    ppermute x31, waiting for transfers between devices: 27.5 us -> 35 us  [send(): return lax.ppermute(value, 'fsdp', way)]
    all_to_all x1, starting transfers between devices: 5.77 us -> 12.8 us  [on_device(): crossed = lax.all_to_all(own_tokens.transpose(1, 0, 2), 'fsdp', 0, 0)]
    all_to_all x1, waiting for transfers between devices: 2.15 us -> 0.01 us  [on_device(): crossed = lax.all_to_all(own_tokens.transpose(1, 0, 2), 'fsdp', 0, 0)]
  transfers between devices with their start and end apart: 34 -> 34, of which waited for: 13 -> 14; matrix products, arithmetic and copies ran while one was open for 2% -> 1% of each run, Pallas kernels for 32% -> 32%
where the time goes in v4:
time: 188 us; the launch traced here: 187 us
  starting transfers between devices  66.6 us (35%)
  Pallas kernels  62.8 us (33%)
  waiting for transfers between devices  47 us (25%)
  local copies, waits for them, and re-layouts  8.36 us (4%)
    pallas_call x23, Pallas kernels, call(): pl.pallas_call(body, grid_spec=pltpu.PrefetchScalarGridSpec(num_scalar_pr...  62.8 us
    ppermute x31, starting transfers between devices, send(): return lax.ppermute(value, 'fsdp', way)  39.5 us
    ppermute x31, waiting for transfers between devices, send(): return lax.ppermute(value, 'fsdp', way)  35 us
    all_to_all x1, starting transfers between devices, on_device(): crossed = lax.all_to_all(own_tokens.transpose(1, 0, 2), 'fsdp', 0, 0)  12.8 us
    all_to_all x1, waiting for transfers between devices, on_device(): rows = lax.all_to_all(local, ('fsdp', 'tp'), 0, 0)  12 us
    all_to_all x1, starting transfers between devices, on_device(): rows = lax.all_to_all(local, ('fsdp', 'tp'), 0, 0)  10.2 us
    unnamed x31, local copies, waits for them, and re-layouts  5.2 us
    all_to_all x1, starting transfers between devices, on_device(): columns = lax.all_to_all(copies(crossed, NX * NL, (sent,)), 'tp', 0, 0)  4.11 us
  transfers between devices with their start and end apart: 34, of which 14 were waited for; matrix products, arithmetic and copies ran while one was open for 1% of the time, Pallas kernels for 32%

profile of v4, /device:TPU:1, one launch (start us, length us, event | category | flops | bytes accessed | tf_op | source)
XLA Modules:
  0.0 186.8 jit_solution(16413327063332776534)
XLA Ops:
  2.5 12.8 %all-to-all-start = ((bf16[32,16,256]{2,1,0:T(8,128)(2,1)}), bf16[32,16,256]{2,1,0:T(8,128)(2,1)S(1)}, u32[]{:S(2)}, u32[]{:S(2)}) async-start(bf16[32,16,256]{2,1,0:T(8,128)(2,1)} %bitcast.13), calls=%async_computation | async-start | bytes 524288 | tf_op jit(solution)/shard_map/all_to_all | solution.py:512
  15.3 3.0 %collective-permute-start = (bf16[256,128]{1,0:T(8,128)(2,1)}, bf16[256,128]{1,0:T(8,128)(2,1)S(1)}, u32[]{:S(2)}, u32[]{:S(2)}) collective-permute-start(bf16[256,128]{1,0:T(8,128)(2,1)} %param.16), channel_id=1, source_target_pairs={{0,16},{8,24},{16,0},{24,8},{32,48},{40,56},{48,32},{56,40},{64,80... | collective-permute-start | bytes 196616 | tf_op jit(solution)/shard_map/ppermute | solution.py:47
  18.9 2.0 %collective-permute-done = bf16[256,128]{1,0:T(8,128)(2,1)S(1)} collective-permute-done((bf16[256,128]{1,0:T(8,128)(2,1)}, bf16[256,128]{1,0:T(8,128)(2,1)S(1)}, u32[]{:S(2)}, u32[]{:S(2)}) %collective-permute-start) | collective-permute-done | bytes 65568 | tf_op jit(solution)/shard_map/ppermute | solution.py:47
  20.9 5.2 %collective-permute-done.2 = bf16[256,128]{1,0:T(8,128)(2,1)S(1)} collective-permute-done((bf16[256,128]{1,0:T(8,128)(2,1)}, bf16[256,128]{1,0:T(8,128)(2,1)S(1)}, u32[]{:S(2)}, u32[]{:S(2)}) %collective-permute-start.2) | collective-permute-done | bytes 65568 | tf_op jit(solution)/shard_map/ppermute | solution.py:47
  27.0 2.0 %collective-permute-start.4 = (bf16[4,256,128]{2,1,0:T(8,128)(2,1)S(1)}, bf16[4,256,128]{2,1,0:T(8,128)(2,1)S(1)}, u32[]{:S(2)}, u32[]{:S(2)}) collective-permute-start(bf16[4,256,128]{2,1,0:T(8,128)(2,1)S(1)} %pad_maximum_fusion.refs_3_.refs_5_), channel_id=1, source_target_pairs={{0,224},{8,232},{16,240},{24,248},{32,0},{40,8},{48,16},{56,24},{6... | collective-permute-start | bytes 786440 | tf_op jit(solution)/shard_map/ppermute | solution.py:47
  32.4 4.6 %shard_map.123.refs_2_.refs_6_.refs_4_ = bf16[4,8,256,256]{3,2,1,0:T(8,128)(2,1)} custom-call(bf16[1024,1024]{1,0:T(8,128)(2,1)S(1)} %copy-done.2, bf16[1024,128]{1,0:T(8,128)(2,1)S(1)} %copy-done.5, bf16[1,8,128,128]{3,2,1,0:T(8,128)(2,1)S(1)} %shard_map.122.refs_2_.refs_4_, bf16[4,256,128]{2,1,0:T(8,128)(2,1)S(1)} %pad_maximum_fusion.refs_3_.refs_5_), custom_call_target="tpu_custom_call" | custom-call | flops 131072 | bytes 2048 | tf_op jit(solution)/shard_map/pallas_call | solution.py:56
  37.4 2.5 %collective-permute-start.7 = (bf16[4,256,128]{2,1,0:T(8,128)(2,1)S(1)}, bf16[4,256,128]{2,1,0:T(8,128)(2,1)S(1)}, u32[]{:S(2)}, u32[]{:S(2)}) collective-permute-start(bf16[4,256,128]{2,1,0:T(8,128)(2,1)S(1)} %get-tuple-element.33.refs_5_), channel_id=1, source_target_pairs={{0,224},{8,232},{16,240},{24,248},{32,0},{40,8},{48,16},{56,24},{6... | collective-permute-start | bytes 786440 | tf_op jit(solution)/shard_map/ppermute | solution.py:47
  39.8 4.2 %shard_map.125 = (f32[1024,128]{1,0:T(8,128)S(1)}, f32[128,128]{1,0:T(8,128)S(1)}, bf16[2,1024,512]{2,1,0:T(8,128)(2,1)S(1)}) custom-call(s32[11]{0:T(128)S(1)} %concatenate.9.refs_0_, bf16[1024,8192]{1,0:T(8,128)(2,1)} %refs_1_.27, bf16[1024,8192]{1,0:T(8,128)(2,1)} %refs_1_.27, bf16[1024,8192]{1,0:T(8,128)(2,1)} %refs_1_.27, bf16[128,8192]{1,0:T(8,128)(2,1)} %refs_1_.20, ...), custom_call_target="tpu_custom_call" | custom-call | flops 65536 | bytes 512 | tf_op jit(solution)/shard_map/pallas_call | solution.py:56
  47.6 2.7 %collective-permute-start.9 = (bf16[4,256,128]{2,1,0:T(8,128)(2,1)S(1)}, bf16[4,256,128]{2,1,0:T(8,128)(2,1)S(1)}, u32[]{:S(2)}, u32[]{:S(2)}) collective-permute-start(bf16[4,256,128]{2,1,0:T(8,128)(2,1)S(1)} %get-tuple-element.36.refs_5_), channel_id=1, source_target_pairs={{0,224},{8,232},{16,240},{24,248},{32,0},{40,8},{48,16},{56,24},{6... | collective-permute-start | bytes 786440 | tf_op jit(solution)/shard_map/ppermute | solution.py:47
  50.3 5.2 %shard_map.127 = (f32[1024,128]{1,0:T(8,128)S(1)}, f32[128,128]{1,0:T(8,128)S(1)}, bf16[2,1024,512]{2,1,0:T(8,128)(2,1)}) custom-call(s32[11]{0:T(128)S(1)} %concatenate.9.refs_0_, bf16[1024,8192]{1,0:T(8,128)(2,1)} %refs_1_.27, bf16[1024,8192]{1,0:T(8,128)(2,1)} %refs_1_.27, bf16[128,8192]{1,0:T(8,128)(2,1)} %refs_1_.20, bf16[128,8192]{1,0:T(8,128)(2,1)} %refs_1_.20, ...), custom_call_target="tpu_custom_call" | custom-call | flops 131072 | bytes 1024 | tf_op jit(solution)/shard_map/pallas_call | solution.py:56
  56.6 5.2 %shard_map.129 = (f32[1024,128]{1,0:T(8,128)S(1)}, f32[128,128]{1,0:T(8,128)S(1)}, bf16[2,1024,512]{2,1,0:T(8,128)(2,1)}) custom-call(s32[11]{0:T(128)S(1)} %concatenate.9.refs_0_, bf16[1024,8192]{1,0:T(8,128)(2,1)} %refs_1_.27, bf16[1024,8192]{1,0:T(8,128)(2,1)} %refs_1_.27, bf16[128,8192]{1,0:T(8,128)(2,1)} %refs_1_.20, bf16[128,8192]{1,0:T(8,128)(2,1)} %refs_1_.20, ...), custom_call_target="tpu_custom_call" | custom-call | flops 131072 | bytes 1024 | tf_op jit(solution)/shard_map/pallas_call | solution.py:56
  63.8 3.0 %collective-permute-start.11 = (bf16[2,256,128]{2,1,0:T(8,128)(2,1)S(1)}, bf16[2,256,128]{2,1,0:T(8,128)(2,1)S(1)}, u32[]{:S(2)}, u32[]{:S(2)}) collective-permute-start(bf16[2,256,128]{2,1,0:T(8,128)(2,1)S(1)} %slice.14), channel_id=1, source_target_pairs={{0,224},{8,232},{16,240},{24,248},{32,0},{40,8},{48,16},{56,24},{6... | collective-permute-start | bytes 393224 | tf_op jit(solution)/shard_map/ppermute | solution.py:47
  66.8 5.3 %shard_map.130 = (f32[1024,128]{1,0:T(8,128)S(1)}, f32[128,128]{1,0:T(8,128)S(1)}, bf16[2,1024,512]{2,1,0:T(8,128)(2,1)}) custom-call(s32[11]{0:T(128)S(1)} %concatenate.9.refs_0_, bf16[1024,8192]{1,0:T(8,128)(2,1)} %refs_1_.27, bf16[1024,8192]{1,0:T(8,128)(2,1)} %refs_1_.27, bf16[128,8192]{1,0:T(8,128)(2,1)} %refs_1_.20, bf16[128,8192]{1,0:T(8,128)(2,1)} %refs_1_.20, ...), custom_call_target="tpu_custom_call" | custom-call | flops 131072 | bytes 1024 | tf_op jit(solution)/shard_map/pallas_call | solution.py:56
  73.7 6.8 %shard_map.132.refs_3_ = bf16[128,1024]{1,0:T(8,128)(2,1)S(1)} custom-call(s32[11]{0:T(128)S(1)} %concatenate.9.refs_0_, bf16[1024,8192]{1,0:T(8,128)(2,1)} %refs_1_.27, bf16[4,256,128]{2,1,0:T(8,128)(2,1)S(1)} %constant_dynamic-update-slice_fusion.refs_2_, f32[1024,128]{1,0:T(8,128)S(1)} %get-tuple-element.44.refs_3_, ...), custom_call_target="tpu_custom_call" | custom-call | flops 262144 | bytes 2048 | tf_op jit(solution)/shard_map/pallas_call | solution.py:56
  81.9 3.3 %collective-permute-done.15 = bf16[128,128]{1,0:T(8,128)(2,1)S(1)} collective-permute-done((bf16[128,128]{1,0:T(8,128)(2,1)S(1)}, bf16[128,128]{1,0:T(8,128)(2,1)S(1)}, u32[]{:S(2)}, u32[]{:S(2)}) %collective-permute-start.15) | collective-permute-done | bytes 32800 | tf_op jit(solution)/shard_map/ppermute | solution.py:47
  86.7 2.4 %shard_map.133.refs_0_ = f32[1,2,512,256]{3,2,1,0:T(8,128)S(1)} custom-call(s32[11]{0:T(128)S(1)} %concatenate.9.refs_0_, bf16[1024,8192]{1,0:T(8,128)(2,1)} %refs_1_.27, bf16[1,1024,512]{2,1,0:T(8,128)(2,1)S(1)} %collective-permute-done.14.refs_2_, bf16[128,1024]{1,0:T(8,128)(2,1)S(1)} %shard_map.132.refs_3_, ...), custom_call_target="tpu_custom_call" | custom-call | flops 65536 | bytes 1280 | tf_op jit(solution)/shard_map/pallas_call | solution.py:56
  91.7 2.7 %collective-permute-start.18 = (bf16[2,1024,512]{2,1,0:T(8,128)(2,1)}, bf16[2,1024,512]{2,1,0:T(8,128)(2,1)}, u32[]{:S(2)}, u32[]{:S(2)}) collective-permute-start(bf16[2,1024,512]{2,1,0:T(8,128)(2,1)} %shard_map.135), channel_id=1, source_target_pairs={{0,8},{8,0},{16,24},{24,16},{32,40},{40,32},{48,56},{56,48},{64,72... | collective-permute-start | bytes 6291464 | tf_op jit(solution)/shard_map/ppermute | solution.py:47
  97.4 4.1 %all-to-all-start.1 = ((bf16[8,32,16,256]{3,2,1,0:T(8,128)(2,1)}), bf16[8,32,16,256]{3,2,1,0:T(8,128)(2,1)S(1)}, u32[]{:S(2)}, u32[]{:S(2)}) async-start(bf16[8,32,16,256]{3,2,1,0:T(8,128)(2,1)} %copy-done.1), calls=%async_computation.1 | async-start | bytes 4194304 | tf_op jit(solution)/shard_map/all_to_all | solution.py:545
  101.5 4.2 %shard_map.136.refs_0_ = f32[2,2,512,256]{3,2,1,0:T(8,128)S(1)} custom-call(s32[11]{0:T(128)S(1)} %concatenate.9.refs_0_, bf16[1024,8192]{1,0:T(8,128)(2,1)} %refs_1_.27, bf16[2,1024,512]{2,1,0:T(8,128)(2,1)} %collective-permute-done.19.refs_2_, bf16[128,1024]{1,0:T(8,128)(2,1)S(1)} %shard_map.132.refs_3_, ...), custom_call_target="tpu_custom_call" | custom-call | flops 131072 | bytes 2560 | tf_op jit(solution)/shard_map/pallas_call | solution.py:56
  108.4 4.2 %shard_map.138.refs_0_ = f32[2,2,512,256]{3,2,1,0:T(8,128)S(1)} custom-call(s32[11]{0:T(128)S(1)} %concatenate.9.refs_0_, bf16[1024,8192]{1,0:T(8,128)(2,1)} %refs_1_.27, bf16[2,1024,512]{2,1,0:T(8,128)(2,1)} %collective-permute-done.18.refs_2_, bf16[128,1024]{1,0:T(8,128)(2,1)S(1)} %shard_map.132.refs_3_, ...), custom_call_target="tpu_custom_call" | custom-call | flops 131072 | bytes 2560 | tf_op jit(solution)/shard_map/pallas_call | solution.py:56
  112.7 7.8 %collective-permute-done.23.refs_2_.refs_3_ = bf16[1152,256]{1,0:T(8,128)(2,1)S(1)} collective-permute-done((bf16[1152,256]{1,0:T(8,128)(2,1)S(1)}, bf16[1152,256]{1,0:T(8,128)(2,1)S(1)}, u32[]{:S(2)}, u32[]{:S(2)}) %collective-permute-start.23) | collective-permute-done | bytes 589856 | tf_op jit(solution)/shard_map/ppermute | solution.py:47
  120.4 2.2 %collective-permute-done.22.refs_1_.refs_5_ = bf16[1152,256]{1,0:T(8,128)(2,1)S(1)} collective-permute-done((bf16[1152,256]{1,0:T(8,128)(2,1)S(1)}, bf16[1152,256]{1,0:T(8,128)(2,1)S(1)}, u32[]{:S(2)}, u32[]{:S(2)}) %collective-permute-start.22) | collective-permute-done | bytes 589856 | tf_op jit(solution)/shard_map/ppermute | solution.py:47
  124.4 3.0 %collective-permute-start.5 = (bf16[1,1024,512]{2,1,0:T(8,128)(2,1)}, bf16[1,1024,512]{2,1,0:T(8,128)(2,1)}, u32[]{:S(2)}, u32[]{:S(2)}) collective-permute-start(bf16[1,1024,512]{2,1,0:T(8,128)(2,1)} %get-tuple-element.61), channel_id=1, source_target_pairs={{0,8},{8,0},{16,24},{24,16},{32,40},{40,32},{48,56},{56,48},{64,72... | collective-permute-start | bytes 3145736 | tf_op jit(solution)/shard_map/ppermute | solution.py:47
  127.4 4.2 %shard_map.140.refs_0_ = f32[2,2,512,256]{3,2,1,0:T(8,128)S(1)} custom-call(s32[11]{0:T(128)S(1)} %concatenate.9.refs_0_, bf16[1024,8192]{1,0:T(8,128)(2,1)} %refs_1_.27, bf16[2,1024,512]{2,1,0:T(8,128)(2,1)} %collective-permute-done.13.refs_2_, bf16[128,1024]{1,0:T(8,128)(2,1)S(1)} %shard_map.132.refs_3_, ...), custom_call_target="tpu_custom_call" | custom-call | flops 131072 | bytes 2560 | tf_op jit(solution)/shard_map/pallas_call | solution.py:56
  131.7 3.6 %collective-permute-done.25.refs_2_ = bf16[1152,256]{1,0:T(8,128)(2,1)S(1)} collective-permute-done((bf16[1152,256]{1,0:T(8,128)(2,1)S(1)}, bf16[1152,256]{1,0:T(8,128)(2,1)S(1)}, u32[]{:S(2)}, u32[]{:S(2)}) %collective-permute-start.25) | collective-permute-done | bytes 589856 | tf_op jit(solution)/shard_map/ppermute | solution.py:47
  139.4 3.4 %collective-permute-start.26 = (bf16[8,128,256]{2,1,0:T(8,128)(2,1)}, bf16[8,128,256]{2,1,0:T(8,128)(2,1)}, u32[]{:S(2)}, u32[]{:S(2)}) collective-permute-start(bf16[8,128,256]{2,1,0:T(8,128)(2,1)} %shard_map.142.refs_2_), channel_id=1, source_target_pairs={{0,8},{8,0},{16,24},{24,16},{32,40},{40,32},{48,56},{56,48},{64,72... | collective-permute-start | bytes 1572872 | tf_op jit(solution)/shard_map/ppermute | solution.py:47
  144.7 2.5 %shard_map.144.refs_6_.refs_3_ = f32[4,128,256]{2,1,0:T(8,128)S(1)} custom-call(s32[11]{0:T(128)S(1)} %concatenate.9.refs_0_, s32[32]{0:T(128)S(1)} %copy-done.13, bf16[8,128,256]{2,1,0:T(8,128)(2,1)} %shard_map.142.refs_2_, bf16[8,128,256]{2,1,0:T(8,128)(2,1)} %collective-permute-done.26.refs_3_, bf16[8,32,16,256]{3,2,1,0:T(8,128)(2,1)S(1)} %all-to-all-done.1.refs_4_), custom_call_target="tpu_custom_call" | custom-call | flops 65536 | bytes 1024 | tf_op jit(solution)/shard_map/pallas_call | solution.py:56
  149.0 2.5 %shard_map.145.refs_0_ = f32[1,2,512,256]{3,2,1,0:T(8,128)S(1)} custom-call(s32[11]{0:T(128)S(1)} %concatenate.9.refs_0_, bf16[1024,8192]{1,0:T(8,128)(2,1)} %refs_1_.27, bf16[1,1024,512]{2,1,0:T(8,128)(2,1)} %collective-permute-done.5.refs_2_, bf16[128,1024]{1,0:T(8,128)(2,1)S(1)} %shard_map.132.refs_3_, ...), custom_call_target="tpu_custom_call" | custom-call | flops 65536 | bytes 1280 | tf_op jit(solution)/shard_map/pallas_call | solution.py:56
  151.5 5.1 %collective-permute-done.28.refs_2_ = bf16[1024,256]{1,0:T(8,128)(2,1)} collective-permute-done((bf16[1024,256]{1,0:T(8,128)(2,1)}, bf16[1024,256]{1,0:T(8,128)(2,1)}, u32[]{:S(2)}, u32[]{:S(2)}) %collective-permute-start.28) | collective-permute-done | bytes 524320 | tf_op jit(solution)/shard_map/ppermute | solution.py:47
  157.3 2.8 %shard_map.146 = (f32[512,256]{1,0:T(8,128)S(1)}, bf16[512,256]{1,0:T(8,128)(2,1)S(1)}, f32[256,1,128]{2,1,0:T(1,128)}) custom-call(f32[1,2,512,256]{3,2,1,0:T(8,128)S(1)} %shard_map.145.refs_0_, bf16[1024,256]{1,0:T(8,128)(2,1)} %collective-permute-done.27.refs_1_, bf16[1024,256]{1,0:T(8,128)(2,1)} %collective-permute-done.28.refs_2_, ...), custom_call_target="tpu_custom_call" | custom-call | flops 1024 | bytes 1024 | tf_op jit(solution)/shard_map/pallas_call | solution.py:56
  161.8 10.2 %all-to-all-start.2 = ((f32[256,1,128]{2,1,0:T(1,128)}), f32[256,1,128]{2,1,0:T(1,128)S(1)}, u32[]{:S(2)}, u32[]{:S(2)}) async-start(f32[256,1,128]{2,1,0:T(1,128)} %get-tuple-element.59), calls=%async_computation.2 | async-start | bytes 262144 | tf_op jit(solution)/shard_map/all_to_all | solution.py:558
  172.9 12.0 %all-to-all-done.2.refs_0_ = f32[256,1,128]{2,1,0:T(1,128)S(1)} async-done(((f32[256,1,128]{2,1,0:T(1,128)}), f32[256,1,128]{2,1,0:T(1,128)S(1)}, u32[]{:S(2)}, u32[]{:S(2)}) %all-to-all-start.2) | async-done | bytes 131104 | tf_op jit(solution)/shard_map/all_to_all | solution.py:558
  (105 shorter events, 41.0 us)
Async XLA Ops:
  2.5 37.3 %all-to-all-start = ((bf16[32,16,256]{2,1,0:T(8,128)(2,1)}), bf16[32,16,256]{2,1,0:T(8,128)(2,1)S(1)}, u32[]{:S(2)}, u32[]{:S(2)}) async-start(bf16[32,16,256]{2,1,0:T(8,128)(2,1)} %bitcast.13), calls=%async_computation | async-start | bytes 524288 | tf_op jit(solution)/shard_map/all_to_all | solution.py:512
  15.3 5.6 %collective-permute-start = (bf16[256,128]{1,0:T(8,128)(2,1)}, bf16[256,128]{1,0:T(8,128)(2,1)S(1)}, u32[]{:S(2)}, u32[]{:S(2)}) collective-permute-start(bf16[256,128]{1,0:T(8,128)(2,1)} %param.16), channel_id=1, source_target_pairs={{0,16},{8,24},{16,0},{24,8},{32,48},{40,56},{48,32},{56,40},{64,80... | collective-permute-start | bytes 196616 | tf_op jit(solution)/shard_map/ppermute | solution.py:47
  18.2 7.9 %collective-permute-start.2 = (bf16[256,128]{1,0:T(8,128)(2,1)}, bf16[256,128]{1,0:T(8,128)(2,1)S(1)}, u32[]{:S(2)}, u32[]{:S(2)}) collective-permute-start(bf16[256,128]{1,0:T(8,128)(2,1)} %param.16), channel_id=1, source_target_pairs={{0,24},{8,16},{16,8},{24,0},{32,56},{40,48},{48,40},{56,32},{64,88... | collective-permute-start | bytes 196616 | tf_op jit(solution)/shard_map/ppermute | solution.py:47
  18.7 7.4 %collective-permute-start.1 = (bf16[256,128]{1,0:T(8,128)(2,1)}, bf16[256,128]{1,0:T(8,128)(2,1)S(1)}, u32[]{:S(2)}, u32[]{:S(2)}) collective-permute-start(bf16[256,128]{1,0:T(8,128)(2,1)} %param.16), channel_id=1, source_target_pairs={{0,8},{8,0},{16,24},{24,16},{32,40},{40,32},{48,56},{56,48},{64,72... | collective-permute-start | bytes 196616 | tf_op jit(solution)/shard_map/ppermute | solution.py:47
  27.0 10.1 %collective-permute-start.4 = (bf16[4,256,128]{2,1,0:T(8,128)(2,1)S(1)}, bf16[4,256,128]{2,1,0:T(8,128)(2,1)S(1)}, u32[]{:S(2)}, u32[]{:S(2)}) collective-permute-start(bf16[4,256,128]{2,1,0:T(8,128)(2,1)S(1)} %pad_maximum_fusion.refs_3_.refs_5_), channel_id=1, source_target_pairs={{0,224},{8,232},{16,240},{24,248},{32,0},{40,8},{48,16},{56,24},{6... | collective-permute-start | bytes 786440 | tf_op jit(solution)/shard_map/ppermute | solution.py:47
  29.0 8.4 %collective-permute-start.3 = (bf16[4,256,128]{2,1,0:T(8,128)(2,1)S(1)}, bf16[4,256,128]{2,1,0:T(8,128)(2,1)S(1)}, u32[]{:S(2)}, u32[]{:S(2)}) collective-permute-start(bf16[4,256,128]{2,1,0:T(8,128)(2,1)S(1)} %pad_maximum_fusion.refs_3_.refs_5_), channel_id=1, source_target_pairs={{0,32},{8,40},{16,48},{24,56},{32,64},{40,72},{48,80},{56,88},{64,... | collective-permute-start | bytes 786440 | tf_op jit(solution)/shard_map/ppermute | solution.py:47
  37.4 9.1 %collective-permute-start.7 = (bf16[4,256,128]{2,1,0:T(8,128)(2,1)S(1)}, bf16[4,256,128]{2,1,0:T(8,128)(2,1)S(1)}, u32[]{:S(2)}, u32[]{:S(2)}) collective-permute-start(bf16[4,256,128]{2,1,0:T(8,128)(2,1)S(1)} %get-tuple-element.33.refs_5_), channel_id=1, source_target_pairs={{0,224},{8,232},{16,240},{24,248},{32,0},{40,8},{48,16},{56,24},{6... | collective-permute-start | bytes 786440 | tf_op jit(solution)/shard_map/ppermute | solution.py:47
  39.8 7.8 %collective-permute-start.6 = (bf16[4,256,128]{2,1,0:T(8,128)(2,1)S(1)}, bf16[4,256,128]{2,1,0:T(8,128)(2,1)S(1)}, u32[]{:S(2)}, u32[]{:S(2)}) collective-permute-start(bf16[4,256,128]{2,1,0:T(8,128)(2,1)S(1)} %get-tuple-element.31.refs_7_.refs_6_), channel_id=1, source_target_pairs={{0,32},{8,40},{16,48},{24,56},{32,64},{40,72},{48,80},{56,88},{64,... | collective-permute-start | bytes 786440 | tf_op jit(solution)/shard_map/ppermute | solution.py:47
  45.2 41.5 %collective-permute-start.14 = (bf16[1,1024,512]{2,1,0:T(8,128)(2,1)S(1)}, bf16[1,1024,512]{2,1,0:T(8,128)(2,1)S(1)}, u32[]{:S(2)}, u32[]{:S(2)}) collective-permute-start(bf16[1,1024,512]{2,1,0:T(8,128)(2,1)S(1)} %get-tuple-element.60), channel_id=1, source_target_pairs={{0,8},{8,0},{16,24},{24,16},{32,40},{40,32},{48,56},{56,48},{64,72... | collective-permute-start | bytes 3145736 | tf_op jit(solution)/shard_map/ppermute | solution.py:47
  47.6 7.9 %collective-permute-start.8 = (bf16[4,256,128]{2,1,0:T(8,128)(2,1)S(1)}, bf16[4,256,128]{2,1,0:T(8,128)(2,1)S(1)}, u32[]{:S(2)}, u32[]{:S(2)}) collective-permute-start(bf16[4,256,128]{2,1,0:T(8,128)(2,1)S(1)} %get-tuple-element.35.refs_6_), channel_id=1, source_target_pairs={{0,32},{8,40},{16,48},{24,56},{32,64},{40,72},{48,80},{56,88},{64,... | collective-permute-start | bytes 786440 | tf_op jit(solution)/shard_map/ppermute | solution.py:47
  47.6 7.9 %collective-permute-start.9 = (bf16[4,256,128]{2,1,0:T(8,128)(2,1)S(1)}, bf16[4,256,128]{2,1,0:T(8,128)(2,1)S(1)}, u32[]{:S(2)}, u32[]{:S(2)}) collective-permute-start(bf16[4,256,128]{2,1,0:T(8,128)(2,1)S(1)} %get-tuple-element.36.refs_5_), channel_id=1, source_target_pairs={{0,224},{8,232},{16,240},{24,248},{32,0},{40,8},{48,16},{56,24},{6... | collective-permute-start | bytes 786440 | tf_op jit(solution)/shard_map/ppermute | solution.py:47
  55.5 16.6 %collective-permute-start.10 = (bf16[2,256,128]{2,1,0:T(8,128)(2,1)S(1)}, bf16[2,256,128]{2,1,0:T(8,128)(2,1)S(1)}, u32[]{:S(2)}, u32[]{:S(2)}) collective-permute-start(bf16[2,256,128]{2,1,0:T(8,128)(2,1)S(1)} %slice.13), channel_id=1, source_target_pairs={{0,32},{8,40},{16,48},{24,56},{32,64},{40,72},{48,80},{56,88},{64,... | collective-permute-start | bytes 393224 | tf_op jit(solution)/shard_map/ppermute | solution.py:47
  61.8 39.7 %collective-permute-start.19 = (bf16[2,1024,512]{2,1,0:T(8,128)(2,1)}, bf16[2,1024,512]{2,1,0:T(8,128)(2,1)}, u32[]{:S(2)}, u32[]{:S(2)}) collective-permute-start(bf16[2,1024,512]{2,1,0:T(8,128)(2,1)} %get-tuple-element.49), channel_id=1, source_target_pairs={{0,8},{8,0},{16,24},{24,16},{32,40},{40,32},{48,56},{56,48},{64,72... | collective-permute-start | bytes 6291464 | tf_op jit(solution)/shard_map/ppermute | solution.py:47
  63.8 8.4 %collective-permute-start.11 = (bf16[2,256,128]{2,1,0:T(8,128)(2,1)S(1)}, bf16[2,256,128]{2,1,0:T(8,128)(2,1)S(1)}, u32[]{:S(2)}, u32[]{:S(2)}) collective-permute-start(bf16[2,256,128]{2,1,0:T(8,128)(2,1)S(1)} %slice.14), channel_id=1, source_target_pairs={{0,224},{8,232},{16,240},{24,248},{32,0},{40,8},{48,16},{56,24},{6... | collective-permute-start | bytes 393224 | tf_op jit(solution)/shard_map/ppermute | solution.py:47
  80.5 6.2 %collective-permute-start.12 = (bf16[128,1024]{1,0:T(8,128)(2,1)S(1)}, bf16[128,1024]{1,0:T(8,128)(2,1)S(1)}, u32[]{:S(2)}, u32[]{:S(2)}) collective-permute-start(bf16[128,1024]{1,0:T(8,128)(2,1)S(1)} %shard_map.132.refs_3_), channel_id=1, source_target_pairs={{0,8},{8,0},{16,24},{24,16},{32,40},{40,32},{48,56},{56,48},{64,72... | collective-permute-start | bytes 786440 | tf_op jit(solution)/shard_map/ppermute | solution.py:47
  86.5 4.3 %collective-permute-start.16 = (bf16[128,256]{1,0:T(8,128)(2,1)S(1)}, bf16[128,256]{1,0:T(8,128)(2,1)S(1)}, u32[]{:S(2)}, u32[]{:S(2)}) collective-permute-start(bf16[128,256]{1,0:T(8,128)(2,1)S(1)} %pad_maximum_fusion.1.refs_0_), channel_id=1, source_target_pairs={{0,32},{8,40},{16,48},{24,56},{32,64},{40,72},{48,80},{56,88},{64,... | collective-permute-start | bytes 196616 | tf_op jit(solution)/shard_map/ppermute | solution.py:47
  91.7 16.8 %collective-permute-start.18 = (bf16[2,1024,512]{2,1,0:T(8,128)(2,1)}, bf16[2,1024,512]{2,1,0:T(8,128)(2,1)}, u32[]{:S(2)}, u32[]{:S(2)}) collective-permute-start(bf16[2,1024,512]{2,1,0:T(8,128)(2,1)} %shard_map.135), channel_id=1, source_target_pairs={{0,8},{8,0},{16,24},{24,16},{32,40},{40,32},{48,56},{56,48},{64,72... | collective-permute-start | bytes 6291464 | tf_op jit(solution)/shard_map/ppermute | solution.py:47
  94.3 33.1 %collective-permute-start.13 = (bf16[2,1024,512]{2,1,0:T(8,128)(2,1)}, bf16[2,1024,512]{2,1,0:T(8,128)(2,1)}, u32[]{:S(2)}, u32[]{:S(2)}) collective-permute-start(bf16[2,1024,512]{2,1,0:T(8,128)(2,1)} %get-tuple-element.46), channel_id=1, source_target_pairs={{0,8},{8,0},{16,24},{24,16},{32,40},{40,32},{48,56},{56,48},{64,72... | collective-permute-start | bytes 6291464 | tf_op jit(solution)/shard_map/ppermute | solution.py:47
  94.3 11.4 %collective-permute-start.21 = (bf16[640,256]{1,0:T(8,128)(2,1)}, bf16[640,256]{1,0:T(8,128)(2,1)S(1)}, u32[]{:S(2)}, u32[]{:S(2)}) collective-permute-start(bf16[640,256]{1,0:T(8,128)(2,1)} %get-tuple-element.50), channel_id=1, source_target_pairs={{0,224},{8,232},{16,240},{24,248},{32,0},{40,8},{48,16},{56,24},{6... | collective-permute-start | bytes 983048 | tf_op jit(solution)/shard_map/ppermute | solution.py:47
  94.3 11.4 %collective-permute-start.20 = (bf16[640,256]{1,0:T(8,128)(2,1)S(1)}, bf16[640,256]{1,0:T(8,128)(2,1)}, u32[]{:S(2)}, u32[]{:S(2)}) collective-permute-start(bf16[640,256]{1,0:T(8,128)(2,1)S(1)} %get-tuple-element.48.refs_1_.refs_5_), channel_id=1, source_target_pairs={{0,32},{8,40},{16,48},{24,56},{32,64},{40,72},{48,80},{56,88},{64,... | collective-permute-start | bytes 983048 | tf_op jit(solution)/shard_map/ppermute | solution.py:47
  97.4 46.9 %all-to-all-start.1 = ((bf16[8,32,16,256]{3,2,1,0:T(8,128)(2,1)}), bf16[8,32,16,256]{3,2,1,0:T(8,128)(2,1)S(1)}, u32[]{:S(2)}, u32[]{:S(2)}) async-start(bf16[8,32,16,256]{3,2,1,0:T(8,128)(2,1)} %copy-done.1), calls=%async_computation.1 | async-start | bytes 4194304 | tf_op jit(solution)/shard_map/all_to_all | solution.py:545
  106.9 13.6 %collective-permute-start.23 = (bf16[1152,256]{1,0:T(8,128)(2,1)S(1)}, bf16[1152,256]{1,0:T(8,128)(2,1)S(1)}, u32[]{:S(2)}, u32[]{:S(2)}) collective-permute-start(bf16[1152,256]{1,0:T(8,128)(2,1)S(1)} %get-tuple-element.52), channel_id=1, source_target_pairs={{0,224},{8,232},{16,240},{24,248},{32,0},{40,8},{48,16},{56,24},{6... | collective-permute-start | bytes 1769480 | tf_op jit(solution)/shard_map/ppermute | solution.py:47
  108.2 14.5 %collective-permute-start.22 = (bf16[1152,256]{1,0:T(8,128)(2,1)S(1)}, bf16[1152,256]{1,0:T(8,128)(2,1)S(1)}, u32[]{:S(2)}, u32[]{:S(2)}) collective-permute-start(bf16[1152,256]{1,0:T(8,128)(2,1)S(1)} %get-tuple-element.51.refs_5_), channel_id=1, source_target_pairs={{0,32},{8,40},{16,48},{24,56},{32,64},{40,72},{48,80},{56,88},{64,... | collective-permute-start | bytes 1769480 | tf_op jit(solution)/shard_map/ppermute | solution.py:47
  122.9 12.4 %collective-permute-start.25 = (bf16[1152,256]{1,0:T(8,128)(2,1)S(1)}, bf16[1152,256]{1,0:T(8,128)(2,1)S(1)}, u32[]{:S(2)}, u32[]{:S(2)}) collective-permute-start(bf16[1152,256]{1,0:T(8,128)(2,1)S(1)} %get-tuple-element.54), channel_id=1, source_target_pairs={{0,224},{8,232},{16,240},{24,248},{32,0},{40,8},{48,16},{56,24},{6... | collective-permute-start | bytes 1769480 | tf_op jit(solution)/shard_map/ppermute | solution.py:47
  123.2 13.6 %collective-permute-start.24 = (bf16[1152,256]{1,0:T(8,128)(2,1)S(1)}, bf16[1152,256]{1,0:T(8,128)(2,1)S(1)}, u32[]{:S(2)}, u32[]{:S(2)}) collective-permute-start(bf16[1152,256]{1,0:T(8,128)(2,1)S(1)} %get-tuple-element.53.refs_5_), channel_id=1, source_target_pairs={{0,32},{8,40},{16,48},{24,56},{32,64},{40,72},{48,80},{56,88},{64,... | collective-permute-start | bytes 1769480 | tf_op jit(solution)/shard_map/ppermute | solution.py:47
  124.4 24.6 %collective-permute-start.5 = (bf16[1,1024,512]{2,1,0:T(8,128)(2,1)}, bf16[1,1024,512]{2,1,0:T(8,128)(2,1)}, u32[]{:S(2)}, u32[]{:S(2)}) collective-permute-start(bf16[1,1024,512]{2,1,0:T(8,128)(2,1)} %get-tuple-element.61), channel_id=1, source_target_pairs={{0,8},{8,0},{16,24},{24,16},{32,40},{40,32},{48,56},{56,48},{64,72... | collective-permute-start | bytes 3145736 | tf_op jit(solution)/shard_map/ppermute | solution.py:47
  139.4 5.3 %collective-permute-start.26 = (bf16[8,128,256]{2,1,0:T(8,128)(2,1)}, bf16[8,128,256]{2,1,0:T(8,128)(2,1)}, u32[]{:S(2)}, u32[]{:S(2)}) collective-permute-start(bf16[8,128,256]{2,1,0:T(8,128)(2,1)} %shard_map.142.refs_2_), channel_id=1, source_target_pairs={{0,8},{8,0},{16,24},{24,16},{32,40},{40,32},{48,56},{56,48},{64,72... | collective-permute-start | bytes 1572872 | tf_op jit(solution)/shard_map/ppermute | solution.py:47
  142.8 13.9 %collective-permute-start.28 = (bf16[1024,256]{1,0:T(8,128)(2,1)}, bf16[1024,256]{1,0:T(8,128)(2,1)}, u32[]{:S(2)}, u32[]{:S(2)}) collective-permute-start(bf16[1024,256]{1,0:T(8,128)(2,1)} %get-tuple-element.56), channel_id=1, source_target_pairs={{0,224},{8,232},{16,240},{24,248},{32,0},{40,8},{48,16},{56,24},{6... | collective-permute-start | bytes 1572872 | tf_op jit(solution)/shard_map/ppermute | solution.py:47
  142.8 14.6 %collective-permute-start.27 = (bf16[1024,256]{1,0:T(8,128)(2,1)S(1)}, bf16[1024,256]{1,0:T(8,128)(2,1)}, u32[]{:S(2)}, u32[]{:S(2)}) collective-permute-start(bf16[1024,256]{1,0:T(8,128)(2,1)S(1)} %get-tuple-element.55.refs_8_.refs_5_), channel_id=1, source_target_pairs={{0,32},{8,40},{16,48},{24,56},{32,64},{40,72},{48,80},{56,88},{64,... | collective-permute-start | bytes 1572872 | tf_op jit(solution)/shard_map/ppermute | solution.py:47
  147.2 10.1 %collective-permute-start.29 = (bf16[4,128,256]{2,1,0:T(8,128)(2,1)S(1)}, bf16[4,128,256]{2,1,0:T(8,128)(2,1)S(1)}, u32[]{:S(2)}, u32[]{:S(2)}) collective-permute-start(bf16[4,128,256]{2,1,0:T(8,128)(2,1)S(1)} %convert_element_type.3), channel_id=1, source_target_pairs={{0,16},{8,24},{16,0},{24,8},{32,48},{40,56},{48,32},{56,40},{64,80... | collective-permute-start | bytes 786440 | tf_op jit(solution)/shard_map/ppermute | solution.py:47
  160.1 11.9 %collective-permute-start.30 = (bf16[512,256]{1,0:T(8,128)(2,1)S(1)}, bf16[512,256]{1,0:T(8,128)(2,1)S(1)}, u32[]{:S(2)}, u32[]{:S(2)}) collective-permute-start(bf16[512,256]{1,0:T(8,128)(2,1)S(1)} %get-tuple-element.58), channel_id=1, source_target_pairs={{0,16},{8,24},{16,0},{24,8},{32,48},{40,56},{48,32},{56,40},{64,80... | collective-permute-start | bytes 786440 | tf_op jit(solution)/shard_map/ppermute | solution.py:47
  161.8 23.1 %all-to-all-start.2 = ((f32[256,1,128]{2,1,0:T(1,128)}), f32[256,1,128]{2,1,0:T(1,128)S(1)}, u32[]{:S(2)}, u32[]{:S(2)}) async-start(f32[256,1,128]{2,1,0:T(1,128)} %get-tuple-element.59), calls=%async_computation.2 | async-start | bytes 262144 | tf_op jit(solution)/shard_map/all_to_all | solution.py:558
  (17 other events, 110.8 us)
